TPU v7x, 32 devices: a whole 2x2x4 slice. The times are simulated.
32 devices in a mesh: expert: 8 (over y, x, core), tensor: 4 (over z).
Axes of the slice: x: 2, y: 2, z: 4, core: 2. Of those that a mesh axis runs over, the one named last changes fastest.
Arguments:
- tokens: bfloat16 [3072, 2048], P('expert'), may hold values from -6 to 6
- w_query: bfloat16 [2048, 2048], P(None, 'tensor'), may hold values from -0.125 to 0.125
- w_key: bfloat16 [2048, 2048], P(None, 'tensor'), may hold values from -0.125 to 0.125
- w_value: bfloat16 [2048, 2048], P(None, 'tensor'), may hold values from -0.125 to 0.125
- w_out: bfloat16 [2048, 2048], P('tensor'), may hold values from -0.5 to 0.5
- attn_gain: float32 [2048], replicated, may hold values from 0.5 to 1.5
- ffn_gain: float32 [2048], replicated, may hold values from 0.5 to 1.5
- qk_gain: float32 [2, 2048], P(None, 'tensor'), may hold values from 1 to 2
- router: bfloat16 [2048, 16], replicated, may hold values from -0.0625 to 0.0625
- w_gate: bfloat16 [16, 2048, 1024], P('expert', None, 'tensor'), may hold values from -0.125 to 0.125
- w_up: bfloat16 [16, 2048, 1024], P('expert', None, 'tensor'), may hold values from -0.125 to 0.125
- w_down: bfloat16 [16, 1024, 2048], P('expert', 'tensor'), may hold values from -4 to 4
- routes: int32 [3072, 8], P('expert'), may hold values from 0 to 15, all different within a row; in each aligned block of 384 rows (0 to 383, 384 to 767, ...) at most 288 rows name the same one
- cont_group: int32 [8], P('expert'), may hold values from 0 to 1, as said below
- cotangent: bfloat16 [3072, 2048], P('expert'), may hold values from -6 to 6
Outputs:
- output: bfloat16 [3072, 2048], P('expert')
- input_grad: float32 [3072, 2048], P('expert')
- w_query_grad: float32 [2048, 2048], P('expert', 'tensor')
- w_key_grad: float32 [2048, 2048], P('expert', 'tensor')
- w_value_grad: float32 [2048, 2048], P('expert', 'tensor')
- w_out_grad: float32 [2048, 2048], P('tensor', 'expert')
- attn_gain_grad: float32 [2048], P('expert')
- ffn_gain_grad: float32 [2048], P('expert')
- qk_gain_grad: float32 [2, 2048], P(None, ('tensor', 'expert'))
- router_grad: float32 [2048, 16], P('expert')
- w_gate_grad: float32 [16, 2048, 1024], P('expert', None, 'tensor')
- w_up_grad: float32 [16, 2048, 1024], P('expert', None, 'tensor')
- w_down_grad: float32 [16, 1024, 2048], P('expert', 'tensor')
Inputs may be any that keep to these rules, and one draw needn't show every extreme that they name: `routes`: within the rows of one index of expert no expert is named more than 288 times, and in every draw some expert is named exactly 288 times by one index's rows. `cont_group`: every prompt is named by exactly 4 continuations.
All inputs are finite; a program needn't handle non-finite values.
Results may differ from a plain program's by a relative error of at most 0.025.
Values may be sent and summed in bfloat16 or wider, within the bound.
A program may use at most 320 MiB of HBM per device.

v0:
```python
import jax
import jax.numpy as jnp
from jax import lax
from jax.sharding import PartitionSpec as P

HD = 128
PROMPT_DEV = 128
CLEN = 256
CONT_DEV = 1


epsilon = 1e-05
masked_value = -1e30


def rotate(field, cosine, sine):
    half = field.shape[-1] // 2
    first = field[..., :half]
    second = field[..., half:]
    return jnp.concatenate(
        [first * cosine - second * sine, second * cosine + first * sine], axis=-1
    )


def unrotate(grad, cosine, sine):
    half = grad.shape[-1] // 2
    first = grad[..., :half]
    second = grad[..., half:]
    return jnp.concatenate(
        [first * cosine + second * sine, second * cosine - first * sine], axis=-1
    )


def send_rows(buffer):
    return lax.all_to_all(buffer, "expert", split_axis=1, concat_axis=1, tiled=True)


def return_rows(parts, slot_index, rows, route_width, weights):
    moved = lax.all_to_all(parts, "expert", split_axis=1, concat_axis=1, tiled=True)
    flat_rows = moved.reshape(-1, moved.shape[3])
    picked = flat_rows[slot_index].reshape(rows, route_width, moved.shape[3]).astype(jnp.float32)
    return (jnp.sum(weights[:, :, None] * picked, axis=1), picked)


def body(
    tokens,
    w_query,
    w_key,
    w_value,
    w_out,
    attn_gain,
    ffn_gain,
    qk_gain,
    router,
    w_gate,
    w_up,
    w_down,
    routes,
    cont_group,
    cotangent,
):
    rows, width = tokens.shape
    local_width = w_query.shape[1]
    head_count = local_width // HD
    experts_total = router.shape[1]
    local_experts = w_gate.shape[0]
    route_width = routes.shape[1]
    ranks = lax.axis_size("expert")
    device = lax.axis_index("expert")
    span = ranks // 2
    prompt_len = PROMPT_DEV * span
    capacity = rows * route_width * 3 // (2 * experts_total)
    factor = HD ** (-0.5)
    local = jnp.arange(rows, dtype=jnp.int32)
    is_prompt = local < PROMPT_DEV
    after = jnp.maximum(local - PROMPT_DEV, 0)
    slot_cont = after // CLEN
    cont_pick = jnp.sum(
        jnp.where(
            slot_cont[:, None] == jnp.arange(CONT_DEV, dtype=jnp.int32)[None, :],
            cont_group[None, :],
            0,
        ),
        axis=1,
    )
    group = jnp.where(is_prompt, device // span, cont_pick)
    position = jnp.where(is_prompt, device % span * PROMPT_DEV + local, prompt_len + after % CLEN)
    tag = jnp.where(is_prompt, -1, slot_cont)
    frequency = 10000.0 ** (-jnp.arange(HD // 2, dtype=jnp.float32) * 2.0 / HD)
    angle = position.astype(jnp.float32)[:, None] * frequency[None, :]
    cosine = jnp.cos(angle)[:, None, :]
    sine = jnp.sin(angle)[:, None, :]
    source = tokens.astype(jnp.float32)
    scale_one = lax.rsqrt(jnp.mean(source * source, axis=1, keepdims=True) + epsilon)
    normed = (source * scale_one * attn_gain).astype(jnp.bfloat16)
    query_raw = jnp.dot(normed, w_query, preferred_element_type=jnp.float32)
    key_raw = jnp.dot(normed, w_key, preferred_element_type=jnp.float32)
    value_raw = jnp.dot(normed, w_value, preferred_element_type=jnp.float32)
    squares = lax.psum(
        jnp.stack(
            [jnp.sum(query_raw * query_raw, axis=1), jnp.sum(key_raw * key_raw, axis=1)], axis=1
        ),
        "tensor",
    )
    scale_query = lax.rsqrt(squares[:, 0:1] / width + epsilon)
    scale_key = lax.rsqrt(squares[:, 1:2] / width + epsilon)
    query_rot = (
        rotate((query_raw * scale_query * qk_gain[0]).reshape(rows, head_count, HD), cosine, sine)
        .reshape(rows, local_width)
        .astype(jnp.bfloat16)
    )
    key_rot = (
        rotate((key_raw * scale_key * qk_gain[1]).reshape(rows, head_count, HD), cosine, sine)
        .reshape(rows, local_width)
        .astype(jnp.bfloat16)
    )
    value_low = value_raw.astype(jnp.bfloat16)
    prompt_keys, prompt_values = (
        lax.all_gather(key_rot[:PROMPT_DEV], "expert", axis=0, tiled=True),
        lax.all_gather(value_low[:PROMPT_DEV], "expert", axis=0, tiled=True),
    )
    prompt_count = prompt_keys.shape[0]
    all_keys = jnp.concatenate([prompt_keys, key_rot[PROMPT_DEV:]], axis=0)
    all_values = jnp.concatenate([prompt_values, value_low[PROMPT_DEV:]], axis=0)
    key_index = jnp.arange(prompt_count, dtype=jnp.int32)
    prompt_mask = (group[:, None] == (key_index // prompt_len)[None, :]) & (
        (key_index % prompt_len)[None, :] <= position[:, None]
    )
    own_mask = (tag[:, None] == tag[None, PROMPT_DEV:]) & (
        position[None, PROMPT_DEV:] <= position[:, None]
    )
    mask = jnp.concatenate([prompt_mask, own_mask], axis=1)

    def head_scores(query_head, key_head):
        scores = (
            jnp.einsum("qd,kd->qk", query_head, key_head, preferred_element_type=jnp.float32)
            * factor
        )
        return jnp.where(mask, scores, masked_value)

    outputs = []
    log_totals = []
    for head in range(head_count):
        start = head * HD
        scores = head_scores(query_rot[:, start : start + HD], all_keys[:, start : start + HD])
        top = jnp.max(scores, axis=1, keepdims=True)
        weights = jnp.exp(scores - top)
        total = jnp.sum(weights, axis=1, keepdims=True)
        shares = (weights / total).astype(jnp.bfloat16)
        outputs.append(
            jnp.dot(shares, all_values[:, start : start + HD], preferred_element_type=jnp.float32)
        )
        log_totals.append(top + jnp.log(total))
    attended = jnp.concatenate(outputs, axis=1).astype(jnp.bfloat16)
    attention = lax.psum(jnp.dot(attended, w_out, preferred_element_type=jnp.float32), "tensor")
    hidden = source + attention
    scale_two = lax.rsqrt(jnp.mean(hidden * hidden, axis=1, keepdims=True) + epsilon)
    normed_two = (hidden * scale_two * ffn_gain).astype(jnp.bfloat16)
    logits = jnp.dot(normed_two, router, preferred_element_type=jnp.float32)
    top = jnp.max(logits, axis=1, keepdims=True)
    weights = jnp.exp(logits - top)
    chances = weights / jnp.sum(weights, axis=1, keepdims=True)
    hits = (routes[:, :, None] == jnp.arange(experts_total, dtype=jnp.int32)[None, None, :]).astype(
        jnp.float32
    )
    gates = jnp.sum(hits * chances[:, None, :], axis=2)
    flat_expert = routes.reshape(-1)
    one_hot = (flat_expert[:, None] == jnp.arange(experts_total, dtype=jnp.int32)[None, :]).astype(
        jnp.int32
    )
    earlier = jnp.cumsum(one_hot, axis=0) - one_hot
    rank = jnp.sum(earlier * one_hot, axis=1)
    owner = flat_expert // local_experts
    which = flat_expert % local_experts
    slot_index = (which * ranks + owner) * capacity + rank
    buffer_rows = local_experts * ranks * capacity
    pick_index = jnp.arange(flat_expert.shape[0], dtype=jnp.int32)
    slot_pick = jnp.zeros((buffer_rows,), jnp.int32).at[slot_index].set(pick_index)
    slot_used = jnp.zeros((buffer_rows,), jnp.bool_).at[slot_index].set(True)
    slot_token = slot_pick // route_width
    outgoing = jnp.where(slot_used[:, None], normed_two[slot_token], jnp.zeros((), jnp.bfloat16))
    arrived = send_rows(outgoing.reshape(local_experts, ranks, capacity, width)).reshape(
        local_experts, ranks * capacity, width
    )
    gate_pre = jnp.einsum("jrd,jdf->jrf", arrived, w_gate, preferred_element_type=jnp.float32)
    up_pre = jnp.einsum("jrd,jdf->jrf", arrived, w_up, preferred_element_type=jnp.float32)
    sigma = jax.nn.sigmoid(gate_pre)
    activated = gate_pre * sigma
    inner = (activated * up_pre).astype(jnp.bfloat16)
    expert_out = jnp.einsum(
        "jrf,jfd->jrd", inner, w_down, preferred_element_type=jnp.float32
    ).astype(jnp.bfloat16)
    mixed_part, picked = return_rows(
        expert_out.reshape(local_experts, ranks, capacity, width),
        slot_index,
        rows,
        route_width,
        gates,
    )
    grad_out = cotangent.astype(jnp.float32)
    mixture = lax.psum(mixed_part.astype(jnp.bfloat16), "tensor").astype(jnp.float32)
    output = (hidden + mixture).astype(jnp.bfloat16)
    gate_grad_part = jnp.sum(grad_out[:, None, :] * picked, axis=2)
    slot_gate = gates.reshape(-1)[slot_pick]
    outgoing_grad = jnp.where(
        slot_used[:, None],
        (slot_gate[:, None] * grad_out[slot_token]).astype(jnp.bfloat16),
        jnp.zeros((), jnp.bfloat16),
    )
    arrived_grad = send_rows(outgoing_grad.reshape(local_experts, ranks, capacity, width)).reshape(
        local_experts, ranks * capacity, width
    )
    act_grad = jnp.einsum("jrd,jfd->jrf", arrived_grad, w_down, preferred_element_type=jnp.float32)
    up_grad = (act_grad * activated).astype(jnp.bfloat16)
    gate_grad = (act_grad * up_pre * sigma * (1.0 + gate_pre * (1.0 - sigma))).astype(jnp.bfloat16)
    grad_w_down = jnp.einsum(
        "jrf,jrd->jfd", inner, arrived_grad, preferred_element_type=jnp.float32
    )
    grad_w_gate = jnp.einsum("jrd,jrf->jdf", arrived, gate_grad, preferred_element_type=jnp.float32)
    grad_w_up = jnp.einsum("jrd,jrf->jdf", arrived, up_grad, preferred_element_type=jnp.float32)
    slot_grad = jnp.einsum("jrf,jdf->jrd", gate_grad, w_gate, preferred_element_type=jnp.float32)
    slot_grad = (
        slot_grad + jnp.einsum("jrf,jdf->jrd", up_grad, w_up, preferred_element_type=jnp.float32)
    ).astype(jnp.bfloat16)
    unit_weights = jnp.ones((rows, route_width), jnp.float32)
    input_part, unused = return_rows(
        slot_grad.reshape(local_experts, ranks, capacity, width),
        slot_index,
        rows,
        route_width,
        unit_weights,
    )
    moe_input_grad, gate_grad_all = lax.psum((input_part, gate_grad_part), "tensor")
    chance_grad = jnp.sum(hits * gate_grad_all[:, :, None], axis=1)
    logit_grad = (
        chances * (chance_grad - jnp.sum(chances * chance_grad, axis=1, keepdims=True))
    ).astype(jnp.bfloat16)
    grad_router = jnp.einsum(
        "td,te->de", normed_two, logit_grad, preferred_element_type=jnp.float32
    )
    normed_two_grad = moe_input_grad + jnp.einsum(
        "te,de->td", logit_grad, router, preferred_element_type=jnp.float32
    )
    weighted_two = ffn_gain * normed_two_grad
    grad_ffn_gain = jnp.sum(normed_two_grad * hidden * scale_two, axis=0)
    hidden_grad = (
        grad_out
        + scale_two * weighted_two
        - hidden * (scale_two**3 / width) * jnp.sum(weighted_two * hidden, axis=1, keepdims=True)
    )
    attention_grad = hidden_grad.astype(jnp.bfloat16)
    grad_w_out = jnp.einsum(
        "td,te->de", attended, attention_grad, preferred_element_type=jnp.float32
    )
    attended_grad = jnp.einsum(
        "te,de->td", attention_grad, w_out, preferred_element_type=jnp.float32
    ).astype(jnp.bfloat16)
    query_grads = []
    key_grads = []
    value_grads = []
    for head in range(head_count):
        start = head * HD
        query_head = query_rot[:, start : start + HD]
        key_head = all_keys[:, start : start + HD]
        value_head = all_values[:, start : start + HD]
        out_grad_head = attended_grad[:, start : start + HD]
        recomputed = jnp.exp(head_scores(query_head, key_head) - log_totals[head])
        share_grad = jnp.einsum(
            "qd,kd->qk", out_grad_head, value_head, preferred_element_type=jnp.float32
        )
        delta = jnp.sum(recomputed * share_grad, axis=1, keepdims=True)
        score_grad = (recomputed * (share_grad - delta)).astype(jnp.bfloat16)
        query_grads.append(
            jnp.dot(score_grad, key_head, preferred_element_type=jnp.float32) * factor
        )
        key_grads.append(
            jnp.einsum("qk,qd->kd", score_grad, query_head, preferred_element_type=jnp.float32)
            * factor
        )
        value_grads.append(
            jnp.einsum(
                "qk,qd->kd",
                recomputed.astype(jnp.bfloat16),
                out_grad_head,
                preferred_element_type=jnp.float32,
            )
        )
    key_grad_all = jnp.concatenate(key_grads, axis=1)
    value_grad_all = jnp.concatenate(value_grads, axis=1)
    prompt_key_grad, prompt_value_grad = (
        lax.psum_scatter(
            key_grad_all[:prompt_count].astype(jnp.bfloat16),
            "expert",
            scatter_dimension=0,
            tiled=True,
        ).astype(jnp.float32),
        lax.psum_scatter(
            value_grad_all[:prompt_count].astype(jnp.bfloat16),
            "expert",
            scatter_dimension=0,
            tiled=True,
        ).astype(jnp.float32),
    )
    key_grad = jnp.concatenate([prompt_key_grad, key_grad_all[prompt_count:]], axis=0)
    value_grad = jnp.concatenate([prompt_value_grad, value_grad_all[prompt_count:]], axis=0)
    query_grad = unrotate(
        jnp.concatenate(query_grads, axis=1).reshape(rows, head_count, HD), cosine, sine
    ).reshape(rows, local_width)
    key_grad = unrotate(key_grad.reshape(rows, head_count, HD), cosine, sine).reshape(
        rows, local_width
    )
    grad_qk_gain = jnp.stack(
        [
            jnp.sum(query_grad * query_raw * scale_query, axis=0),
            jnp.sum(key_grad * key_raw * scale_key, axis=0),
        ],
        axis=0,
    )
    weighted_query = qk_gain[0] * query_grad
    weighted_key = qk_gain[1] * key_grad
    inner_sums = lax.psum(
        jnp.stack(
            [jnp.sum(weighted_query * query_raw, axis=1), jnp.sum(weighted_key * key_raw, axis=1)],
            axis=1,
        ),
        "tensor",
    )
    query_raw_grad = (
        scale_query * weighted_query - query_raw * (scale_query**3 / width) * inner_sums[:, 0:1]
    ).astype(jnp.bfloat16)
    key_raw_grad = (
        scale_key * weighted_key - key_raw * (scale_key**3 / width) * inner_sums[:, 1:2]
    ).astype(jnp.bfloat16)
    value_raw_grad = value_grad.astype(jnp.bfloat16)
    grad_w_query = jnp.einsum(
        "td,te->de", normed, query_raw_grad, preferred_element_type=jnp.float32
    )
    grad_w_key = jnp.einsum("td,te->de", normed, key_raw_grad, preferred_element_type=jnp.float32)
    grad_w_value = jnp.einsum(
        "td,te->de", normed, value_raw_grad, preferred_element_type=jnp.float32
    )
    normed_part = jnp.einsum(
        "te,de->td", query_raw_grad, w_query, preferred_element_type=jnp.float32
    )
    normed_part = normed_part + jnp.einsum(
        "te,de->td", key_raw_grad, w_key, preferred_element_type=jnp.float32
    )
    normed_part = normed_part + jnp.einsum(
        "te,de->td", value_raw_grad, w_value, preferred_element_type=jnp.float32
    )
    normed_grad = lax.psum(normed_part.astype(jnp.bfloat16), "tensor").astype(jnp.float32)
    weighted_one = attn_gain * normed_grad
    grad_attn_gain = jnp.sum(normed_grad * source * scale_one, axis=0)
    input_grad = (
        hidden_grad
        + scale_one * weighted_one
        - source * (scale_one**3 / width) * jnp.sum(weighted_one * source, axis=1, keepdims=True)
    )
    summed = (
        lax.psum_scatter(
            grad_w_query.astype(jnp.bfloat16), "expert", scatter_dimension=0, tiled=True
        ).astype(jnp.float32),
        lax.psum_scatter(
            grad_w_key.astype(jnp.bfloat16), "expert", scatter_dimension=0, tiled=True
        ).astype(jnp.float32),
        lax.psum_scatter(
            grad_w_value.astype(jnp.bfloat16), "expert", scatter_dimension=0, tiled=True
        ).astype(jnp.float32),
        lax.psum_scatter(
            grad_w_out.astype(jnp.bfloat16), "expert", scatter_dimension=1, tiled=True
        ).astype(jnp.float32),
        lax.psum_scatter(
            grad_attn_gain.astype(jnp.bfloat16), "expert", scatter_dimension=0, tiled=True
        ).astype(jnp.float32),
        lax.psum_scatter(
            grad_ffn_gain.astype(jnp.bfloat16), "expert", scatter_dimension=0, tiled=True
        ).astype(jnp.float32),
        lax.psum_scatter(
            grad_qk_gain.astype(jnp.bfloat16), "expert", scatter_dimension=1, tiled=True
        ).astype(jnp.float32),
        lax.psum_scatter(
            grad_router.astype(jnp.bfloat16), "expert", scatter_dimension=0, tiled=True
        ).astype(jnp.float32),
    )
    return (
        output,
        input_grad,
        summed[0],
        summed[1],
        summed[2],
        summed[3],
        summed[4],
        summed[5],
        summed[6],
        summed[7],
        grad_w_gate,
        grad_w_up,
        grad_w_down,
    )


def solution(mesh):
    return jax.shard_map(
        body,
        mesh=mesh,
        in_specs=(
            P("expert", None),
            P(None, "tensor"),
            P(None, "tensor"),
            P(None, "tensor"),
            P("tensor", None),
            P(),
            P(),
            P(None, "tensor"),
            P(),
            P("expert", None, "tensor"),
            P("expert", None, "tensor"),
            P("expert", "tensor", None),
            P("expert", None),
            P("expert"),
            P("expert", None),
        ),
        out_specs=(
            P("expert", None),
            P("expert", None),
            P("expert", "tensor"),
            P("expert", "tensor"),
            P("expert", "tensor"),
            P("tensor", "expert"),
            P("expert"),
            P("expert"),
            P(None, ("tensor", "expert")),
            P("expert", None),
            P("expert", None, "tensor"),
            P("expert", None, "tensor"),
            P("expert", "tensor", None),
        ),
        check_vma=False,
    )
```

profile of v0, /device:TPU:0, one launch (start us, length us, event | category | flops | bytes accessed | tf_op | source)
XLA Modules:
  0.0 1823.1 jit_solution(11396369852720098080)
XLA Ops:
  74.5 16.6 all-gather.5.cloned.1.call-done
  139.9 36.4 %gather_fusion.3 = f32[4608,2048]{1,0:T(8,128)} fusion(f32[384,2048]{1,0:T(8,128)} %convert_element_type.210, s32[5120]{0:T(1024)S(1)} %pad_clamp_fusion.1), kind=kCustom, calls=%fused_computation.3 | custom fusion | bytes 75515904 | tf_op jit(solution)/shard_map/gather | solution.py:207
  176.3 48.4 %all-reduce.8.cloned.1.call-done = f32[384,2048]{1,0:T(8,128)} async-done(((f32[384,2048]{1,0:T(8,128)}), f32[384,2048]{1,0:T(8,128)}) %all-reduce.8.cloned.1.call-update) | async-done | bytes 3145744 | tf_op jit(solution)/shard_map/psum | solution.py:155
  230.7 36.7 %gather_fusion = bf16[4608,2048]{1,0:T(8,128)(2,1)} fusion(bf16[384,2048]{1,0:T(8,128)(2,1)} %multiply_convert_fusion.3, s32[5120]{0:T(1024)S(1)} %pad_clamp_fusion.1), kind=kCustom, calls=%fused_computation | custom fusion | bytes 37767168 | tf_op jit(solution)/shard_map/gather | solution.py:181
  270.4 24.1 %gather_fusion.2 = f32[4608]{0:T(1024)S(1)} fusion(f32[3072]{0:T(1024)S(1)} %reshape.464, s32[5120]{0:T(1024)S(1)} %pad_clamp_fusion), kind=kCustom, calls=%fused_computation.2 | custom fusion | bytes 55296 | tf_op jit(solution)/shard_map/gather | solution.py:204
  294.6 31.9 %fusion.3 = (bf16[2,8,288,2048]{3,2,0,1:T(8,128)(2,1)}, bf16[2,8,288,2048]{3,2,0,1:T(8,128)(2,1)}) fusion(f32[2,8,288,2048]{3,2,1,0:T(8,128)} %bitcast.131, f32[2,8,288]{2,0,1:T(2,128)S(1)} %copy.123, pred[2,8,288]{2,0,1:T(4,128)(4,1)S(1)} %copy-done.99, bf16[2,8,288,2048]{3,2,1,0:T(8,128)(2,1)} %bitcast.135), kind=kLoop, calls=%fused_computation.15 | loop fusion | flops 37748736 | bytes 94394880 | tf_op jit(solution)/shard_map/jit(_where)/select_n | solution.py:205
  326.5 214.4 %all_to_all.20 = bf16[2,8,288,2048]{3,2,0,1:T(8,128)(2,1)} all-to-all(bf16[2,8,288,2048]{3,2,0,1:T(8,128)(2,1)} %get-tuple-element.57), channel_id=1, replica_groups=mesh['expert'=8,'tensor'=4] {'expert'}, dimensions={1} | all-to-all | bytes 37748736 | tf_op jit(solution)/shard_map/all_to_all | solution.py:35
  571.9 181.4 %all-to-all-done.2 = bf16[2,8,288,2048]{3,2,0,1:T(8,128)(2,1)} async-done(((bf16[2,8,288,2048]{3,2,0,1:T(8,128)(2,1)}), bf16[2,8,288,2048]{3,2,0,1:T(8,128)(2,1)}, u32[]{:S(2)}, u32[]{:S(2)}) %all-to-all-start.2) | async-done | bytes 18874400 | tf_op jit(solution)/shard_map/all_to_all | solution.py:35
  753.4 16.9 copy.125
  799.4 22.5 %add_convert_fusion = bf16[2,2304,2048]{2,1,0:T(8,128)(2,1)} fusion(f32[2,2304,2048]{2,1,0:T(8,128)} %fusion.148, bf16[2,2304,256]{2,1,0:T(8,128)(2,1)} %get-tuple-element.35, bf16[2,2048,256]{2,1,0:T(8,128)(2,1)} %param.25), kind=kOutput, calls=%fused_computation.9 | convolution fusion | flops 4850712576 | bytes 61079552 | tf_op jit(solution)/shard_map/jrf,jdf->jrd/dot_general | solution.py:223
  821.9 17.0 copy.126
  855.5 16.9 copy.120
  872.4 178.7 %all-to-all-done.3 = bf16[2,8,288,2048]{3,2,0,1:T(8,128)(2,1)} async-done(((bf16[2,8,288,2048]{3,2,0,1:T(8,128)(2,1)}), bf16[2,8,288,2048]{3,2,0,1:T(8,128)(2,1)}, u32[]{:S(2)}, u32[]{:S(2)}) %all-to-all-start.3) | async-done | bytes 18874400 | tf_op jit(solution)/shard_map/all_to_all | solution.py:39
  1057.1 17.0 copy.127
  1074.1 32.6 %gather_fusion.4 = bf16[3072,2048]{1,0:T(8,128)(2,1)} fusion(bf16[4608,2048]{1,0:T(8,128)(2,1)} %bitcast.130, s32[3072]{0:T(1024)S(1)} %broadcast_clamp_fusion), kind=kCustom, calls=%fused_computation.4 | custom fusion | bytes 25178112 | tf_op jit(solution)/shard_map/gather | solution.py:41
  1119.5 144.0 %all-to-all-done.1 = bf16[2,8,288,2048]{3,2,0,1:T(8,128)(2,1)} async-done(((bf16[2,8,288,2048]{3,2,0,1:T(8,128)(2,1)}), bf16[2,8,288,2048]{3,2,0,1:T(8,128)(2,1)}, u32[]{:S(2)}, u32[]{:S(2)}) %all-to-all-start.1) | async-done | bytes 18874400 | tf_op jit(solution)/shard_map/all_to_all | solution.py:39
  1263.5 16.9 copy.121
  1280.4 32.7 %gather_fusion.1 = bf16[3072,2048]{1,0:T(8,128)(2,1)} fusion(bf16[4608,2048]{1,0:T(8,128)(2,1)} %bitcast.129, s32[3072]{0:T(1024)S(1)} %broadcast_clamp_fusion), kind=kCustom, calls=%fused_computation.1 | custom fusion | bytes 25178112 | tf_op jit(solution)/shard_map/gather | solution.py:41
  1326.1 20.0 %psum.53 = f32[384,8]{1,0:T(8,128)S(1)} all-reduce(f32[384,8]{1,0:T(8,128)S(1)} %get-tuple-element.13), channel_id=1, replica_groups=mesh['expert'=8,'tensor'=4] {'tensor'}, use_global_device_ids=true, to_apply=%region_27.28 | all-reduce | flops 3072 | bytes 24576 | tf_op jit(solution)/shard_map/psum | solution.py:233
  1513.7 43.2 %reduce-scatter.21.cloned.1.call-done = bf16[512,256]{1,0:T(8,128)(2,1)} async-done(((bf16[512,2048]{1,0:T(8,128)(2,1)}), bf16[512,256]{1,0:T(8,128)(2,1)}) %reduce-scatter.21.cloned.1.call-update) | async-done | bytes 262160 | tf_op jit(solution)/shard_map/reduce_scatter | solution.py:369
  1558.7 43.0 %reduce-scatter.17.cloned.1.call-done = bf16[256,512]{1,0:T(8,128)(2,1)} async-done(((bf16[2048,512]{1,0:T(8,128)(2,1)}), bf16[256,512]{1,0:T(8,128)(2,1)}) %reduce-scatter.17.cloned.1.call-update) | async-done | bytes 262160 | tf_op jit(solution)/shard_map/reduce_scatter | solution.py:363
  1603.5 42.7 %reduce-scatter.15.cloned.1.call-done = bf16[256,512]{1,0:T(8,128)(2,1)} async-done(((bf16[2048,512]{1,0:T(8,128)(2,1)}), bf16[256,512]{1,0:T(8,128)(2,1)}) %reduce-scatter.15.cloned.1.call-update) | async-done | bytes 262160 | tf_op jit(solution)/shard_map/reduce_scatter | solution.py:360
  1648.0 122.6 %all-reduce.12.cloned.1.call-done = (bf16[384,2048]{1,0:T(8,128)(2,1)}, bf16[384,2048]{1,0:T(8,128)(2,1)}) async-done(((bf16[384,2048]{1,0:T(8,128)(2,1)}, bf16[384,2048]{1,0:T(8,128)(2,1)}), (bf16[384,2048]{1,0:T(8,128)(2,1)}, bf16[384,2048]{1,0:T(8,128)(2,1)})) %all-reduce.12.cloned.1.call-update) | async-done | bytes 3145744 | tf_op jit(solution)/shard_map/psum | solution.py:201
  1796.1 18.5 %reduce-scatter.19.cloned.1.call-done = bf16[256,512]{1,0:T(8,128)(2,1)} async-done(((bf16[2048,512]{1,0:T(8,128)(2,1)}), bf16[256,512]{1,0:T(8,128)(2,1)}) %reduce-scatter.19.cloned.1.call-update) | async-done | bytes 262160 | tf_op jit(solution)/shard_map/reduce_scatter | solution.py:366
  (490 shorter events, 430.6 us)
Async XLA Ops:
  7.2 763.1 %copy-start = (bf16[2,256,2048]{2,1,0:T(8,128)(2,1)S(1)}, bf16[2,256,2048]{2,1,0:T(8,128)(2,1)}, u32[]{:S(2)}) copy-start(bf16[2,256,2048]{2,1,0:T(8,128)(2,1)} %param.26) | copy-start | bytes 6291460
  7.2 57.9 %all-gather.3.cloned.1.call-start = ((), (), s32[]{:S(2)}) async-start(), calls=%async_computation.12 | async-start | bytes 1179648 | tf_op jit(solution)/shard_map/all_gather | solution.py:119
  9.8 33.4 %copy-start.114 = (f32[384]{0:T(512)}, f32[384]{0:T(512)S(1)}, u32[]{:S(2)}) copy-start(f32[384]{0:T(512)S(1)} %get-tuple-element.63) | copy-start | bytes 4612
  43.2 47.9 %all-gather.5.cloned.1.call-start = ((), (), s32[]{:S(2)}) async-start(), calls=%async_computation.13 | async-start | bytes 1179648 | tf_op jit(solution)/shard_map/all_gather | solution.py:120
  47.8 176.9 %all-reduce.8.cloned.1.call-start = ((), (), s32[]{:S(2)}) async-start(), calls=%async_computation.14 | async-start | bytes 6291456 | tf_op jit(solution)/shard_map/psum | solution.py:155
  53.4 45.6 %copy-start.35 = (bf16[256,512]{1,0:T(8,128)(2,1)}, bf16[256,512]{1,0:T(8,128)(2,1)S(1)}, u32[]{:S(2)}) copy-start(bf16[256,512]{1,0:T(8,128)(2,1)S(1)} %slice.212) | copy-start | bytes 786436
  176.3 52.9 %copy-start.93 = (f32[2048]{0:T(1024)S(1)}, f32[2048]{0:T(1024)}, u32[]{:S(2)}) copy-start(f32[2048]{0:T(1024)} %param.21) | copy-start | bytes 24580
  230.7 36.7 %copy-start.88 = (bf16[2048,16]{0,1:T(8,128)(2,1)S(1)}, bf16[2048,16]{0,1:T(8,128)(2,1)}, u32[]{:S(2)}) copy-start(bf16[2048,16]{0,1:T(8,128)(2,1)} %param.23) | copy-start | bytes 196612
  540.8 212.5 %all-to-all-start.2 = ((bf16[2,8,288,2048]{3,2,0,1:T(8,128)(2,1)}), bf16[2,8,288,2048]{3,2,0,1:T(8,128)(2,1)}, u32[]{:S(2)}, u32[]{:S(2)}) async-start(bf16[2,8,288,2048]{3,2,0,1:T(8,128)(2,1)} %get-tuple-element.56), calls=%async_computation.2 | async-start | bytes 37748736 | tf_op jit(solution)/shard_map/all_to_all | solution.py:35
  838.8 212.3 %all-to-all-start.3 = ((bf16[2,8,288,2048]{3,2,0,1:T(8,128)(2,1)}), bf16[2,8,288,2048]{3,2,0,1:T(8,128)(2,1)}, u32[]{:S(2)}, u32[]{:S(2)}) async-start(bf16[2,8,288,2048]{3,2,0,1:T(8,128)(2,1)} %copy.126), calls=%async_computation.3 | async-start | bytes 37748736 | tf_op jit(solution)/shard_map/all_to_all | solution.py:39
  872.4 184.7 %copy-start.98 = (s32[3072,1]{0,1:T(1,128)S(1)}, s32[3072,1]{0,1:T(1,128)}, u32[]{:S(2)}) copy-start(s32[3072,1]{0,1:T(1,128)} %copy-done.97) | copy-start | bytes 36868
  1051.1 212.4 %all-to-all-start.1 = ((bf16[2,8,288,2048]{3,2,0,1:T(8,128)(2,1)}), bf16[2,8,288,2048]{3,2,0,1:T(8,128)(2,1)}, u32[]{:S(2)}, u32[]{:S(2)}) async-start(bf16[2,8,288,2048]{3,2,0,1:T(8,128)(2,1)} %copy.120), calls=%async_computation.1 | async-start | bytes 37748736 | tf_op jit(solution)/shard_map/all_to_all | solution.py:39
  1057.1 289.3 %all-reduce.10.cloned.1.call-start = ((), (), s32[]{:S(2)}) async-start(), calls=%async_computation.15 | async-start | bytes 6291456 | tf_op jit(solution)/shard_map/psum | solution.py:233
  1118.8 283.4 %reduce-scatter.25.cloned.1.call-start = ((), (), s32[]{:S(2)}) async-start(), calls=%async_computation.21 | async-start | bytes 1179648
  1313.1 33.3 %copy-start.89 = (bf16[2048,16]{0,1:T(8,128)(2,1)S(1)}, bf16[2048,16]{0,1:T(8,128)(2,1)}, u32[]{:S(2)}) copy-start(bf16[2048,16]{0,1:T(8,128)(2,1)} %param.23) | copy-start | bytes 196612
  1313.1 33.3 %copy-start.94 = (f32[2048]{0:T(1024)S(1)}, f32[2048]{0:T(1024)}, u32[]{:S(2)}) copy-start(f32[2048]{0:T(1024)} %param.21) | copy-start | bytes 24580
  1369.4 78.1 %reduce-scatter.27.cloned.1.call-start = ((), (), s32[]{:S(2)}) async-start(), calls=%async_computation.22 | async-start | bytes 1179648
  1379.2 117.9 %reduce-scatter.23.cloned.1.call-start = ((), (), s32[]{:S(2)}) async-start(), calls=%async_computation.20 | async-start | bytes 73728 | tf_op jit(solution)/shard_map/reduce_scatter | solution.py:381
  1381.6 130.7 %reduce-scatter.29.cloned.1.call-start = ((), (), s32[]{:S(2)}) async-start(), calls=%async_computation.23 | async-start | bytes 147456
  1414.9 142.0 %reduce-scatter.21.cloned.1.call-start = ((), (), s32[]{:S(2)}) async-start(), calls=%async_computation.19 | async-start | bytes 2359296 | tf_op jit(solution)/shard_map/reduce_scatter | solution.py:369
  1419.6 182.1 %reduce-scatter.17.cloned.1.call-start = ((), (), s32[]{:S(2)}) async-start(), calls=%async_computation.17 | async-start | bytes 2359296 | tf_op jit(solution)/shard_map/reduce_scatter | solution.py:363
  1437.9 208.3 %reduce-scatter.15.cloned.1.call-start = ((), (), s32[]{:S(2)}) async-start(), calls=%async_computation.16 | async-start | bytes 2359296 | tf_op jit(solution)/shard_map/reduce_scatter | solution.py:360
  1444.8 325.8 %all-reduce.12.cloned.1.call-start = ((), (), s32[]{:S(2)}) async-start(), calls=%async_computation.24 | async-start | bytes 6291456 | tf_op jit(solution)/shard_map/psum | solution.py:201
  1455.2 359.3 %reduce-scatter.19.cloned.1.call-start = ((), (), s32[]{:S(2)}) async-start(), calls=%async_computation.18 | async-start | bytes 2359296 | tf_op jit(solution)/shard_map/reduce_scatter | solution.py:366
  (129 other events, 867.2 us)
Sparse Core Ops, SparseCore 0:
  43.3 21.7 all-gather.2
  67.5 23.4 all-gather.4
  103.5 121.1 all-reduce.7
  1118.9 120.4 all-reduce.9
  1369.5 32.7 reduce-scatter.24
  1405.3 35.9 reduce-scatter.26
  1444.3 31.3 reduce-scatter.22
  1478.9 33.3 reduce-scatter.28
  1515.6 41.2 reduce-scatter.20
  1560.4 41.2 reduce-scatter.16
  1605.0 41.1 reduce-scatter.14
  1649.2 121.4 all-reduce.11
  1774.3 40.2 reduce-scatter.18
where the time goes:
time: 1830 us; the launch traced here: 1820 us
  waiting for transfers between devices  873 us (48%)
  local copies, waits for them, and re-layouts  335 us (18%)
  blocking collectives  273 us (15%)
  matrix products  184 us (10%)
  other arithmetic  121 us (7%)
  starting transfers between devices  19.3 us (1%)
    all_to_all x2, waiting for transfers between devices, return_rows(): lax.all_to_all(parts, 'expert', split_axis=1, concat_axis=1, tiled=True)  323 us
    all_to_all x1, blocking collectives, send_rows(): lax.all_to_all(buffer, 'expert', split_axis=1, concat_axis=1, tiled=True)  214 us
    all_to_all x1, waiting for transfers between devices, send_rows(): lax.all_to_all(buffer, 'expert', split_axis=1, concat_axis=1, tiled=True)  181 us
    psum x1, waiting for transfers between devices, body(): lax.psum(mixed_part.astype(jnp.bfloat16), 'tensor').astype(jnp.float32)  123 us
    gather x2, local copies, waits for them, and re-layouts, return_rows(): flat_rows[slot_index].reshape(rows, route_width, moved.shape[3])  65.3 us
    psum x1, waiting for transfers between devices, body(): lax.psum(jnp.dot(attended, w_out, preferred_element_type=jnp.float32), 't...  48.4 us
    reduce_scatter x1, waiting for transfers between devices, body(): lax.psum_scatter(grad_w_out.astype(jnp.bfloat16), 'expert', scatter_dimen...  43.2 us
    reduce_scatter x1, waiting for transfers between devices, body(): lax.psum_scatter(grad_w_key.astype(jnp.bfloat16), 'expert', scatter_dimen...  43 us
  transfers between devices with their start and end apart: 16, of which 13 were waited for; matrix products, arithmetic and copies ran while one was open for 21% of the time, Pallas kernels for 0%

commit v1 on v0

--- a/solution.py
+++ b/solution.py
@@ -31,15 +31,48 @@
     )
 
 
-def send_rows(buffer):
-    return lax.all_to_all(buffer, "expert", split_axis=1, concat_axis=1, tiled=True)
-
-
-def return_rows(parts, slot_index, rows, route_width, weights):
-    moved = lax.all_to_all(parts, "expert", split_axis=1, concat_axis=1, tiled=True)
-    flat_rows = moved.reshape(-1, moved.shape[3])
-    picked = flat_rows[slot_index].reshape(rows, route_width, moved.shape[3]).astype(jnp.float32)
-    return (jnp.sum(weights[:, :, None] * picked, axis=1), picked)
+def experts(normed_two, cotangent, gates, w_gate, w_up, w_down, experts_total):
+    local_experts = w_gate.shape[0]
+    device = lax.axis_index("expert")
+    arrived = lax.all_gather(normed_two, "expert", axis=0, tiled=True)
+    arrived_grad = lax.all_gather(cotangent, "expert", axis=0, tiled=True)
+    gate_pre = jnp.einsum("rd,jdf->jrf", arrived, w_gate, preferred_element_type=jnp.float32)
+    up_pre = jnp.einsum("rd,jdf->jrf", arrived, w_up, preferred_element_type=jnp.float32)
+    raw_grad = jnp.einsum("rd,jfd->jrf", arrived_grad, w_down, preferred_element_type=jnp.float32)
+    sigma = jax.nn.sigmoid(gate_pre)
+    activated = gate_pre * sigma
+    inner = activated * up_pre
+    gated = (gates[:, :, None] * inner).astype(jnp.bfloat16)
+    mixed_part = jnp.einsum("jrf,jfd->rd", gated, w_down, preferred_element_type=jnp.float32)
+    mixture = lax.psum(
+        lax.psum_scatter(
+            mixed_part.astype(jnp.bfloat16), "expert", scatter_dimension=0, tiled=True
+        ),
+        "tensor",
+    ).astype(jnp.float32)
+    gate_grad_part = jnp.sum(raw_grad * inner, axis=2)
+    act_grad = gates[:, :, None] * raw_grad
+    up_grad = (act_grad * activated).astype(jnp.bfloat16)
+    gate_grad = (act_grad * up_pre * sigma * (1.0 + gate_pre * (1.0 - sigma))).astype(jnp.bfloat16)
+    grad_w_down = jnp.einsum("jrf,rd->jfd", gated, arrived_grad, preferred_element_type=jnp.float32)
+    grad_w_gate = jnp.einsum("rd,jrf->jdf", arrived, gate_grad, preferred_element_type=jnp.float32)
+    grad_w_up = jnp.einsum("rd,jrf->jdf", arrived, up_grad, preferred_element_type=jnp.float32)
+    slot_grad = jnp.einsum("jrf,jdf->rd", gate_grad, w_gate, preferred_element_type=jnp.float32)
+    slot_grad = slot_grad + jnp.einsum(
+        "jrf,jdf->rd", up_grad, w_up, preferred_element_type=jnp.float32
+    )
+    moe_input_grad = lax.psum(
+        lax.psum_scatter(
+            slot_grad.astype(jnp.bfloat16), "expert", scatter_dimension=0, tiled=True
+        ),
+        "tensor",
+    ).astype(jnp.float32)
+    placed = jnp.zeros((arrived.shape[0], experts_total), jnp.float32)
+    placed = lax.dynamic_update_slice_in_dim(placed, gate_grad_part.T, device * local_experts, 1)
+    chance_grad = lax.psum(
+        lax.psum_scatter(placed, "expert", scatter_dimension=0, tiled=True), "tensor"
+    )
+    return mixture, moe_input_grad, chance_grad, [grad_w_gate, grad_w_up, grad_w_down]
 
 
 def body(
@@ -64,12 +97,10 @@
     head_count = local_width // HD
     experts_total = router.shape[1]
     local_experts = w_gate.shape[0]
-    route_width = routes.shape[1]
     ranks = lax.axis_size("expert")
     device = lax.axis_index("expert")
     span = ranks // 2
     prompt_len = PROMPT_DEV * span
-    capacity = rows * route_width * 3 // (2 * experts_total)
     factor = HD ** (-0.5)
     local = jnp.arange(rows, dtype=jnp.int32)
     is_prompt = local < PROMPT_DEV
@@ -163,75 +194,40 @@
     hits = (routes[:, :, None] == jnp.arange(experts_total, dtype=jnp.int32)[None, None, :]).astype(
         jnp.float32
     )
-    gates = jnp.sum(hits * chances[:, None, :], axis=2)
-    flat_expert = routes.reshape(-1)
-    one_hot = (flat_expert[:, None] == jnp.arange(experts_total, dtype=jnp.int32)[None, :]).astype(
-        jnp.int32
-    )
-    earlier = jnp.cumsum(one_hot, axis=0) - one_hot
-    rank = jnp.sum(earlier * one_hot, axis=1)
-    owner = flat_expert // local_experts
-    which = flat_expert % local_experts
-    slot_index = (which * ranks + owner) * capacity + rank
-    buffer_rows = local_experts * ranks * capacity
-    pick_index = jnp.arange(flat_expert.shape[0], dtype=jnp.int32)
-    slot_pick = jnp.zeros((buffer_rows,), jnp.int32).at[slot_index].set(pick_index)
-    slot_used = jnp.zeros((buffer_rows,), jnp.bool_).at[slot_index].set(True)
-    slot_token = slot_pick // route_width
-    outgoing = jnp.where(slot_used[:, None], normed_two[slot_token], jnp.zeros((), jnp.bfloat16))
-    arrived = send_rows(outgoing.reshape(local_experts, ranks, capacity, width)).reshape(
-        local_experts, ranks * capacity, width
-    )
-    gate_pre = jnp.einsum("jrd,jdf->jrf", arrived, w_gate, preferred_element_type=jnp.float32)
-    up_pre = jnp.einsum("jrd,jdf->jrf", arrived, w_up, preferred_element_type=jnp.float32)
-    sigma = jax.nn.sigmoid(gate_pre)
-    activated = gate_pre * sigma
-    inner = (activated * up_pre).astype(jnp.bfloat16)
-    expert_out = jnp.einsum(
-        "jrf,jfd->jrd", inner, w_down, preferred_element_type=jnp.float32
-    ).astype(jnp.bfloat16)
-    mixed_part, picked = return_rows(
-        expert_out.reshape(local_experts, ranks, capacity, width),
-        slot_index,
-        rows,
-        route_width,
-        gates,
-    )
+    rows_mask = jnp.sum(hits, axis=1)
+    routed = lax.all_gather(
+        (rows_mask * chances).astype(jnp.float32), "expert", axis=0, tiled=True
+    )
+    gates = lax.dynamic_slice_in_dim(routed, device * local_experts, local_experts, 1).T
     grad_out = cotangent.astype(jnp.float32)
-    mixture = lax.psum(mixed_part.astype(jnp.bfloat16), "tensor").astype(jnp.float32)
+    pieces = max(1, ranks * rows // 4096)
+    piece = rows // pieces
+    split_gates = gates.reshape(local_experts, ranks, rows)
+    results = []
+    weight_grads = None
+    for number in range(pieces):
+        part = slice(number * piece, (number + 1) * piece)
+        sources = (normed_two[part], cotangent[part])
+        if results:
+            sources, results, weight_grads = lax.optimization_barrier(
+                (sources, results, weight_grads)
+            )
+        *result, grads = experts(
+            *sources,
+            split_gates[:, :, part].reshape(local_experts, ranks * piece),
+            w_gate,
+            w_up,
+            w_down,
+            experts_total,
+        )
+        results.append(result)
+        weight_grads = grads if weight_grads is None else [a + b for a, b in zip(weight_grads, grads)]
+    mixture, moe_input_grad, chance_grad = (
+        jnp.concatenate(list(group_of), axis=0) for group_of in zip(*results)
+    )
+    grad_w_gate, grad_w_up, grad_w_down = weight_grads
+    chance_grad = rows_mask * chance_grad
     output = (hidden + mixture).astype(jnp.bfloat16)
-    gate_grad_part = jnp.sum(grad_out[:, None, :] * picked, axis=2)
-    slot_gate = gates.reshape(-1)[slot_pick]
-    outgoing_grad = jnp.where(
-        slot_used[:, None],
-        (slot_gate[:, None] * grad_out[slot_token]).astype(jnp.bfloat16),
-        jnp.zeros((), jnp.bfloat16),
-    )
-    arrived_grad = send_rows(outgoing_grad.reshape(local_experts, ranks, capacity, width)).reshape(
-        local_experts, ranks * capacity, width
-    )
-    act_grad = jnp.einsum("jrd,jfd->jrf", arrived_grad, w_down, preferred_element_type=jnp.float32)
-    up_grad = (act_grad * activated).astype(jnp.bfloat16)
-    gate_grad = (act_grad * up_pre * sigma * (1.0 + gate_pre * (1.0 - sigma))).astype(jnp.bfloat16)
-    grad_w_down = jnp.einsum(
-        "jrf,jrd->jfd", inner, arrived_grad, preferred_element_type=jnp.float32
-    )
-    grad_w_gate = jnp.einsum("jrd,jrf->jdf", arrived, gate_grad, preferred_element_type=jnp.float32)
-    grad_w_up = jnp.einsum("jrd,jrf->jdf", arrived, up_grad, preferred_element_type=jnp.float32)
-    slot_grad = jnp.einsum("jrf,jdf->jrd", gate_grad, w_gate, preferred_element_type=jnp.float32)
-    slot_grad = (
-        slot_grad + jnp.einsum("jrf,jdf->jrd", up_grad, w_up, preferred_element_type=jnp.float32)
-    ).astype(jnp.bfloat16)
-    unit_weights = jnp.ones((rows, route_width), jnp.float32)
-    input_part, unused = return_rows(
-        slot_grad.reshape(local_experts, ranks, capacity, width),
-        slot_index,
-        rows,
-        route_width,
-        unit_weights,
-    )
-    moe_input_grad, gate_grad_all = lax.psum((input_part, gate_grad_part), "tensor")
-    chance_grad = jnp.sum(hits * gate_grad_all[:, :, None], axis=1)
     logit_grad = (
         chances * (chance_grad - jnp.sum(chances * chance_grad, axis=1, keepdims=True))
     ).astype(jnp.bfloat16)

time: 1830 us -> 1210 us (0.66)
  local copies, waits for them, and re-layouts: 335 us -> 56.8 us
  blocking collectives: 273 us -> 69.4 us
  waiting for transfers between devices: 873 us -> 805 us
  other arithmetic: 121 us -> 59.5 us
    all_to_all x3 -> x0, waiting for transfers between devices: 504 us -> none  [the longest x2 323 us: return_rows(): lax.all_to_all(parts, 'expert', split_axis=1, concat_axis=1, tiled=True)]
    all_to_all x1 -> x0, blocking collectives: 214 us -> none  [send_rows(): lax.all_to_all(buffer, 'expert', split_axis=1, concat_axis=1, tiled=True)]
    reduce_scatter x0 -> x3, waiting for transfers between devices: none -> 205 us  [the longest x1 91.1 us: experts(): lax.psum_scatter(slot_grad.astype(jnp.bfloat16), 'expert', scatter_dimens...]
    gather x5 -> x0, local copies, waits for them, and re-layouts: 162 us -> none  [the longest x2 65.3 us: return_rows(): flat_rows[slot_index].reshape(rows, route_width, moved.shape[3])]
    all_gather x0 -> x2, waiting for transfers between devices: none -> 110 us  [the longest x1 58 us: experts(): arrived = lax.all_gather(normed_two, 'expert', axis=0, tiled=True)]
    psum x1, waiting for transfers between devices: 48.4 us -> 121 us  [body(): lax.psum(jnp.dot(attended, w_out, preferred_element_type=jnp.float32), 't...]
    all_to_all x4 -> x0, local copies, waits for them, and re-layouts: 60.7 us -> none  [the longest x2 33.9 us: return_rows(): lax.all_to_all(parts, 'expert', split_axis=1, concat_axis=1, tiled=True)]
    psum x2, waiting for transfers between devices: 123 us -> 173 us  [the longest x1 123 us: experts(): lax.psum(lax.psum_scatter(mixed_part.astype(jnp.bfloat16), 'expert', scat...]
  transfers between devices with their start and end apart: 16 -> 18, of which waited for: 13 -> 16; matrix products, arithmetic and copies ran while one was open for 21% -> 16% of each run, Pallas kernels for 0% -> 0%
where the time goes in v1:
time: 1210 us; the launch traced here: 1200 us
  waiting for transfers between devices  805 us (67%)
  matrix products  193 us (16%)
  blocking collectives  69.4 us (6%)
  other arithmetic  59.5 us (5%)
  local copies, waits for them, and re-layouts  56.8 us (5%)
  between operations  17.4 us (1%)
    psum x1, waiting for transfers between devices, experts(): lax.psum(lax.psum_scatter(mixed_part.astype(jnp.bfloat16), 'expert', scat...  123 us
    psum x1, waiting for transfers between devices, body(): lax.psum(jnp.dot(attended, w_out, preferred_element_type=jnp.float32), 't...  121 us
    reduce_scatter x1, waiting for transfers between devices, experts(): lax.psum_scatter(slot_grad.astype(jnp.bfloat16), 'expert', scatter_dimens...  91.1 us
    reduce_scatter x1, waiting for transfers between devices, experts(): lax.psum_scatter(mixed_part.astype(jnp.bfloat16), 'expert', scatter_dimen...  82.6 us
    all_gather x1, waiting for transfers between devices, experts(): arrived = lax.all_gather(normed_two, 'expert', axis=0, tiled=True)  58 us
    all_gather x1, waiting for transfers between devices, experts(): arrived_grad = lax.all_gather(cotangent, 'expert', axis=0, tiled=True)  51.8 us
    psum x1, waiting for transfers between devices, experts(): lax.psum(lax.psum_scatter(slot_grad.astype(jnp.bfloat16), 'expert', scatt...  50.6 us
    unnamed x252, local copies, waits for them, and re-layouts  45.8 us
  transfers between devices with their start and end apart: 18, of which 16 were waited for; matrix products, arithmetic and copies ran while one was open for 16% of the time, Pallas kernels for 0%

profile of v1, /device:TPU:0, one launch (start us, length us, event | category | flops | bytes accessed | tf_op | source)
XLA Modules:
  0.0 1202.4 jit_solution(7009935029459759188)
XLA Ops:
  16.0 13.4 %psum.49 = f32[384,2]{0,1:T(2,128)S(1)} all-reduce(f32[384,2]{0,1:T(2,128)S(1)} %pad_maximum_fusion.14), channel_id=1, replica_groups=mesh['expert'=8,'tensor'=4] {'tensor'}, use_global_device_ids=true, to_apply=%region_3.4 | all-reduce | flops 768 | bytes 6144 | tf_op jit(solution)/shard_map/psum | solution.py:130
  74.4 16.7 %all-gather.7.cloned.1.call-done = bf16[1024,512]{1,0:T(8,128)(2,1)} async-done(((bf16[128,512]{1,0:T(8,128)(2,1)}), bf16[1024,512]{1,0:T(8,128)(2,1)}) %all-gather.7.cloned.1.call-update) | async-done | bytes 1048592 | tf_op jit(solution)/shard_map/all_gather | solution.py:151
  103.4 121.2 %all-reduce.8.cloned.1.call-done = f32[384,2048]{1,0:T(8,128)} async-done(((f32[384,2048]{1,0:T(8,128)}), f32[384,2048]{1,0:T(8,128)}) %all-reduce.8.cloned.1.call-update) | async-done | bytes 3145744 | tf_op jit(solution)/shard_map/psum | solution.py:186
  243.9 58.0 %all-gather.9.cloned.1.call-done = bf16[3072,2048]{1,0:T(8,128)(2,1)} async-done(((bf16[384,2048]{1,0:T(8,128)(2,1)}), bf16[3072,2048]{1,0:T(8,128)(2,1)}) %all-gather.9.cloned.1.call-update) | async-done | bytes 12582928 | tf_op jit(solution)/shard_map/all_gather | solution.py:37
  301.9 13.1 %fusion.9 = f32[3072,2,256]{0,2,1:T(8,128)} fusion(bf16[2,2048,256]{2,1,0:T(8,128)(2,1)} %param.25, bf16[3072,2048]{1,0:T(8,128)(2,1)} %all-gather.9.cloned.1.call-done), kind=kOutput, calls=%fused_computation.11 | convolution fusion | flops 6442450944 | bytes 20971520 | tf_op jit(solution)/shard_map/rd,jdf->jrf/dot_general | solution.py:40
  324.0 51.8 %all-gather.11.cloned.1.call-done = bf16[3072,2048]{1,0:T(8,128)(2,1)} async-done(((bf16[384,2048]{1,0:T(8,128)(2,1)}), bf16[3072,2048]{1,0:T(8,128)(2,1)}) %all-gather.11.cloned.1.call-update) | async-done | bytes 12582928 | tf_op jit(solution)/shard_map/all_gather | solution.py:38
  375.8 22.7 %fusion.13 = (f32[2,3072]{1,0:T(2,128)S(1)}, bf16[2,3072,256]{1,2,0:T(8,128)(2,1)}, bf16[2,3072,256]{1,2,0:T(8,128)(2,1)}, bf16[2,3072,256]{1,2,0:T(8,128)(2,1)}) fusion(f32[3072,2,256]{0,2,1:T(8,128)} %fusion.9, f32[3072,2,256]{0,2,1:T(8,128)} %fusion.11, f32[2,3072]{1,0:T(2,128)} %dynamic-slice_bitcast_fusion, bf16[2,256,2048]{2,1,0:T(8,128)(2,1)S(1)} %copy-done, ...), kind=kOutput, calls=%fused_computation.23 | convolution fusion | flops 6472329216 | bytes 36749312 | tf_op jit(solution)/shard_map/rd,jfd->jrf/dot_general | solution.py:41
  398.5 14.4 %fusion.157 = f32[3072,2048,1]{1,0,2:T(8,128)} fusion(bf16[2,3072,256]{1,2,0:T(8,128)(2,1)} %get-tuple-element.88, bf16[2,2048,256]{2,1,0:T(8,128)(2,1)} %param.24), kind=kOutput, calls=%fused_computation.295 | convolution fusion | flops 6442450944 | bytes 30408704 | tf_op jit(solution)/shard_map/jrf,jdf->rd/dot_general | solution.py:60
  412.9 15.9 %fusion = bf16[3072,2048]{1,0:T(8,128)(2,1)} fusion(f32[3072,2048,1]{1,0,2:T(8,128)} %fusion.157, bf16[2,3072,256]{1,2,0:T(8,128)(2,1)} %get-tuple-element.90, bf16[2,2048,256]{2,1,0:T(8,128)(2,1)} %param.25), kind=kOutput, calls=%fused_computation.1 | convolution fusion | flops 6455033856 | bytes 42991616 | tf_op jit(solution)/shard_map/jrf,jdf->rd/dot_general | solution.py:61
  430.2 91.1 %reduce-scatter.20.cloned.1.call-done = bf16[384,2048]{1,0:T(8,128)(2,1)} async-done(((bf16[3072,2048]{1,0:T(8,128)(2,1)}), bf16[384,2048]{1,0:T(8,128)(2,1)}) %reduce-scatter.20.cloned.1.call-update) | async-done | bytes 1572880 | tf_op jit(solution)/shard_map/reduce_scatter | solution.py:65
  526.5 31.1 %reduce-scatter.22.cloned.1.call-done = f32[384,16]{0,1:T(8,128)} async-done(((f32[3072,16]{0,1:T(8,128)}), f32[384,16]{0,1:T(8,128)}) %reduce-scatter.22.cloned.1.call-update) | async-done | bytes 24592 | tf_op jit(solution)/shard_map/reduce_scatter | solution.py:73
  557.7 20.5 %psum.53 = f32[384,16]{0,1:T(8,128)S(1)} all-reduce(f32[384,16]{0,1:T(8,128)} %reduce-scatter.22.cloned.1.call-done), channel_id=1, replica_groups=mesh['expert'=8,'tensor'=4] {'tensor'}, use_global_device_ids=true, to_apply=%region_23.24 | all-reduce | flops 6144 | bytes 49152 | tf_op jit(solution)/shard_map/psum | solution.py:72
  579.0 50.6 %all-reduce.10.cloned.1.call-done = bf16[384,2048]{1,0:T(8,128)(2,1)} async-done(((bf16[384,2048]{1,0:T(8,128)(2,1)}), bf16[384,2048]{1,0:T(8,128)(2,1)}) %all-reduce.10.cloned.1.call-update) | async-done | bytes 1572880 | tf_op jit(solution)/shard_map/psum | solution.py:64
  657.9 12.0 bitcast_convert_fusion
  738.2 82.6 %reduce-scatter.18.cloned.1.call-done = bf16[384,2048]{1,0:T(8,128)(2,1)} async-done(((bf16[3072,2048]{1,0:T(8,128)(2,1)}), bf16[384,2048]{1,0:T(8,128)(2,1)}) %reduce-scatter.18.cloned.1.call-update) | async-done | bytes 1572880 | tf_op jit(solution)/shard_map/reduce_scatter | solution.py:48
  821.0 11.9 fusion.25
  859.7 11.9 fusion.1
  872.9 18.9 %reduce-scatter.38.cloned.1.call-done = bf16[64,2]{1,0:T(8,128)(2,1)} async-done(((bf16[512,2]{1,0:T(8,128)(2,1)}), bf16[64,2]{1,0:T(8,128)(2,1)}) %reduce-scatter.38.cloned.1.call-update) | async-done | bytes 272
  893.1 43.1 %reduce-scatter.30.cloned.1.call-done = bf16[512,256]{1,0:T(8,128)(2,1)} async-done(((bf16[512,2048]{1,0:T(8,128)(2,1)}), bf16[512,256]{1,0:T(8,128)(2,1)}) %reduce-scatter.30.cloned.1.call-update) | async-done | bytes 262160 | tf_op jit(solution)/shard_map/reduce_scatter | solution.py:365
  938.0 43.0 %reduce-scatter.26.cloned.1.call-done = bf16[256,512]{1,0:T(8,128)(2,1)} async-done(((bf16[2048,512]{1,0:T(8,128)(2,1)}), bf16[256,512]{1,0:T(8,128)(2,1)}) %reduce-scatter.26.cloned.1.call-update) | async-done | bytes 262160 | tf_op jit(solution)/shard_map/reduce_scatter | solution.py:359
  982.8 42.6 %reduce-scatter.24.cloned.1.call-done = bf16[256,512]{1,0:T(8,128)(2,1)} async-done(((bf16[2048,512]{1,0:T(8,128)(2,1)}), bf16[256,512]{1,0:T(8,128)(2,1)}) %reduce-scatter.24.cloned.1.call-update) | async-done | bytes 262160 | tf_op jit(solution)/shard_map/reduce_scatter | solution.py:356
  1027.2 122.6 %all-reduce.12.cloned.1.call-done = (bf16[384,2048]{1,0:T(8,128)(2,1)}, bf16[384,2048]{1,0:T(8,128)(2,1)}) async-done(((bf16[384,2048]{1,0:T(8,128)(2,1)}, bf16[384,2048]{1,0:T(8,128)(2,1)}), (bf16[384,2048]{1,0:T(8,128)(2,1)}, bf16[384,2048]{1,0:T(8,128)(2,1)})) %all-reduce.12.cloned.1.call-update) | async-done | bytes 3145744 | tf_op jit(solution)/shard_map/psum | solution.py:47
  1152.7 13.9 %all-reduce.2 = (bf16[2048]{0:T(1024)(128)(2,1)S(1)}, bf16[2048]{0:T(1024)(128)(2,1)S(1)}) all-reduce(bf16[2048]{0:T(1024)(128)(2,1)S(1)} %get-tuple-element.67, bf16[2048]{0:T(1024)(128)(2,1)S(1)} %copy-done.101), channel_id=11, replica_groups=mesh['expert'=8,'tensor'=4] {'expert'}, use_global_device_ids=true, to_apply=%region_42.43.clone | all-reduce | flops 4096 | bytes 16384
  1175.2 18.3 %reduce-scatter.28.cloned.1.call-done = bf16[256,512]{1,0:T(8,128)(2,1)} async-done(((bf16[2048,512]{1,0:T(8,128)(2,1)}), bf16[256,512]{1,0:T(8,128)(2,1)}) %reduce-scatter.28.cloned.1.call-update) | async-done | bytes 262160 | tf_op jit(solution)/shard_map/reduce_scatter | solution.py:362
  (424 shorter events, 243.6 us)
Async XLA Ops:
  7.2 368.6 %copy-start = (bf16[2,256,2048]{2,1,0:T(8,128)(2,1)S(1)}, bf16[2,256,2048]{2,1,0:T(8,128)(2,1)}, u32[]{:S(2)}) copy-start(bf16[2,256,2048]{2,1,0:T(8,128)(2,1)} %param.26) | copy-start | bytes 6291460
  7.2 57.9 %all-gather.5.cloned.1.call-start = ((), (), s32[]{:S(2)}) async-start(), calls=%async_computation.11 | async-start | bytes 1179648 | tf_op jit(solution)/shard_map/all_gather | solution.py:150
  43.2 47.8 %all-gather.7.cloned.1.call-start = ((), (), s32[]{:S(2)}) async-start(), calls=%async_computation.12 | async-start | bytes 1179648 | tf_op jit(solution)/shard_map/all_gather | solution.py:151
  47.8 176.7 %all-reduce.8.cloned.1.call-start = ((), (), s32[]{:S(2)}) async-start(), calls=%async_computation.13 | async-start | bytes 6291456 | tf_op jit(solution)/shard_map/psum | solution.py:186
  103.3 125.8 %copy-start.78 = (f32[2048]{0:T(1024)S(1)}, f32[2048]{0:T(1024)}, u32[]{:S(2)}) copy-start(f32[2048]{0:T(1024)} %param.21) | copy-start | bytes 24580
  103.3 198.5 %all-gather.9.cloned.1.call-start = ((), (), s32[]{:S(2)}) async-start(), calls=%async_computation.14 | async-start | bytes 14155776 | tf_op jit(solution)/shard_map/all_gather | solution.py:37
  230.6 145.2 %all-gather.11.cloned.1.call-start = ((), (), s32[]{:S(2)}) async-start(), calls=%async_computation.16 | async-start | bytes 14155776 | tf_op jit(solution)/shard_map/all_gather | solution.py:38
  231.2 290.2 %reduce-scatter.20.cloned.1.call-start = ((), (), s32[]{:S(2)}) async-start(), calls=%async_computation.17 | async-start | bytes 14155776 | tf_op jit(solution)/shard_map/reduce_scatter | solution.py:65
  233.4 344.8 %copy-start.83 = (f32[384]{0:T(512)}, f32[384]{0:T(512)S(1)}, u32[]{:S(2)}) copy-start(f32[384]{0:T(512)S(1)} %fusion.101) | copy-start | bytes 4612
  428.8 128.9 %reduce-scatter.22.cloned.1.call-start = ((), (), s32[]{:S(2)}) async-start(), calls=%async_computation.19 | async-start | bytes 221184 | tf_op jit(solution)/shard_map/reduce_scatter | solution.py:73
  430.2 199.5 %all-reduce.10.cloned.1.call-start = ((), (), s32[]{:S(2)}) async-start(), calls=%async_computation.18 | async-start | bytes 3145728 | tf_op jit(solution)/shard_map/psum | solution.py:64
  521.4 163.8 %reduce-scatter.34.cloned.1.call-start = ((), (), s32[]{:S(2)}) async-start(), calls=%async_computation.25 | async-start | bytes 1179648
  579.0 54.9 %copy-start.79 = (f32[2048]{0:T(1024)S(1)}, f32[2048]{0:T(1024)}, u32[]{:S(2)}) copy-start(f32[2048]{0:T(1024)} %param.21) | copy-start | bytes 24580
  579.0 54.9 %copy-start.82 = (f32[384]{0:T(512)S(1)}, f32[384]{0:T(512)}, u32[]{:S(2)}) copy-start(f32[384]{0:T(512)} %copy-done.81) | copy-start | bytes 4612
  650.0 80.4 %reduce-scatter.36.cloned.1.call-start = ((), (), s32[]{:S(2)}) async-start(), calls=%async_computation.26 | async-start | bytes 1179648
  657.8 163.0 %reduce-scatter.18.cloned.1.call-start = ((), (), s32[]{:S(2)}) async-start(), calls=%async_computation.15 | async-start | bytes 14155776 | tf_op jit(solution)/shard_map/reduce_scatter | solution.py:48
  669.9 201.7 %reduce-scatter.32.cloned.1.call-start = ((), (), s32[]{:S(2)}) async-start(), calls=%async_computation.24 | async-start | bytes 73728 | tf_op jit(solution)/shard_map/reduce_scatter | solution.py:377
  672.4 219.3 %reduce-scatter.38.cloned.1.call-start = ((), (), s32[]{:S(2)}) async-start(), calls=%async_computation.27 | async-start | bytes 147456
  697.9 238.3 %reduce-scatter.30.cloned.1.call-start = ((), (), s32[]{:S(2)}) async-start(), calls=%async_computation.23 | async-start | bytes 2359296 | tf_op jit(solution)/shard_map/reduce_scatter | solution.py:365
  702.5 278.4 %reduce-scatter.26.cloned.1.call-start = ((), (), s32[]{:S(2)}) async-start(), calls=%async_computation.21 | async-start | bytes 2359296 | tf_op jit(solution)/shard_map/reduce_scatter | solution.py:359
  720.9 304.5 %reduce-scatter.24.cloned.1.call-start = ((), (), s32[]{:S(2)}) async-start(), calls=%async_computation.20 | async-start | bytes 2359296 | tf_op jit(solution)/shard_map/reduce_scatter | solution.py:356
  727.8 422.0 %all-reduce.12.cloned.1.call-start = ((), (), s32[]{:S(2)}) async-start(), calls=%async_computation.28 | async-start | bytes 6291456 | tf_op jit(solution)/shard_map/psum | solution.py:47
  820.8 372.7 %reduce-scatter.28.cloned.1.call-start = ((), (), s32[]{:S(2)}) async-start(), calls=%async_computation.22 | async-start | bytes 2359296 | tf_op jit(solution)/shard_map/reduce_scatter | solution.py:362
  982.8 169.9 %copy-start.101 = (bf16[2048]{0:T(1024)(128)(2,1)S(1)}, bf16[2048]{0:T(1024)(128)(2,1)}, u32[]{:S(2)}) copy-start(bf16[2048]{0:T(1024)(128)(2,1)} %get-tuple-element.65) | copy-start | bytes 12292
  (112 other events, 601.0 us)
Sparse Core Ops, SparseCore 0:
  43.3 21.6 all-gather.4
  67.6 23.4 all-gather.6
  103.5 121.0 all-reduce.7
  230.7 71.1 all-gather.8
  303.6 72.1 all-gather.10
  428.9 92.3 reduce-scatter.19
  524.9 32.6 reduce-scatter.21
  560.0 69.5 all-reduce.9
  650.1 35.0 reduce-scatter.33
  688.8 36.0 reduce-scatter.35
  728.4 92.3 reduce-scatter.17
  823.7 31.4 reduce-scatter.31
  858.4 33.3 reduce-scatter.37
  894.9 41.2 reduce-scatter.29
  939.7 41.2 reduce-scatter.25
  984.1 41.2 reduce-scatter.23
  1028.3 121.4 all-reduce.11
  1153.3 40.2 reduce-scatter.27

commit v2 on v1

--- a/solution.py
+++ b/solution.py
@@ -1,12 +1,475 @@
 import jax
 import jax.numpy as jnp
 from jax import lax
+from jax.experimental import pallas as pl
+from jax.experimental.pallas import tpu as pltpu
 from jax.sharding import PartitionSpec as P
 
 HD = 128
 PROMPT_DEV = 128
 CLEN = 256
 CONT_DEV = 1
+
+
+MESH = pl.DeviceIdType.MESH
+STEP = 16
+LANE = 128
+
+
+def remote(source, target, sent, received, **where):
+    return pltpu.make_async_remote_copy(
+        src_ref=source,
+        dst_ref=target,
+        send_sem=sent,
+        recv_sem=received,
+        device_id=where,
+        device_id_type=MESH,
+    )
+
+
+def greet(places):
+    barrier = pltpu.get_barrier_semaphore()
+    for condition, where in places:
+        def signal(where=where):
+            pl.semaphore_signal(barrier, inc=1, device_id=where, device_id_type=MESH)
+        if condition is None:
+            signal()
+        else:
+            pl.when(condition)(signal)
+    count = 0
+    for condition, _ in places:
+        count = count + (1 if condition is None else jnp.where(condition, 1, 0))
+    pl.semaphore_wait(barrier, count)
+
+
+class Line:
+    def __init__(self, own, arrived, total, sems):
+        self.own, self.arrived, self.total = own, arrived, total
+        self.up_sent, self.up_got, self.down_sent, self.down_got = (sems.at[i] for i in range(4))
+        self.size = lax.axis_size("tensor")
+        self.here = lax.axis_index("tensor")
+        self.half = own.shape[0] // 2
+        self.pieces = self.half // STEP
+
+    @staticmethod
+    def semaphores(rows):
+        return pltpu.SemaphoreType.DMA((4, 2, rows // 2 // STEP))
+
+    def neighbours(self):
+        here, size = self.here, self.size
+        return [
+            (here > 0, {"tensor": jnp.maximum(here - 1, 0)}),
+            (here < size - 1, {"tensor": jnp.minimum(here + 1, size - 1)}),
+        ]
+
+    def lane(self, lane):
+        here, size = self.here, self.size
+        if lane == 0:
+            return here, here + 1, here - 1
+        return size - 1 - here, here - 1, here + 1
+
+    def rows(self, lane, piece):
+        return pl.ds(pl.multiple_of(lane * self.half + piece * STEP, STEP), STEP)
+
+    def up_copy(self, lane, piece):
+        rows = self.rows(lane, piece)
+        onward = self.lane(lane)[1]
+        return remote(
+            self.own.at[rows], self.arrived.at[rows],
+            self.up_sent.at[lane, piece], self.up_got.at[lane, piece], tensor=onward,
+        )
+
+    def down_copy(self, lane, piece):
+        rows = self.rows(lane, piece)
+        back = self.lane(lane)[2]
+        return remote(
+            self.total.at[rows], self.total.at[rows],
+            self.down_sent.at[lane, piece], self.down_got.at[lane, piece], tensor=back,
+        )
+
+    def rise(self, lane, piece):
+        place = self.lane(lane)[0]
+        rows = self.rows(lane, piece)
+
+        @pl.when(place > 0)
+        def _():
+            self.up_copy(lane, piece).wait_recv()
+            summed = (
+                self.own[rows].astype(jnp.float32) + self.arrived[rows].astype(jnp.float32)
+            ).astype(jnp.bfloat16)
+
+            @pl.when(place < self.size - 1)
+            def _():
+                self.own[rows] = summed
+
+            @pl.when(place == self.size - 1)
+            def _():
+                self.total[rows] = summed
+                self.down_copy(lane, piece).start()
+
+        @pl.when(place < self.size - 1)
+        def _():
+            self.up_copy(lane, piece).start()
+
+    def fall(self, lane, piece):
+        place = self.lane(lane)[0]
+
+        @pl.when(place < self.size - 1)
+        def _():
+            self.down_copy(lane, piece).wait_recv()
+
+            @pl.when(place > 0)
+            def _():
+                self.down_copy(lane, piece).start()
+
+    def lag(self, lane, per_hop):
+        return per_hop * (self.size - 1 - self.lane(lane)[0])
+
+    def advance(self, step, per_hop):
+        @pl.when(step < self.pieces)
+        def _():
+            for lane in range(2):
+                self.rise(lane, step)
+
+        for lane in range(2):
+            piece = step - self.lag(lane, per_hop)
+
+            @pl.when((piece >= 0) & (piece < self.pieces))
+            def _():
+                self.fall(lane, piece)
+
+    def steps(self, per_hop):
+        return self.pieces + per_hop * (self.size - 1)
+
+    def finish(self):
+        def one(piece, carry):
+            for lane in range(2):
+                place = self.lane(lane)[0]
+
+                @pl.when(place < self.size - 1)
+                def _():
+                    self.up_copy(lane, piece).wait_send()
+
+                @pl.when(place > 0)
+                def _():
+                    self.down_copy(lane, piece).wait_send()
+            return carry
+
+        lax.fori_loop(0, self.pieces, one, 0)
+
+
+class Plane:
+    def __init__(self, own, spare, paired, from_x, from_y, pair_sems, x_sems, y_sems):
+        self.own, self.spare, self.paired, self.from_x, self.from_y = own, spare, paired, from_x, from_y
+        self.pair_sems, self.x_sems, self.y_sems = pair_sems, x_sems, y_sems
+        here = lax.axis_index("expert")
+        self.here = here
+        self.core, self.x, self.y = here % 2, here // 2 % 2, here // 4
+        self.sibling = here + 1 - 2 * self.core
+        self.x_chip = here + 2 - 4 * self.x
+        self.y_chip = here + 4 - 8 * self.y
+        self.half = own.shape[1] // 2
+        self.pieces = self.half // STEP
+
+    @staticmethod
+    def semaphores(rows):
+        pieces = rows // 2 // STEP
+        return [
+            pltpu.SemaphoreType.DMA((2, 4)),
+            pltpu.SemaphoreType.DMA((2, 3, pieces)),
+            pltpu.SemaphoreType.DMA((2, 3, pieces)),
+        ]
+
+    def neighbours(self):
+        return [(None, {"expert": i}) for i in (self.sibling, self.x_chip, self.y_chip)]
+
+    def block(self, chip, core):
+        x = self.x + (1 - chip // 2) * (1 - 2 * self.x)
+        y = self.y + (1 - chip % 2) * (1 - 2 * self.y)
+        return 4 * y + 2 * x + core
+
+    def pair_copy(self, chip):
+        return remote(
+            self.spare.at[chip], self.paired.at[chip],
+            self.pair_sems.at[0, chip], self.pair_sems.at[1, chip], expert=self.sibling,
+        )
+
+    def rows(self, side, piece):
+        return pl.ds(pl.multiple_of(side * self.half + piece * STEP, STEP), STEP)
+
+    def landing(self, piece):
+        return pl.ds(pl.multiple_of(piece * STEP, STEP), STEP)
+
+    def x_copy(self, kind, piece):
+        chip, side = ((0, 0), (1, 0), (1, 1))[kind]
+        return remote(
+            self.own.at[chip, self.rows(side, piece)], self.from_x.at[kind, self.landing(piece)],
+            self.x_sems.at[0, kind, piece], self.x_sems.at[1, kind, piece], expert=self.x_chip,
+        )
+
+    def y_copy(self, kind, piece):
+        chip, side = ((0, 1), (2, 1), (2, 0))[kind]
+        return remote(
+            self.own.at[chip, self.rows(side, piece)], self.from_y.at[kind, self.landing(piece)],
+            self.y_sems.at[0, kind, piece], self.y_sems.at[1, kind, piece], expert=self.y_chip,
+        )
+
+    def add_pair(self, chip, side, piece):
+        rows = self.rows(side, piece)
+        self.own[chip, rows] = (
+            self.own[chip, rows].astype(jnp.float32) + self.paired[chip, rows].astype(jnp.float32)
+        ).astype(jnp.bfloat16)
+
+    def each(self, step):
+        def one(piece, carry):
+            step(piece)
+            return carry
+
+        lax.fori_loop(0, self.pieces, one, 0)
+
+    def send_first(self, chip):
+        def step(piece):
+            if chip in (0, 1):
+                self.add_pair(chip, 0, piece)
+                self.x_copy(chip, piece).start()
+            if chip in (0, 2):
+                self.add_pair(chip, 1, piece)
+                self.y_copy(chip // 2, piece).start()
+
+        self.each(step)
+
+    def send_second(self):
+        def step(piece):
+            landed = self.landing(piece)
+            self.y_copy(0, piece).wait_recv()
+            rows = self.rows(1, piece)
+            self.own[1, rows] = (
+                self.own[1, rows].astype(jnp.float32)
+                + self.paired[1, rows].astype(jnp.float32)
+                + self.from_y[0, landed].astype(jnp.float32)
+            ).astype(jnp.bfloat16)
+            self.x_copy(2, piece).start()
+            self.x_copy(0, piece).wait_recv()
+            rows = self.rows(0, piece)
+            self.own[2, rows] = (
+                self.own[2, rows].astype(jnp.float32)
+                + self.paired[2, rows].astype(jnp.float32)
+                + self.from_x[0, landed].astype(jnp.float32)
+            ).astype(jnp.bfloat16)
+            self.y_copy(2, piece).start()
+
+        self.each(step)
+
+    def last_sum(self, piece):
+        landed = self.landing(piece)
+        sums = []
+        for side in range(2):
+            first, second = (self.x_copy(1, piece), self.y_copy(2, piece)) if side == 0 else (self.y_copy(1, piece), self.x_copy(2, piece))
+            first.wait_recv()
+            second.wait_recv()
+            a, b = (self.from_x[1, landed], self.from_y[2, landed]) if side == 0 else (self.from_y[1, landed], self.from_x[2, landed])
+            rows = self.rows(side, piece)
+            sums.append(
+                self.own[3, rows].astype(jnp.float32)
+                + self.paired[3, rows].astype(jnp.float32)
+                + a.astype(jnp.float32)
+                + b.astype(jnp.float32)
+            )
+        return sums
+
+    def finish(self):
+        for chip in range(4):
+            self.pair_copy(chip).wait_send()
+
+        def step(piece):
+            for kind in range(3):
+                self.x_copy(kind, piece).wait_send()
+                self.y_copy(kind, piece).wait_send()
+
+        self.each(step)
+
+
+def wide_dot(left, right):
+    return jnp.dot(left, right, preferred_element_type=jnp.float32)
+
+
+def turned_dot(left, right):
+    return lax.dot_general(left, right, (((1,), (1,)), ((), ())), preferred_element_type=jnp.float32)
+
+
+def expert_kernel(
+    x_all, g_all, mask, router, bias, w_gate, w_up, w_down,
+    reduced, gated_all, gate_all, up_all, mixed_all,
+    x_buf, g_buf, part, paired, from_x, from_y, line_in, small, mixed,
+    in_sems, out_sems, pair_sems, x_sems, y_sems, line_sems,
+):
+    experts, width, hidden = w_gate.shape
+    rows = x_buf.shape[1]
+    tile = min(512, width)
+    plane = Plane(part.at[1], part.at[0], paired, from_x, from_y, pair_sems, x_sems, y_sems)
+    line = Line(part.at[1, 3], line_in, reduced, line_sems)
+    first_expert = lax.axis_index("expert") * experts
+    outs = (gated_all, gate_all, up_all)
+
+    def block_of(i):
+        return plane.block(i // 2, (plane.core + 1 - i % 2) % 2)
+
+    def fetch(i):
+        slot, block = i % 2, block_of(i)
+        return (
+            pltpu.make_async_copy(x_all.at[block], x_buf.at[slot], in_sems.at[0, slot]),
+            pltpu.make_async_copy(g_all.at[block], g_buf.at[slot], in_sems.at[1, slot]),
+        )
+
+    def store(i):
+        slot, block = i % 2, block_of(i)
+        return [
+            pltpu.make_async_copy(small.at[slot, n], outs[n].at[block], out_sems.at[n, slot])
+            for n in range(3)
+        ] + [pltpu.make_async_copy(mixed.at[slot], mixed_all.at[block], out_sems.at[3, slot])]
+
+    def compute(i):
+        slot = i % 2
+        block = block_of(i)
+        x = x_buf.at[slot]
+        g = g_buf.at[slot]
+        logits = wide_dot(x[...], router[...]) + bias[...]
+        weights = jnp.exp(logits - jnp.max(logits, axis=1, keepdims=True))
+        gates = weights / jnp.sum(weights, axis=1, keepdims=True) * mask[block]
+        column = lax.broadcasted_iota(jnp.int32, (rows, LANE), 1)
+        extra = jnp.zeros((rows, LANE), jnp.float32)
+        for j in range(experts):
+            gate_pre = wide_dot(x[...], w_gate[j])
+            up_pre = wide_dot(x[...], w_up[j])
+            raw = turned_dot(g[...], w_down[j])
+            gate = gates[:, j : j + 1]
+            sigma = jax.nn.sigmoid(gate_pre)
+            activated = gate_pre * sigma
+            inner = activated * up_pre
+            act = gate * raw
+            span = slice(j * hidden, (j + 1) * hidden)
+            small[slot, 0, :, span] = (gate * inner).astype(jnp.bfloat16)
+            small[slot, 1, :, span] = (
+                act * up_pre * sigma * (1.0 + gate_pre * (1.0 - sigma))
+            ).astype(jnp.bfloat16)
+            small[slot, 2, :, span] = (act * activated).astype(jnp.bfloat16)
+            gain = jnp.sum(raw * inner, axis=1, keepdims=True)
+            extra = jnp.where(column == first_expert + j, gain, extra)
+        for start in range(0, width, tile):
+            columns = slice(start, start + tile)
+            slot_grad = None
+            mix = None
+            for j in range(experts):
+                span = slice(j * hidden, (j + 1) * hidden)
+                term = turned_dot(small[slot, 1, :, span], w_gate[j, columns]) + turned_dot(
+                    small[slot, 2, :, span], w_up[j, columns]
+                )
+                more = wide_dot(small[slot, 0, :, span], w_down[j, :, columns])
+                slot_grad = term if slot_grad is None else slot_grad + term
+                mix = more if mix is None else mix + more
+            part[i % 2, i // 2, :, columns] = slot_grad.astype(jnp.bfloat16)
+            mixed[slot, :, columns] = mix.astype(jnp.bfloat16)
+        part[i % 2, i // 2, :, width:] = extra.astype(jnp.bfloat16)
+
+    for copy in fetch(0):
+        copy.start()
+    greet(plane.neighbours() + line.neighbours())
+
+    def step(i, carry):
+        @pl.when(i < 7)
+        def _():
+            for copy in fetch(i + 1):
+                copy.start()
+
+        for copy in fetch(i):
+            copy.wait()
+
+        @pl.when(i >= 2)
+        def _():
+            for copy in store(i - 2):
+                copy.wait()
+
+        compute(i)
+        for copy in store(i):
+            copy.start()
+
+        @pl.when(i % 2 == 0)
+        def _():
+            plane.pair_copy(i // 2).start()
+
+        @pl.when(i % 2 == 1)
+        def _():
+            plane.pair_copy(i // 2).wait_recv()
+
+        for chip in range(3):
+
+            @pl.when(i == 2 * chip + 1)
+            def _():
+                plane.send_first(chip)
+                if chip == 2:
+                    plane.send_second()
+
+        return carry
+
+    lax.fori_loop(0, 8, step, 0)
+
+    def last(step, carry):
+        @pl.when(step < plane.pieces)
+        def _():
+            for side, total in enumerate(plane.last_sum(step)):
+                plane.own[3, plane.rows(side, step)] = total.astype(jnp.bfloat16)
+
+        line.advance(step, 2)
+        return carry
+
+    lax.fori_loop(0, line.steps(2), last, 0)
+    for i in (6, 7):
+        for copy in store(i):
+            copy.wait()
+    plane.finish()
+    line.finish()
+
+
+def experts_fused(arrived, arrived_grad, mask, router, bias, w_gate, w_up, w_down):
+    ranks, rows, width = arrived.shape
+    experts, _, hidden = w_gate.shape
+    wide = width + LANE
+    inner = experts * hidden
+    half = rows // 2
+    low = jnp.bfloat16
+    any_space = pl.BlockSpec(memory_space=pl.ANY)
+    vmem = pl.BlockSpec(memory_space=pltpu.VMEM)
+    small_shape = jax.ShapeDtypeStruct((ranks, rows, inner), low)
+    return pl.pallas_call(
+        expert_kernel,
+        out_shape=(
+            jax.ShapeDtypeStruct((rows, wide), low), small_shape, small_shape, small_shape,
+            jax.ShapeDtypeStruct((ranks, rows, width), low),
+        ),
+        in_specs=[any_space, any_space] + [vmem] * 6,
+        out_specs=(vmem, any_space, any_space, any_space, any_space),
+        scratch_shapes=[
+            pltpu.VMEM((2, rows, width), low),
+            pltpu.VMEM((2, rows, width), low),
+            pltpu.VMEM((2, 4, rows, wide), low),
+            pltpu.VMEM((4, rows, wide), low),
+            pltpu.VMEM((3, half, wide), low),
+            pltpu.VMEM((3, half, wide), low),
+            pltpu.VMEM((rows, wide), low),
+            pltpu.VMEM((2, 3, rows, inner), low),
+            pltpu.VMEM((2, rows, width), low),
+            pltpu.SemaphoreType.DMA((2, 2)),
+            pltpu.SemaphoreType.DMA((4, 2)),
+            *Plane.semaphores(rows),
+            Line.semaphores(rows),
+        ],
+        compiler_params=pltpu.CompilerParams(
+            collective_id=0, has_side_effects=True, vmem_limit_bytes=61 * 2**20
+        ),
+        cost_estimate=pl.CostEstimate(
+            flops=12 * ranks * rows * width * inner, bytes_accessed=8 * ranks * rows * width, transcendentals=0
+        ),
+    )(arrived, arrived_grad, mask, router, bias, w_gate, w_up, w_down)
 
 
 epsilon = 1e-05
@@ -195,37 +658,73 @@
         jnp.float32
     )
     rows_mask = jnp.sum(hits, axis=1)
-    routed = lax.all_gather(
-        (rows_mask * chances).astype(jnp.float32), "expert", axis=0, tiled=True
-    )
-    gates = lax.dynamic_slice_in_dim(routed, device * local_experts, local_experts, 1).T
     grad_out = cotangent.astype(jnp.float32)
-    pieces = max(1, ranks * rows // 4096)
-    piece = rows // pieces
-    split_gates = gates.reshape(local_experts, ranks, rows)
-    results = []
-    weight_grads = None
-    for number in range(pieces):
-        part = slice(number * piece, (number + 1) * piece)
-        sources = (normed_two[part], cotangent[part])
-        if results:
-            sources, results, weight_grads = lax.optimization_barrier(
-                (sources, results, weight_grads)
+    if ranks == 8:
+        routes_all = lax.all_gather(routes, "expert", axis=0)
+        own_expert = device * local_experts + jnp.arange(local_experts, dtype=jnp.int32)
+        own_mask = jnp.any(routes_all[:, :, :, None] == own_expert, axis=2).astype(jnp.float32)
+        own_mask = jnp.pad(own_mask, ((0, 0), (0, 0), (0, LANE - local_experts)))
+        own_first = jnp.roll(router, -device * local_experts, axis=1)
+        own_first = jnp.pad(own_first, ((0, 0), (0, LANE - experts_total)))
+        bias = jnp.where(jnp.arange(LANE) < experts_total, 0.0, masked_value)
+        bias = bias.astype(jnp.float32)[None]
+        arrived = lax.all_gather(normed_two, "expert", axis=0)
+        arrived_grad = lax.all_gather(cotangent, "expert", axis=0)
+        reduced, gated, gate_grad, up_grad, mixed_part = experts_fused(
+            arrived, arrived_grad, own_mask, own_first, bias, w_gate, w_up, w_down
+        )
+        moe_input_grad = reduced[:, :width].astype(jnp.float32)
+        chance_grad = reduced[:, width : width + experts_total].astype(jnp.float32)
+        mixture = lax.psum(
+            lax.psum_scatter(
+                mixed_part.reshape(ranks * rows, width), "expert", scatter_dimension=0, tiled=True
+            ),
+            "tensor",
+        ).astype(jnp.float32)
+        hidden_units = w_gate.shape[2]
+
+        def per_expert(j):
+            span = slice(j * hidden_units, (j + 1) * hidden_units)
+            return (
+                jnp.einsum("nrd,nrf->df", arrived, gate_grad[:, :, span], preferred_element_type=jnp.float32),
+                jnp.einsum("nrd,nrf->df", arrived, up_grad[:, :, span], preferred_element_type=jnp.float32),
+                jnp.einsum("nrf,nrd->fd", gated[:, :, span], arrived_grad, preferred_element_type=jnp.float32),
             )
-        *result, grads = experts(
-            *sources,
-            split_gates[:, :, part].reshape(local_experts, ranks * piece),
-            w_gate,
-            w_up,
-            w_down,
-            experts_total,
-        )
-        results.append(result)
-        weight_grads = grads if weight_grads is None else [a + b for a, b in zip(weight_grads, grads)]
-    mixture, moe_input_grad, chance_grad = (
-        jnp.concatenate(list(group_of), axis=0) for group_of in zip(*results)
-    )
-    grad_w_gate, grad_w_up, grad_w_down = weight_grads
+
+        grad_w_gate, grad_w_up, grad_w_down = (
+            jnp.stack(list(parts)) for parts in zip(*(per_expert(j) for j in range(local_experts)))
+        )
+    else:
+        routed = lax.all_gather(
+            (rows_mask * chances).astype(jnp.float32), "expert", axis=0, tiled=True
+        )
+        gates = lax.dynamic_slice_in_dim(routed, device * local_experts, local_experts, 1).T
+        pieces = max(1, ranks * rows // 4096)
+        piece = rows // pieces
+        split_gates = gates.reshape(local_experts, ranks, rows)
+        results = []
+        weight_grads = None
+        for number in range(pieces):
+            part = slice(number * piece, (number + 1) * piece)
+            sources = (normed_two[part], cotangent[part])
+            if results:
+                sources, results, weight_grads = lax.optimization_barrier(
+                    (sources, results, weight_grads)
+                )
+            *result, grads = experts(
+                *sources,
+                split_gates[:, :, part].reshape(local_experts, ranks * piece),
+                w_gate,
+                w_up,
+                w_down,
+                experts_total,
+            )
+            results.append(result)
+            weight_grads = grads if weight_grads is None else [a + b for a, b in zip(weight_grads, grads)]
+        mixture, moe_input_grad, chance_grad = (
+            jnp.concatenate(list(group_of), axis=0) for group_of in zip(*results)
+        )
+        grad_w_gate, grad_w_up, grad_w_down = weight_grads
     chance_grad = rows_mask * chance_grad
     output = (hidden + mixture).astype(jnp.bfloat16)
     logit_grad = (

time: 1210 us -> 1320 us (1.091)
  Pallas kernels: 0 us -> 338 us
  waiting for transfers between devices: 805 us -> 671 us
  matrix products: 193 us -> 113 us
  blocking collectives: 69.4 us -> 48.4 us
    pallas_call x0 -> x1, Pallas kernels: none -> 338 us  [experts_fused(): pl.pallas_call(expert_kernel, out_shape=(jax.ShapeDtypeStruct((rows, wide...]
    reduce_scatter x3 -> x1, waiting for transfers between devices: 205 us -> 41.9 us  [body(): lax.psum_scatter(mixed_part.reshape(ranks * rows, width), 'expert', scatt...]
    dot_general x9 -> x6, matrix products: 123 us -> 50.9 us  [the longest x2 21 us: per_expert(): jnp.einsum('nrf,nrd->fd', gated[:, :, span], arrived_grad, preferred_elem...]
    psum x2 -> x1, waiting for transfers between devices: 173 us -> 123 us  [body(): lax.psum(lax.psum_scatter(mixed_part.reshape(ranks * rows, width), 'exper...]
    unnamed x21 -> x18, waiting for transfers between devices: 20.9 us -> 51.3 us
    reduce_scatter x1, waiting for transfers between devices: 18.3 us -> 42.9 us  [body(): lax.psum_scatter(grad_w_value.astype(jnp.bfloat16), 'expert', scatter_dim...]
    psum x1 -> x0, blocking collectives: 20.5 us -> none  [experts(): lax.psum(lax.psum_scatter(placed, 'expert', scatter_dimension=0, tiled=Tr...]
    reduce_scatter x1, waiting for transfers between devices: 0.01 us -> 14.4 us  [body(): lax.psum_scatter(grad_router.astype(jnp.bfloat16), 'expert', scatter_dime...]
  transfers between devices with their start and end apart: 18 -> 15, of which waited for: 16 -> 14; matrix products, arithmetic and copies ran while one was open for 16% -> 12% of each run, Pallas kernels for 0% -> 0%
where the time goes in v2:
time: 1320 us; the launch traced here: 1310 us
  waiting for transfers between devices  671 us (51%)
  Pallas kernels  338 us (26%)
  matrix products  113 us (9%)
  other arithmetic  72.3 us (5%)
  local copies, waits for them, and re-layouts  52.1 us (4%)
  blocking collectives  48.4 us (4%)
  between operations  17.3 us (1%)
    pallas_call x1, Pallas kernels, experts_fused(): pl.pallas_call(expert_kernel, out_shape=(jax.ShapeDtypeStruct((rows, wide...  338 us
    psum x1, waiting for transfers between devices, body(): lax.psum(lax.psum_scatter(mixed_part.reshape(ranks * rows, width), 'exper...  123 us
    psum x1, waiting for transfers between devices, body(): lax.psum(jnp.dot(attended, w_out, preferred_element_type=jnp.float32), 't...  121 us
    all_gather x1, waiting for transfers between devices, body(): arrived = lax.all_gather(normed_two, 'expert', axis=0)  74.5 us
    unnamed x18, waiting for transfers between devices  51.3 us
    all_gather x1, waiting for transfers between devices, body(): arrived_grad = lax.all_gather(cotangent, 'expert', axis=0)  47.2 us
    reduce_scatter x1, waiting for transfers between devices, body(): lax.psum_scatter(grad_w_out.astype(jnp.bfloat16), 'expert', scatter_dimen...  43.2 us
    reduce_scatter x1, waiting for transfers between devices, body(): lax.psum_scatter(grad_w_query.astype(jnp.bfloat16), 'expert', scatter_dim...  43 us
  transfers between devices with their start and end apart: 15, of which 14 were waited for; matrix products, arithmetic and copies ran while one was open for 12% of the time, Pallas kernels for 0%

profile of v2, /device:TPU:0, one launch (start us, length us, event | category | flops | bytes accessed | tf_op | source)
XLA Modules:
  0.0 1314.7 jit_solution(9136144958575650146)
XLA Ops:
  15.3 13.5 %psum.35 = f32[384,2]{0,1:T(2,128)S(1)} all-reduce(f32[384,2]{0,1:T(2,128)S(1)} %pad_maximum_fusion.17), channel_id=1, replica_groups=mesh['expert'=8,'tensor'=4] {'tensor'}, use_global_device_ids=true, to_apply=%region_3.4 | all-reduce | flops 768 | bytes 6144 | tf_op jit(solution)/shard_map/psum | solution.py:593
  54.1 10.5 all-gather.8.cloned.1.call-done
  73.8 16.8 %all-gather.10.cloned.1.call-done = bf16[1024,512]{1,0:T(8,128)(2,1)} async-done(((bf16[128,512]{1,0:T(8,128)(2,1)}), bf16[1024,512]{1,0:T(8,128)(2,1)}) %all-gather.10.cloned.1.call-update) | async-done | bytes 1048592 | tf_op jit(solution)/shard_map/all_gather | solution.py:614
  103.8 120.6 %all-reduce.9.cloned.1.call-done = f32[384,2048]{1,0:T(8,128)} async-done(((f32[384,2048]{1,0:T(8,128)}), f32[384,2048]{1,0:T(8,128)}) %all-reduce.9.cloned.1.call-update) | async-done | bytes 3145744 | tf_op jit(solution)/shard_map/psum | solution.py:649
  230.5 9.4 all-gather.2
  250.1 47.2 %all-gather.14.cloned.1.call-done = bf16[3072,2048]{1,0:T(8,128)(2,1)} async-done(((bf16[384,2048]{1,0:T(8,128)(2,1)}), bf16[3072,2048]{1,0:T(8,128)(2,1)}) %all-gather.14.cloned.1.call-update) | async-done | bytes 12582928 | tf_op jit(solution)/shard_map/all_gather | solution.py:672
  297.3 74.5 %all-gather.12.cloned.1.call-done = bf16[3072,2048]{1,0:T(8,128)(2,1)} async-done(((bf16[384,2048]{1,0:T(8,128)(2,1)}), bf16[3072,2048]{1,0:T(8,128)(2,1)}) %all-gather.12.cloned.1.call-update) | async-done | bytes 12582928 | tf_op jit(solution)/shard_map/all_gather | solution.py:671
  371.8 338.4 %shard_map.246 = (bf16[384,2176]{1,0:T(8,128)(2,1)}, bf16[8,384,512]{2,1,0:T(8,128)(2,1)}, bf16[8,384,512]{2,1,0:T(8,128)(2,1)}, bf16[8,384,512]{2,1,0:T(8,128)(2,1)}, bf16[8,384,2048]{2,1,0:T(8,128)(2,1)}) custom-call(bf16[8,384,2048]{2,1,0:T(8,128)(2,1)} %bitcast.131, bf16[8,384,2048]{2,1,0:T(8,128)(2,1)} %bitcast.100, ...), custom_call_target="tpu_custom_call" | custom-call | flops 38654705664 | bytes 50331648 | tf_op jit(solution)/shard_map/pallas_call | solution.py:443
  757.7 14.7 %reduce-scatter.28.cloned.1.call-done = bf16[128,512]{1,0:T(8,128)(2,1)} async-done(((bf16[1024,512]{1,0:T(8,128)(2,1)}), bf16[128,512]{1,0:T(8,128)(2,1)}) %reduce-scatter.28.cloned.1.call-update) | async-done | bytes 131088
  789.8 11.7 psum.38
  815.0 10.0 convolution_bitcast_fusion
  824.9 10.9 convolution_bitcast_fusion.4
  841.4 11.0 convolution_bitcast_fusion.1
  852.5 8.1 convolution_bitcast_fusion.5
  866.2 41.9 %reduce-scatter.16.cloned.1.call-done = bf16[384,2048]{1,0:T(8,128)(2,1)} async-done(((bf16[3072,2048]{1,0:T(8,128)(2,1)}), bf16[384,2048]{1,0:T(8,128)(2,1)}) %reduce-scatter.16.cloned.1.call-update) | async-done | bytes 1572880 | tf_op jit(solution)/shard_map/reduce_scatter | solution.py:679
  913.0 7.0 convolution_bitcast_fusion.2
  928.2 14.4 %reduce-scatter.26.cloned.1.call-done = bf16[256,16]{0,1:T(8,128)(2,1)} async-done(((bf16[2048,16]{0,1:T(8,128)(2,1)}), bf16[256,16]{0,1:T(8,128)(2,1)}) %reduce-scatter.26.cloned.1.call-update) | async-done | bytes 8208 | tf_op jit(solution)/shard_map/reduce_scatter | solution.py:876
  943.8 35.2 %reduce-scatter.32.cloned.1.call-done = bf16[64,2]{1,0:T(8,128)(2,1)} async-done(((bf16[512,2]{1,0:T(8,128)(2,1)}), bf16[64,2]{1,0:T(8,128)(2,1)}) %reduce-scatter.32.cloned.1.call-update) | async-done | bytes 272
  980.4 43.2 %reduce-scatter.24.cloned.1.call-done = bf16[512,256]{1,0:T(8,128)(2,1)} async-done(((bf16[512,2048]{1,0:T(8,128)(2,1)}), bf16[512,256]{1,0:T(8,128)(2,1)}) %reduce-scatter.24.cloned.1.call-update) | async-done | bytes 262160 | tf_op jit(solution)/shard_map/reduce_scatter | solution.py:864
  1025.4 43.0 %reduce-scatter.18.cloned.1.call-done = bf16[256,512]{1,0:T(8,128)(2,1)} async-done(((bf16[2048,512]{1,0:T(8,128)(2,1)}), bf16[256,512]{1,0:T(8,128)(2,1)}) %reduce-scatter.18.cloned.1.call-update) | async-done | bytes 262160 | tf_op jit(solution)/shard_map/reduce_scatter | solution.py:855
  1070.2 42.7 %reduce-scatter.20.cloned.1.call-done = bf16[256,512]{1,0:T(8,128)(2,1)} async-done(((bf16[2048,512]{1,0:T(8,128)(2,1)}), bf16[256,512]{1,0:T(8,128)(2,1)}) %reduce-scatter.20.cloned.1.call-update) | async-done | bytes 262160 | tf_op jit(solution)/shard_map/reduce_scatter | solution.py:858
  1114.7 42.9 %reduce-scatter.22.cloned.1.call-done = bf16[256,512]{1,0:T(8,128)(2,1)} async-done(((bf16[2048,512]{1,0:T(8,128)(2,1)}), bf16[256,512]{1,0:T(8,128)(2,1)}) %reduce-scatter.22.cloned.1.call-update) | async-done | bytes 262160 | tf_op jit(solution)/shard_map/reduce_scatter | solution.py:861
  1159.4 122.5 %all-reduce.11.cloned.1.call-done = (bf16[384,2048]{1,0:T(8,128)(2,1)}, bf16[384,2048]{1,0:T(8,128)(2,1)}) async-done(((bf16[384,2048]{1,0:T(8,128)(2,1)}, bf16[384,2048]{1,0:T(8,128)(2,1)}), (bf16[384,2048]{1,0:T(8,128)(2,1)}, bf16[384,2048]{1,0:T(8,128)(2,1)})) %all-reduce.11.cloned.1.call-update) | async-done | bytes 3145744 | tf_op jit(solution)/shard_map/psum | solution.py:678
  1287.1 13.9 %all-reduce.4 = (bf16[2048]{0:T(1024)(128)(2,1)S(1)}, bf16[2048]{0:T(1024)(128)(2,1)S(1)}) all-reduce(bf16[2048]{0:T(1024)(128)(2,1)S(1)} %get-tuple-element.25, bf16[2048]{0:T(1024)(128)(2,1)S(1)} %copy-done.119), channel_id=12, replica_groups=mesh['expert'=8,'tensor'=4] {'expert'}, use_global_device_ids=true, to_apply=%region_38.39.clone | all-reduce | flops 4096 | bytes 16384
  (440 shorter events, 193.4 us)
Async XLA Ops:
  7.2 57.4 %all-gather.8.cloned.1.call-start = ((), (), s32[]{:S(2)}) async-start(), calls=%async_computation.9 | async-start | bytes 1179648 | tf_op jit(solution)/shard_map/all_gather | solution.py:613
  9.8 33.0 %copy-start.104 = (f32[384]{0:T(512)}, f32[384]{0:T(512)S(1)}, u32[]{:S(2)}) copy-start(f32[384]{0:T(512)S(1)} %get-tuple-element.64) | copy-start | bytes 4612
  42.8 47.8 %all-gather.10.cloned.1.call-start = ((), (), s32[]{:S(2)}) async-start(), calls=%async_computation.10 | async-start | bytes 1179648 | tf_op jit(solution)/shard_map/all_gather | solution.py:614
  47.4 177.0 %all-reduce.9.cloned.1.call-start = ((), (), s32[]{:S(2)}) async-start(), calls=%async_computation.11 | async-start | bytes 6291456 | tf_op jit(solution)/shard_map/psum | solution.py:649
  70.2 27.0 %copy-start.110 = (f32[384]{0:T(512)}, f32[384]{0:T(512)S(1)}, u32[]{:S(2)}) copy-start(f32[384]{0:T(512)S(1)} %get-tuple-element.73) | copy-start | bytes 4612
  72.0 26.2 %copy-start.111 = (f32[384]{0:T(512)}, f32[384]{0:T(512)S(1)}, u32[]{:S(2)}) copy-start(f32[384]{0:T(512)S(1)} %get-tuple-element.75) | copy-start | bytes 4612
  103.2 194.2 %all-gather.14.cloned.1.call-start = ((), (), s32[]{:S(2)}) async-start(), calls=%async_computation.19 | async-start | bytes 14155776 | tf_op jit(solution)/shard_map/all_gather | solution.py:672
  103.8 125.2 %copy-start.87 = (f32[2048]{0:T(1024)S(1)}, f32[2048]{0:T(1024)}, u32[]{:S(2)}) copy-start(f32[2048]{0:T(1024)} %param.21) | copy-start | bytes 24580
  103.8 268.0 %all-gather.12.cloned.1.call-start = ((), (), s32[]{:S(2)}) async-start(), calls=%async_computation.18 | async-start | bytes 14155776 | tf_op jit(solution)/shard_map/all_gather | solution.py:671
  230.5 541.9 %reduce-scatter.28.cloned.1.call-start = ((), (), s32[]{:S(2)}) async-start(), calls=%async_computation.20 | async-start | bytes 1179648
  242.6 468.7 %copy-start.74 = (f32[384,16]{1,0:T(8,128)}, f32[384,16]{1,0:T(8,128)S(1)}, u32[]{:S(2)}) copy-start(f32[384,16]{1,0:T(8,128)S(1)} %copy.90) | copy-start | bytes 73732
  249.8 461.6 %copy-start.100 = (f32[384]{0:T(512)}, f32[384]{0:T(512)S(1)}, u32[]{:S(2)}) copy-start(f32[384]{0:T(512)S(1)} %get-tuple-element.79) | copy-start | bytes 4612
  249.9 461.5 %copy-start.63 = (f32[384,16]{1,0:T(8,128)}, f32[384,16]{1,0:T(8,128)S(1)}, u32[]{:S(2)}) copy-start(f32[384,16]{1,0:T(8,128)S(1)} %copy.88) | copy-start | bytes 73732
  250.1 461.2 %copy-start.106 = (f32[384]{0:T(512)}, f32[384]{0:T(512)S(1)}, u32[]{:S(2)}) copy-start(f32[384]{0:T(512)S(1)} %fusion.59) | copy-start | bytes 4612
  371.8 339.6 %copy-start.103 = (f32[384]{0:T(512)S(1)}, f32[384]{0:T(512)}, u32[]{:S(2)}) copy-start(f32[384]{0:T(512)} %copy-done.102) | copy-start | bytes 4612
  734.5 101.3 %reduce-scatter.30.cloned.1.call-start = ((), (), s32[]{:S(2)}) async-start(), calls=%async_computation.21 | async-start | bytes 1179648
  743.4 164.6 %reduce-scatter.16.cloned.1.call-start = ((), (), s32[]{:S(2)}) async-start(), calls=%async_computation.12 | async-start | bytes 14155776 | tf_op jit(solution)/shard_map/reduce_scatter | solution.py:679
  744.2 198.3 %reduce-scatter.26.cloned.1.call-start = ((), (), s32[]{:S(2)}) async-start(), calls=%async_computation.17 | async-start | bytes 73728 | tf_op jit(solution)/shard_map/reduce_scatter | solution.py:876
  757.7 221.4 %reduce-scatter.32.cloned.1.call-start = ((), (), s32[]{:S(2)}) async-start(), calls=%async_computation.22 | async-start | bytes 147456
  785.0 238.6 %reduce-scatter.24.cloned.1.call-start = ((), (), s32[]{:S(2)}) async-start(), calls=%async_computation.16 | async-start | bytes 2359296 | tf_op jit(solution)/shard_map/reduce_scatter | solution.py:864
  789.7 278.7 %reduce-scatter.18.cloned.1.call-start = ((), (), s32[]{:S(2)}) async-start(), calls=%async_computation.13 | async-start | bytes 2359296 | tf_op jit(solution)/shard_map/reduce_scatter | solution.py:855
  806.8 306.1 %reduce-scatter.20.cloned.1.call-start = ((), (), s32[]{:S(2)}) async-start(), calls=%async_computation.14 | async-start | bytes 2359296 | tf_op jit(solution)/shard_map/reduce_scatter | solution.py:858
  812.4 345.3 %reduce-scatter.22.cloned.1.call-start = ((), (), s32[]{:S(2)}) async-start(), calls=%async_computation.15 | async-start | bytes 2359296 | tf_op jit(solution)/shard_map/reduce_scatter | solution.py:861
  841.1 440.8 %all-reduce.11.cloned.1.call-start = ((), (), s32[]{:S(2)}) async-start(), calls=%async_computation.23 | async-start | bytes 6291456 | tf_op jit(solution)/shard_map/psum | solution.py:678
  (120 other events, 564.8 us)
Sparse Core Ops, SparseCore 0:
  42.9 21.6 all-gather.7
  67.1 23.4 all-gather.9
  103.3 121.0 all-reduce.8
  226.2 71.1 all-gather.13
  299.7 72.1 all-gather.11
  734.6 37.6 reduce-scatter.27
  776.1 35.9 reduce-scatter.29
  815.7 92.3 reduce-scatter.15
  911.1 31.3 reduce-scatter.25
  945.7 33.3 reduce-scatter.31
  982.3 41.2 reduce-scatter.23
  1027.1 41.2 reduce-scatter.17
  1071.6 41.1 reduce-scatter.19
  1116.4 41.2 reduce-scatter.21
  1160.5 121.4 all-reduce.10

commit v3 on v2

--- a/solution.py
+++ b/solution.py
@@ -122,24 +122,22 @@
             def _():
                 self.down_copy(lane, piece).start()
 
-    def lag(self, lane, per_hop):
-        return per_hop * (self.size - 1 - self.lane(lane)[0])
-
-    def advance(self, step, per_hop):
-        @pl.when(step < self.pieces)
-        def _():
+    def advance(self, step, skew=1):
+        for act, far in ((self.rise, False), (self.fall, True)):
             for lane in range(2):
-                self.rise(lane, step)
-
-        for lane in range(2):
-            piece = step - self.lag(lane, per_hop)
-
-            @pl.when((piece >= 0) & (piece < self.pieces))
-            def _():
-                self.fall(lane, piece)
-
-    def steps(self, per_hop):
-        return self.pieces + per_hop * (self.size - 1)
+                place = self.lane(lane)[0]
+                piece = step - skew * (2 * (self.size - 1) - place if far else place)
+
+                @pl.when((piece >= 0) & (piece < self.pieces))
+                def _():
+                    act(lane, piece)
+
+    def step_body(self, step, carry):
+        self.advance(step)
+        return carry
+
+    def steps(self, skew=1):
+        return self.pieces + skew * 2 * (self.size - 1)
 
     def finish(self):
         def one(piece, carry):
@@ -158,16 +156,29 @@
         lax.fori_loop(0, self.pieces, one, 0)
 
 
-class Plane:
-    def __init__(self, own, spare, paired, from_x, from_y, pair_sems, x_sems, y_sems):
-        self.own, self.spare, self.paired, self.from_x, self.from_y = own, spare, paired, from_x, from_y
-        self.pair_sems, self.x_sems, self.y_sems = pair_sems, x_sems, y_sems
+class Place:
+    def __init__(self):
         here = lax.axis_index("expert")
         self.here = here
         self.core, self.x, self.y = here % 2, here // 2 % 2, here // 4
         self.sibling = here + 1 - 2 * self.core
         self.x_chip = here + 2 - 4 * self.x
         self.y_chip = here + 4 - 8 * self.y
+
+    def neighbours(self):
+        return [(None, {"expert": i}) for i in (self.sibling, self.x_chip, self.y_chip)]
+
+    def block(self, chip, core):
+        x = self.x + (1 - chip // 2) * (1 - 2 * self.x)
+        y = self.y + (1 - chip % 2) * (1 - 2 * self.y)
+        return 4 * y + 2 * x + core
+
+
+class Plane(Place):
+    def __init__(self, own, spare, paired, from_x, from_y, pair_sems, x_sems, y_sems):
+        self.own, self.spare, self.paired, self.from_x, self.from_y = own, spare, paired, from_x, from_y
+        self.pair_sems, self.x_sems, self.y_sems = pair_sems, x_sems, y_sems
+        super().__init__()
         self.half = own.shape[1] // 2
         self.pieces = self.half // STEP
 
@@ -180,14 +191,6 @@
             pltpu.SemaphoreType.DMA((2, 3, pieces)),
         ]
 
-    def neighbours(self):
-        return [(None, {"expert": i}) for i in (self.sibling, self.x_chip, self.y_chip)]
-
-    def block(self, chip, core):
-        x = self.x + (1 - chip // 2) * (1 - 2 * self.x)
-        y = self.y + (1 - chip % 2) * (1 - 2 * self.y)
-        return 4 * y + 2 * x + core
-
     def pair_copy(self, chip):
         return remote(
             self.spare.at[chip], self.paired.at[chip],
@@ -238,27 +241,27 @@
 
         self.each(step)
 
+    def second_piece(self, piece):
+        landed = self.landing(piece)
+        self.y_copy(0, piece).wait_recv()
+        rows = self.rows(1, piece)
+        self.own[1, rows] = (
+            self.own[1, rows].astype(jnp.float32)
+            + self.paired[1, rows].astype(jnp.float32)
+            + self.from_y[0, landed].astype(jnp.float32)
+        ).astype(jnp.bfloat16)
+        self.x_copy(2, piece).start()
+        self.x_copy(0, piece).wait_recv()
+        rows = self.rows(0, piece)
+        self.own[2, rows] = (
+            self.own[2, rows].astype(jnp.float32)
+            + self.paired[2, rows].astype(jnp.float32)
+            + self.from_x[0, landed].astype(jnp.float32)
+        ).astype(jnp.bfloat16)
+        self.y_copy(2, piece).start()
+
     def send_second(self):
-        def step(piece):
-            landed = self.landing(piece)
-            self.y_copy(0, piece).wait_recv()
-            rows = self.rows(1, piece)
-            self.own[1, rows] = (
-                self.own[1, rows].astype(jnp.float32)
-                + self.paired[1, rows].astype(jnp.float32)
-                + self.from_y[0, landed].astype(jnp.float32)
-            ).astype(jnp.bfloat16)
-            self.x_copy(2, piece).start()
-            self.x_copy(0, piece).wait_recv()
-            rows = self.rows(0, piece)
-            self.own[2, rows] = (
-                self.own[2, rows].astype(jnp.float32)
-                + self.paired[2, rows].astype(jnp.float32)
-                + self.from_x[0, landed].astype(jnp.float32)
-            ).astype(jnp.bfloat16)
-            self.y_copy(2, piece).start()
-
-        self.each(step)
+        self.each(self.second_piece)
 
     def last_sum(self, piece):
         landed = self.landing(piece)
@@ -287,6 +290,97 @@
                 self.y_copy(kind, piece).wait_send()
 
         self.each(step)
+
+
+class Gather:
+    def __init__(self, source, target, place, x_sems, y_sems, far_sems, pair_sems, own_sem, pieces):
+        self.source, self.target = source, target
+        self.place = place
+        self.x_sems, self.y_sems, self.far_sems, self.pair_sems, self.own_sem = x_sems, y_sems, far_sems, pair_sems, own_sem
+        self.pieces = pieces
+        self.rows_each = source.shape[0] // pieces
+
+    @staticmethod
+    def semaphores(pieces):
+        return [
+            pltpu.SemaphoreType.DMA((2, pieces)),
+            pltpu.SemaphoreType.DMA((2, pieces)),
+            pltpu.SemaphoreType.DMA((2, pieces)),
+            pltpu.SemaphoreType.DMA((2, 4, pieces)),
+            pltpu.SemaphoreType.DMA,
+        ]
+
+    def rows(self, piece):
+        return pl.ds(piece * self.rows_each, self.rows_each)
+
+    def own_copy(self):
+        return pltpu.make_async_copy(self.source, self.target.at[self.place.here], self.own_sem)
+
+    def x_copy(self, piece):
+        rows = self.rows(piece)
+        return remote(
+            self.source.at[rows], self.target.at[self.place.here, rows],
+            self.x_sems.at[0, piece], self.x_sems.at[1, piece], expert=self.place.x_chip,
+        )
+
+    def y_copy(self, piece):
+        rows = self.rows(piece)
+        return remote(
+            self.source.at[rows], self.target.at[self.place.here, rows],
+            self.y_sems.at[0, piece], self.y_sems.at[1, piece], expert=self.place.y_chip,
+        )
+
+    def far_copy(self, piece):
+        rows = self.rows(piece)
+        came, goes = (
+            (self.place.x_chip, self.place.y_chip) if piece < self.pieces // 2 else (self.place.y_chip, self.place.x_chip)
+        )
+        return remote(
+            self.target.at[came, rows], self.target.at[came, rows],
+            self.far_sems.at[0, piece], self.far_sems.at[1, piece], expert=goes,
+        )
+
+    def pair_copy(self, kind, piece):
+        rows = self.rows(piece)
+        block = self.place.block(kind, self.place.core)
+        source = self.source.at[rows] if kind == 3 else self.target.at[block, rows]
+        return remote(
+            source, self.target.at[block, rows],
+            self.pair_sems.at[0, kind, piece], self.pair_sems.at[1, kind, piece], expert=self.place.sibling,
+        )
+
+    def start(self):
+        for piece in range(self.pieces):
+            self.x_copy(piece).start()
+            self.y_copy(piece).start()
+            self.pair_copy(3, piece).start()
+        self.own_copy().start()
+
+    def near(self, piece):
+        self.x_copy(piece).wait_recv()
+        if piece < self.pieces // 2:
+            self.far_copy(piece).start()
+        self.pair_copy(1, piece).start()
+        self.y_copy(piece).wait_recv()
+        if piece >= self.pieces // 2:
+            self.far_copy(piece).start()
+        self.pair_copy(2, piece).start()
+
+    def far(self, piece):
+        self.far_copy(piece).wait_recv()
+        self.pair_copy(0, piece).start()
+
+    def paired(self, kind, piece):
+        self.pair_copy(kind, piece).wait_recv()
+
+    def finish_sends(self):
+        self.own_copy().wait()
+        for piece in range(self.pieces):
+            self.x_copy(piece).wait_send()
+            self.y_copy(piece).wait_send()
+            self.far_copy(piece).wait_send()
+            for kind in range(4):
+                self.pair_copy(kind, piece).wait_send()
 
 
 def wide_dot(left, right):
@@ -419,10 +513,10 @@
             for side, total in enumerate(plane.last_sum(step)):
                 plane.own[3, plane.rows(side, step)] = total.astype(jnp.bfloat16)
 
-        line.advance(step, 2)
+        line.advance(step)
         return carry
 
-    lax.fori_loop(0, line.steps(2), last, 0)
+    lax.fori_loop(0, line.steps(), last, 0)
     for i in (6, 7):
         for copy in store(i):
             copy.wait()
@@ -470,6 +564,160 @@
             flops=12 * ranks * rows * width * inner, bytes_accessed=8 * ranks * rows * width, transcendentals=0
         ),
     )(arrived, arrived_grad, mask, router, bias, w_gate, w_up, w_down)
+
+
+def product_kernel(left, right, spread, total, gathered, own, arrived, sems, *gather_sems):
+    line = Line(own, arrived, total, sems)
+    place = Place()
+    gather = Gather(spread, gathered, place, *gather_sems, pieces=GATHER_PIECES)
+    greet(place.neighbours() + line.neighbours())
+    gather.start()
+    width = right.shape[1]
+    tile = min(512, width)
+    for start in range(0, width, tile):
+        columns = slice(start, start + tile)
+        own[:, columns] = wide_dot(left[...], right[:, columns]).astype(jnp.bfloat16)
+    steps = line.pieces + 2 * (line.size - 1)
+    done = 0
+    for piece in range(GATHER_PIECES):
+        upto = steps * (piece + 1) * 2 // (3 * GATHER_PIECES)
+        lax.fori_loop(done, upto, line.step_body, 0)
+        done = upto
+        gather.near(piece)
+    lax.fori_loop(done, steps, line.step_body, 0)
+    for piece in range(GATHER_PIECES):
+        gather.far(piece)
+    for kind in range(4):
+        for piece in range(GATHER_PIECES):
+            gather.paired(kind, piece)
+    gather.finish_sends()
+    line.finish()
+
+
+GATHER_PIECES = 4
+
+
+def summed_product(left, right, spread, collective_id):
+    rows, width = left.shape[0], right.shape[1]
+    vmem = pl.BlockSpec(memory_space=pltpu.VMEM)
+    any_space = pl.BlockSpec(memory_space=pl.ANY)
+    return pl.pallas_call(
+        product_kernel,
+        out_shape=(
+            jax.ShapeDtypeStruct((rows, width), jnp.bfloat16),
+            jax.ShapeDtypeStruct((lax.axis_size("expert"),) + spread.shape, spread.dtype),
+        ),
+        in_specs=[vmem, vmem, any_space],
+        out_specs=(vmem, any_space),
+        scratch_shapes=[
+            pltpu.VMEM((rows, width), jnp.bfloat16),
+            pltpu.VMEM((rows, width), jnp.bfloat16),
+            Line.semaphores(rows),
+            *Gather.semaphores(GATHER_PIECES),
+        ],
+        compiler_params=pltpu.CompilerParams(
+            collective_id=collective_id, has_side_effects=True, vmem_limit_bytes=40 * 2**20
+        ),
+    )(left, right, spread)
+
+
+def crossed_dot(left, right):
+    return lax.dot_general(left, right, (((0,), (0,)), ((), ())), preferred_element_type=jnp.float32)
+
+
+def closing_kernel(
+    normed, query_grad, key_grad, value_grad, attended, attention_grad, w_query, w_key, w_value, extras,
+    total, sums,
+    line_own, line_in, part, paired, from_x, from_y, line_sems, pair_sems, x_sems, y_sems,
+):
+    rows, width = normed.shape
+    heads = query_grad.shape[1]
+    share = part.shape[2]
+    tile = min(512, width)
+    line = Line(line_own, line_in, total, line_sems)
+    plane = Plane(part.at[1], part.at[0], paired, from_x, from_y, pair_sems, x_sems, y_sems)
+    greet(plane.neighbours() + line.neighbours())
+    for start in range(0, width, tile):
+        columns = slice(start, start + tile)
+        line_own[:, columns] = (
+            turned_dot(query_grad[...], w_query[columns])
+            + turned_dot(key_grad[...], w_key[columns])
+            + turned_dot(value_grad[...], w_value[columns])
+        ).astype(jnp.bfloat16)
+
+    def pair(chip, carry):
+        for sub in range(2):
+            block = plane.block(chip, (plane.core + 1 - sub) % 2)
+            columns = pl.ds(pl.multiple_of(block * share, share), share)
+            source = normed[:, columns]
+            part[sub, chip, :, 0:heads] = crossed_dot(source, query_grad[...]).astype(jnp.bfloat16)
+            part[sub, chip, :, heads : 2 * heads] = crossed_dot(source, key_grad[...]).astype(jnp.bfloat16)
+            part[sub, chip, :, 2 * heads : 3 * heads] = crossed_dot(source, value_grad[...]).astype(jnp.bfloat16)
+            part[sub, chip, :, 3 * heads : 4 * heads] = crossed_dot(
+                attention_grad[:, columns], attended[...]
+            ).astype(jnp.bfloat16)
+            part[sub, chip, :, 4 * heads :] = extras[block]
+            if sub == 0:
+                plane.pair_copy(chip).start()
+        line.advance(chip)
+        return carry
+
+    lax.fori_loop(0, 4, pair, 0)
+    for chip in range(4):
+        plane.pair_copy(chip).wait_recv()
+    for chip in range(3):
+        plane.send_first(chip)
+    late = plane.pieces + 2
+
+    def step(s, carry):
+        line.advance(s)
+
+        @pl.when(s - 4 < plane.pieces)
+        def _():
+            plane.second_piece(s - 4)
+
+        @pl.when((s >= 4 + late) & (s - 4 - late < plane.pieces))
+        def _():
+            piece = s - 4 - late
+            for side, summed in enumerate(plane.last_sum(piece)):
+                sums[plane.rows(side, piece)] = summed
+
+        return carry
+
+    lax.fori_loop(4, jnp.maximum(line.steps(), 4 + late + plane.pieces), step, 0)
+    plane.finish()
+    line.finish()
+
+
+def closing(normed, query_grad, key_grad, value_grad, attended, attention_grad, w_query, w_key, w_value, extras):
+    rows, width = normed.shape
+    heads = query_grad.shape[1]
+    ranks, share, more = extras.shape
+    wide = 4 * heads + more
+    low = jnp.bfloat16
+    vmem = pl.BlockSpec(memory_space=pltpu.VMEM)
+    return pl.pallas_call(
+        closing_kernel,
+        out_shape=(
+            jax.ShapeDtypeStruct((rows, width), low),
+            jax.ShapeDtypeStruct((share, wide), jnp.float32),
+        ),
+        in_specs=[vmem] * 10,
+        out_specs=(vmem, vmem),
+        scratch_shapes=[
+            pltpu.VMEM((rows, width), low),
+            pltpu.VMEM((rows, width), low),
+            pltpu.VMEM((2, 4, share, wide), low),
+            pltpu.VMEM((4, share, wide), low),
+            pltpu.VMEM((3, share // 2, wide), low),
+            pltpu.VMEM((3, share // 2, wide), low),
+            Line.semaphores(rows),
+            *Plane.semaphores(share),
+        ],
+        compiler_params=pltpu.CompilerParams(
+            collective_id=2, has_side_effects=True, vmem_limit_bytes=58 * 2**20
+        ),
+    )(normed, query_grad, key_grad, value_grad, attended, attention_grad, w_query, w_key, w_value, extras)
 
 
 epsilon = 1e-05
@@ -563,6 +811,7 @@
     ranks = lax.axis_size("expert")
     device = lax.axis_index("expert")
     span = ranks // 2
+    compact = ranks == 8
     prompt_len = PROMPT_DEV * span
     factor = HD ** (-0.5)
     local = jnp.arange(rows, dtype=jnp.int32)
@@ -609,10 +858,13 @@
         .astype(jnp.bfloat16)
     )
     value_low = value_raw.astype(jnp.bfloat16)
-    prompt_keys, prompt_values = (
-        lax.all_gather(key_rot[:PROMPT_DEV], "expert", axis=0, tiled=True),
-        lax.all_gather(value_low[:PROMPT_DEV], "expert", axis=0, tiled=True),
-    )
+    prompts = lax.all_gather(
+        jnp.concatenate([key_rot[:PROMPT_DEV], value_low[:PROMPT_DEV]], axis=1),
+        "expert",
+        axis=0,
+        tiled=True,
+    )
+    prompt_keys, prompt_values = prompts[:, :local_width], prompts[:, local_width:]
     prompt_count = prompt_keys.shape[0]
     all_keys = jnp.concatenate([prompt_keys, key_rot[PROMPT_DEV:]], axis=0)
     all_values = jnp.concatenate([prompt_values, value_low[PROMPT_DEV:]], axis=0)
@@ -646,7 +898,13 @@
         )
         log_totals.append(top + jnp.log(total))
     attended = jnp.concatenate(outputs, axis=1).astype(jnp.bfloat16)
-    attention = lax.psum(jnp.dot(attended, w_out, preferred_element_type=jnp.float32), "tensor")
+    if compact:
+        attention, arrived_grad = summed_product(attended, w_out, cotangent, 1)
+        attention = attention.astype(jnp.float32)
+    else:
+        attention = lax.psum(
+            jnp.dot(attended, w_out, preferred_element_type=jnp.float32), "tensor"
+        )
     hidden = source + attention
     scale_two = lax.rsqrt(jnp.mean(hidden * hidden, axis=1, keepdims=True) + epsilon)
     normed_two = (hidden * scale_two * ffn_gain).astype(jnp.bfloat16)
@@ -659,7 +917,7 @@
     )
     rows_mask = jnp.sum(hits, axis=1)
     grad_out = cotangent.astype(jnp.float32)
-    if ranks == 8:
+    if compact:
         routes_all = lax.all_gather(routes, "expert", axis=0)
         own_expert = device * local_experts + jnp.arange(local_experts, dtype=jnp.int32)
         own_mask = jnp.any(routes_all[:, :, :, None] == own_expert, axis=2).astype(jnp.float32)
@@ -669,7 +927,6 @@
         bias = jnp.where(jnp.arange(LANE) < experts_total, 0.0, masked_value)
         bias = bias.astype(jnp.float32)[None]
         arrived = lax.all_gather(normed_two, "expert", axis=0)
-        arrived_grad = lax.all_gather(cotangent, "expert", axis=0)
         reduced, gated, gate_grad, up_grad, mixed_part = experts_fused(
             arrived, arrived_grad, own_mask, own_first, bias, w_gate, w_up, w_down
         )
@@ -744,9 +1001,6 @@
         - hidden * (scale_two**3 / width) * jnp.sum(weighted_two * hidden, axis=1, keepdims=True)
     )
     attention_grad = hidden_grad.astype(jnp.bfloat16)
-    grad_w_out = jnp.einsum(
-        "td,te->de", attended, attention_grad, preferred_element_type=jnp.float32
-    )
     attended_grad = jnp.einsum(
         "te,de->td", attention_grad, w_out, preferred_element_type=jnp.float32
     ).astype(jnp.bfloat16)
@@ -782,20 +1036,15 @@
         )
     key_grad_all = jnp.concatenate(key_grads, axis=1)
     value_grad_all = jnp.concatenate(value_grads, axis=1)
-    prompt_key_grad, prompt_value_grad = (
-        lax.psum_scatter(
-            key_grad_all[:prompt_count].astype(jnp.bfloat16),
-            "expert",
-            scatter_dimension=0,
-            tiled=True,
-        ).astype(jnp.float32),
-        lax.psum_scatter(
-            value_grad_all[:prompt_count].astype(jnp.bfloat16),
-            "expert",
-            scatter_dimension=0,
-            tiled=True,
-        ).astype(jnp.float32),
-    )
+    prompt_grads = lax.psum_scatter(
+        jnp.concatenate(
+            [key_grad_all[:prompt_count], value_grad_all[:prompt_count]], axis=1
+        ).astype(jnp.bfloat16),
+        "expert",
+        scatter_dimension=0,
+        tiled=True,
+    ).astype(jnp.float32)
+    prompt_key_grad, prompt_value_grad = prompt_grads[:, :local_width], prompt_grads[:, local_width:]
     key_grad = jnp.concatenate([prompt_key_grad, key_grad_all[prompt_count:]], axis=0)
     value_grad = jnp.concatenate([prompt_value_grad, value_grad_all[prompt_count:]], axis=0)
     query_grad = unrotate(
@@ -827,23 +1076,55 @@
         scale_key * weighted_key - key_raw * (scale_key**3 / width) * inner_sums[:, 1:2]
     ).astype(jnp.bfloat16)
     value_raw_grad = value_grad.astype(jnp.bfloat16)
-    grad_w_query = jnp.einsum(
-        "td,te->de", normed, query_raw_grad, preferred_element_type=jnp.float32
-    )
-    grad_w_key = jnp.einsum("td,te->de", normed, key_raw_grad, preferred_element_type=jnp.float32)
-    grad_w_value = jnp.einsum(
-        "td,te->de", normed, value_raw_grad, preferred_element_type=jnp.float32
-    )
-    normed_part = jnp.einsum(
-        "te,de->td", query_raw_grad, w_query, preferred_element_type=jnp.float32
-    )
-    normed_part = normed_part + jnp.einsum(
-        "te,de->td", key_raw_grad, w_key, preferred_element_type=jnp.float32
-    )
-    normed_part = normed_part + jnp.einsum(
-        "te,de->td", value_raw_grad, w_value, preferred_element_type=jnp.float32
-    )
-    normed_grad = lax.psum(normed_part.astype(jnp.bfloat16), "tensor").astype(jnp.float32)
+    if compact:
+        small_part = local_width // ranks
+        gains = jnp.pad(
+            grad_qk_gain.reshape(2, ranks, small_part).transpose(1, 2, 0),
+            ((0, 0), (0, width // ranks - small_part), (0, 0)),
+        )
+        extras = jnp.concatenate(
+            [
+                grad_router.reshape(ranks, width // ranks, experts_total),
+                grad_ffn_gain.reshape(ranks, width // ranks, 1),
+                gains,
+            ],
+            axis=2,
+        ).astype(jnp.bfloat16)
+        extras = jnp.pad(extras, ((0, 0), (0, 0), (0, LANE - experts_total - 3)))
+        normed_grad, sums = closing(
+            normed,
+            query_raw_grad,
+            key_raw_grad,
+            value_raw_grad,
+            attended,
+            attention_grad,
+            w_query,
+            w_key,
+            w_value,
+            extras,
+        )
+        normed_grad = normed_grad.astype(jnp.float32)
+    else:
+        grad_w_out = jnp.einsum(
+            "td,te->de", attended, attention_grad, preferred_element_type=jnp.float32
+        )
+        grad_w_query = jnp.einsum(
+            "td,te->de", normed, query_raw_grad, preferred_element_type=jnp.float32
+        )
+        grad_w_key = jnp.einsum("td,te->de", normed, key_raw_grad, preferred_element_type=jnp.float32)
+        grad_w_value = jnp.einsum(
+            "td,te->de", normed, value_raw_grad, preferred_element_type=jnp.float32
+        )
+        normed_part = jnp.einsum(
+            "te,de->td", query_raw_grad, w_query, preferred_element_type=jnp.float32
+        )
+        normed_part = normed_part + jnp.einsum(
+            "te,de->td", key_raw_grad, w_key, preferred_element_type=jnp.float32
+        )
+        normed_part = normed_part + jnp.einsum(
+            "te,de->td", value_raw_grad, w_value, preferred_element_type=jnp.float32
+        )
+        normed_grad = lax.psum(normed_part.astype(jnp.bfloat16), "tensor").astype(jnp.float32)
     weighted_one = attn_gain * normed_grad
     grad_attn_gain = jnp.sum(normed_grad * source * scale_one, axis=0)
     input_grad = (
@@ -851,32 +1132,47 @@
         + scale_one * weighted_one
         - source * (scale_one**3 / width) * jnp.sum(weighted_one * source, axis=1, keepdims=True)
     )
-    summed = (
-        lax.psum_scatter(
-            grad_w_query.astype(jnp.bfloat16), "expert", scatter_dimension=0, tiled=True
-        ).astype(jnp.float32),
-        lax.psum_scatter(
-            grad_w_key.astype(jnp.bfloat16), "expert", scatter_dimension=0, tiled=True
-        ).astype(jnp.float32),
-        lax.psum_scatter(
-            grad_w_value.astype(jnp.bfloat16), "expert", scatter_dimension=0, tiled=True
-        ).astype(jnp.float32),
-        lax.psum_scatter(
-            grad_w_out.astype(jnp.bfloat16), "expert", scatter_dimension=1, tiled=True
-        ).astype(jnp.float32),
-        lax.psum_scatter(
-            grad_attn_gain.astype(jnp.bfloat16), "expert", scatter_dimension=0, tiled=True
-        ).astype(jnp.float32),
-        lax.psum_scatter(
-            grad_ffn_gain.astype(jnp.bfloat16), "expert", scatter_dimension=0, tiled=True
-        ).astype(jnp.float32),
-        lax.psum_scatter(
-            grad_qk_gain.astype(jnp.bfloat16), "expert", scatter_dimension=1, tiled=True
-        ).astype(jnp.float32),
-        lax.psum_scatter(
-            grad_router.astype(jnp.bfloat16), "expert", scatter_dimension=0, tiled=True
-        ).astype(jnp.float32),
-    )
+    if compact:
+        edge = 4 * local_width
+        summed = (
+            sums[:, :local_width],
+            sums[:, local_width : 2 * local_width],
+            sums[:, 2 * local_width : 3 * local_width],
+            sums[:, 3 * local_width : edge].T,
+            lax.psum_scatter(
+                grad_attn_gain.astype(jnp.bfloat16), "expert", scatter_dimension=0, tiled=True
+            ).astype(jnp.float32),
+            sums[:, edge + experts_total],
+            sums[:small_part, edge + experts_total + 1 : edge + experts_total + 3].T,
+            sums[:, edge : edge + experts_total],
+        )
+    else:
+        summed = (
+            lax.psum_scatter(
+                grad_w_query.astype(jnp.bfloat16), "expert", scatter_dimension=0, tiled=True
+            ).astype(jnp.float32),
+            lax.psum_scatter(
+                grad_w_key.astype(jnp.bfloat16), "expert", scatter_dimension=0, tiled=True
+            ).astype(jnp.float32),
+            lax.psum_scatter(
+                grad_w_value.astype(jnp.bfloat16), "expert", scatter_dimension=0, tiled=True
+            ).astype(jnp.float32),
+            lax.psum_scatter(
+                grad_w_out.astype(jnp.bfloat16), "expert", scatter_dimension=1, tiled=True
+            ).astype(jnp.float32),
+            lax.psum_scatter(
+                grad_attn_gain.astype(jnp.bfloat16), "expert", scatter_dimension=0, tiled=True
+            ).astype(jnp.float32),
+            lax.psum_scatter(
+                grad_ffn_gain.astype(jnp.bfloat16), "expert", scatter_dimension=0, tiled=True
+            ).astype(jnp.float32),
+            lax.psum_scatter(
+                grad_qk_gain.astype(jnp.bfloat16), "expert", scatter_dimension=1, tiled=True
+            ).astype(jnp.float32),
+            lax.psum_scatter(
+                grad_router.astype(jnp.bfloat16), "expert", scatter_dimension=0, tiled=True
+            ).astype(jnp.float32),
+        )
     return (
         output,
         input_grad,

time: 1320 us -> 666 us (0.50)
  waiting for transfers between devices: 671 us -> 134 us
  matrix products: 113 us -> 58.5 us
  Pallas kernels: 338 us -> 307 us
  other arithmetic: 72.3 us -> 56 us
    pallas_call x1, Pallas kernels: 338 us -> 128 us  [experts_fused(): pl.pallas_call(expert_kernel, out_shape=(jax.ShapeDtypeStruct((rows, wide...]
    reduce_scatter x5 -> x1, waiting for transfers between devices: 186 us -> 0.01 us  [body(): lax.psum_scatter(jnp.concatenate([key_grad_all[:prompt_count], value_grad...]
    pallas_call x0 -> x2, Pallas kernels: none -> 179 us  [the longest x1 109 us: closing(): pl.pallas_call(closing_kernel, out_shape=(jax.ShapeDtypeStruct((rows, wid...]
    psum x1, waiting for transfers between devices: 123 us -> 0.01 us  [body(): lax.psum(lax.psum_scatter(mixed_part.reshape(ranks * rows, width), 'exper...]
    psum x1 -> x0, waiting for transfers between devices: 121 us -> none  [body(): lax.psum(jnp.dot(attended, w_out, preferred_element_type=jnp.float32), 't...]
    all_gather x3 -> x1, waiting for transfers between devices: 74.5 us -> 23.6 us  [body(): lax.all_gather(jnp.concatenate([key_rot[:PROMPT_DEV], value_low[:PROMPT_D...]
    unnamed x18 -> x5, waiting for transfers between devices: 51.3 us -> 0.56 us
    all_gather x1, waiting for transfers between devices: 74.5 us -> 50.4 us  [body(): arrived = lax.all_gather(normed_two, 'expert', axis=0)]
  transfers between devices with their start and end apart: 15 -> 5, of which waited for: 14 -> 3; matrix products, arithmetic and copies ran while one was open for 12% -> 14% of each run, Pallas kernels for 0% -> 17%
where the time goes in v3:
time: 666 us; the launch traced here: 660 us
  Pallas kernels  307 us (46%)
  waiting for transfers between devices  134 us (20%)
  matrix products  58.5 us (9%)
  other arithmetic  56 us (8%)
  blocking collectives  45.7 us (7%)
  local copies, waits for them, and re-layouts  41.1 us (6%)
  between operations  17.1 us (3%)
    pallas_call x1, Pallas kernels, experts_fused(): pl.pallas_call(expert_kernel, out_shape=(jax.ShapeDtypeStruct((rows, wide...  128 us
    pallas_call x1, Pallas kernels, closing(): pl.pallas_call(closing_kernel, out_shape=(jax.ShapeDtypeStruct((rows, wid...  109 us
    pallas_call x1, Pallas kernels, summed_product(): pl.pallas_call(product_kernel, out_shape=(jax.ShapeDtypeStruct((rows, wid...  69.5 us
    reduce_scatter x1, waiting for transfers between devices, body(): lax.psum_scatter(mixed_part.reshape(ranks * rows, width), 'expert', scatt...  59.1 us
    all_gather x1, waiting for transfers between devices, body(): arrived = lax.all_gather(normed_two, 'expert', axis=0)  50.4 us
    all_gather x1, waiting for transfers between devices, body(): lax.all_gather(jnp.concatenate([key_rot[:PROMPT_DEV], value_low[:PROMPT_D...  23.6 us
    unnamed x259, local copies, waits for them, and re-layouts  22.6 us
    dot_general x2, matrix products, per_expert(): jnp.einsum('nrf,nrd->fd', gated[:, :, span], arrived_grad, preferred_elem...  14.2 us
  transfers between devices with their start and end apart: 5, of which 3 were waited for; matrix products, arithmetic and copies ran while one was open for 14% of the time, Pallas kernels for 17%

profile of v3, /device:TPU:0, one launch (start us, length us, event | category | flops | bytes accessed | tf_op | source)
XLA Modules:
  0.0 659.7 jit_solution(2992001482938227199)
XLA Ops:
  16.8 13.5 %psum.21 = f32[384,2]{0,1:T(2,128)S(1)} all-reduce(f32[384,2]{0,1:T(2,128)S(1)} %pad_maximum_fusion.16), channel_id=1, replica_groups=mesh['expert'=8,'tensor'=4] {'tensor'}, use_global_device_ids=true, to_apply=%region_3.4 | all-reduce | flops 768 | bytes 6144 | tf_op jit(solution)/shard_map/psum | solution.py:842
  38.0 23.6 %all-gather.5.cloned.1.call-done = bf16[1024,1024]{1,0:T(8,128)(2,1)} async-done(((bf16[128,1024]{1,0:T(8,128)(2,1)}), bf16[1024,1024]{1,0:T(8,128)(2,1)}) %all-gather.5.cloned.1.call-update) | async-done | bytes 2097168 | tf_op jit(solution)/shard_map/all_gather | solution.py:861
  71.8 69.5 %shard_map.246 = (bf16[384,2048]{1,0:T(8,128)(2,1)S(1)}, bf16[8,384,2048]{2,1,0:T(8,128)(2,1)}) custom-call(bf16[384,512]{1,0:T(8,128)(2,1)S(1)} %pad_maximum_fusion.9.left.attended, bf16[512,2048]{1,0:T(8,128)(2,1)S(1)} %copy-done.3, bf16[384,2048]{1,0:T(8,128)(2,1)S(1)} %copy-done), custom_call_target="tpu_custom_call" | custom-call | tf_op jit(solution)/shard_map/pallas_call | solution.py:604
  145.4 8.5 %all-gather.1 = s32[3072,8]{0,1:T(8,128)S(1)} all-gather(s32[384,8]{0,1:T(8,128)S(1)} %copy-done.72), channel_id=3, replica_groups=mesh['expert'=8,'tensor'=4] {'expert'}, dimensions={0}, use_global_device_ids=true | all-gather | bytes 110592 | tf_op jit(solution)/shard_map/all_gather | solution.py:921
  164.1 50.4 %all-gather.7.cloned.1.call-done = bf16[3072,2048]{1,0:T(8,128)(2,1)} async-done(((bf16[384,2048]{1,0:T(8,128)(2,1)}), bf16[3072,2048]{1,0:T(8,128)(2,1)}) %all-gather.7.cloned.1.call-update) | async-done | bytes 12582928 | tf_op jit(solution)/shard_map/all_gather | solution.py:929
  214.5 128.3 %shard_map.247 = (bf16[384,2176]{1,0:T(8,128)(2,1)}, bf16[8,384,512]{2,1,0:T(8,128)(2,1)}, bf16[8,384,512]{2,1,0:T(8,128)(2,1)}, bf16[8,384,512]{2,1,0:T(8,128)(2,1)}, bf16[8,384,2048]{2,1,0:T(8,128)(2,1)}) custom-call(bf16[8,384,2048]{2,1,0:T(8,128)(2,1)} %bitcast.137, bf16[8,384,2048]{2,1,0:T(8,128)(2,1)} %get-tuple-element.23.g_all, ...), custom_call_target="tpu_custom_call" | custom-call | flops 38654705664 | bytes 50331648 | tf_op jit(solution)/shard_map/pallas_call | solution.py:537
  344.2 4.2 multiply_reduce_fusion
  384.1 7.1 %convolution_bitcast_fusion = f32[1,256,2048]{2,1,0:T(8,128)S(1)} fusion(bf16[8,384,2048]{2,1,0:T(8,128)(2,1)} %get-tuple-element.23.g_all, bf16[8,384,512]{2,1,0:T(8,128)(2,1)} %get-tuple-element.30), kind=kOutput, calls=%fused_computation.35 | convolution fusion | flops 3221225472 | bytes 16252928 | tf_op jit(solution)/shard_map/nrf,nrd->fd/dot_general | solution.py:948
  391.2 7.2 %convolution_bitcast_fusion.1 = f32[1,256,2048]{2,1,0:T(8,128)S(1)} fusion(bf16[8,384,2048]{2,1,0:T(8,128)(2,1)} %get-tuple-element.23.g_all, bf16[8,384,512]{2,1,0:T(8,128)(2,1)S(1)} %copy-done.44), kind=kOutput, calls=%fused_computation.36 | convolution fusion | flops 3221225472 | bytes 16252928 | tf_op jit(solution)/shard_map/nrf,nrd->fd/dot_general | solution.py:948
  398.4 2.5 pad_maximum_fusion.2
  401.5 3.9 convolution_bitcast_fusion.4
  405.4 3.9 convolution_bitcast_fusion.5
  409.3 5.4 convolution_bitcast_fusion.2
  414.8 5.5 convolution_bitcast_fusion.3
  420.3 5.1 pad_maximum_fusion
  430.3 2.4 multiply_add_fusion
  437.1 11.9 %psum.23 = f32[384,2]{0,1:T(2,128)S(1)} all-reduce(f32[384,2]{0,1:T(2,128)S(1)} %pad_maximum_fusion.17), channel_id=1, replica_groups=mesh['expert'=8,'tensor'=4] {'tensor'}, use_global_device_ids=true, to_apply=%region_28.29 | all-reduce | flops 768 | bytes 6144 | tf_op jit(solution)/shard_map/psum | solution.py:1065
  449.8 59.1 %reduce-scatter.3.cloned.1.call-done = bf16[384,2048]{1,0:T(8,128)(2,1)} async-done(((bf16[3072,2048]{1,0:T(8,128)(2,1)}), bf16[384,2048]{1,0:T(8,128)(2,1)}) %reduce-scatter.3.cloned.1.call-update) | async-done | bytes 1572880 | tf_op jit(solution)/shard_map/reduce_scatter | solution.py:936
  509.0 2.3 subtract_convert_fusion.1.query_grad
  513.4 109.3 %shard_map.248 = (bf16[384,2048]{1,0:T(8,128)(2,1)}, f32[256,2176]{1,0:T(8,128)}) custom-call(bf16[384,2048]{1,0:T(8,128)(2,1)} %copy-done.35, bf16[384,512]{1,0:T(8,128)(2,1)} %subtract_convert_fusion.1.query_grad, bf16[384,512]{1,0:T(8,128)(2,1)} %subtract_convert_fusion.key_grad, bf16[384,512]{1,0:T(8,128)(2,1)} %pad_maximum_fusion.10.value_grad, ...), custom_call_target="tpu_custom_call" | custom-call | tf_op jit(solution)/shard_map/pallas_call | solution.py:699
  625.8 2.7 slice_bitcast_fusion
  629.5 2.9 fusion.9
  632.3 11.8 %all-reduce.4 = bf16[2048]{0:T(1024)(128)(2,1)S(1)} all-reduce(bf16[2048]{0:T(1024)(128)(2,1)S(1)} %get-tuple-element.98), channel_id=6, replica_groups=mesh['expert'=8,'tensor'=4] {'expert'}, use_global_device_ids=true, to_apply=%region_34.35.clone | all-reduce | flops 2048 | bytes 8192
  646.5 6.5 fusion.2
  (398 shorter events, 95.1 us)
Async XLA Ops:
  7.2 54.4 %all-gather.5.cloned.1.call-start = ((), (), s32[]{:S(2)}) async-start(), calls=%async_computation.2 | async-start | bytes 2359296 | tf_op jit(solution)/shard_map/all_gather | solution.py:861
  10.6 20.4 %copy-start.79 = (f32[1,512]{1,0:T(1,128)}, f32[1,512]{1,0:T(1,128)S(1)}, u32[]{:S(2)}) copy-start(f32[1,512]{1,0:T(1,128)S(1)} %get-tuple-element.135) | copy-start | bytes 6148
  10.6 21.4 %copy-start.81 = (f32[1,512]{1,0:T(1,128)}, f32[1,512]{1,0:T(1,128)S(1)}, u32[]{:S(2)}) copy-start(f32[1,512]{1,0:T(1,128)S(1)} %get-tuple-element.134) | copy-start | bytes 6148
  15.2 16.7 %copy-start.29 = (f32[384,512]{1,0:T(8,128)}, f32[384,512]{1,0:T(8,128)S(1)}, u32[]{:S(2)}) copy-start(f32[384,512]{1,0:T(8,128)S(1)} %get-tuple-element.145) | copy-start | bytes 2359300
  16.8 15.3 %copy-start.27 = (f32[384,512]{1,0:T(8,128)}, f32[384,512]{1,0:T(8,128)S(1)}, u32[]{:S(2)}) copy-start(f32[384,512]{1,0:T(8,128)S(1)} %get-tuple-element.143) | copy-start | bytes 2359300
  35.3 179.2 %all-gather.7.cloned.1.call-start = ((), (), s32[]{:S(2)}) async-start(), calls=%async_computation.6 | async-start | bytes 14155776 | tf_op jit(solution)/shard_map/all_gather | solution.py:929
  35.6 33.0 %copy-start.33 = (bf16[256,512]{1,0:T(8,128)(2,1)}, bf16[256,512]{1,0:T(8,128)(2,1)S(1)}, u32[]{:S(2)}) copy-start(bf16[256,512]{1,0:T(8,128)(2,1)S(1)} %slice.278) | copy-start | bytes 786436
  37.0 28.1 %copy-start.58 = (bf16[48,8,4,128]{3,1,2,0:T(8,128)(2,1)}, bf16[48,8,4,128]{3,1,2,0:T(8,128)(2,1)S(1)}, u32[]{:S(2)}) copy-start(bf16[48,8,4,128]{3,1,2,0:T(8,128)(2,1)S(1)} %copy.210) | copy-start | bytes 1179652
  71.7 69.5 %copy-start.2 = (bf16[384,512]{1,0:T(8,128)(2,1)}, bf16[384,512]{1,0:T(8,128)(2,1)S(1)}, u32[]{:S(2)}) copy-start(bf16[384,512]{1,0:T(8,128)(2,1)S(1)} %pad_maximum_fusion.9.left.attended) | copy-start | bytes 1179652
  71.7 69.6 %copy-start.6 = (bf16[384,2048]{1,0:T(8,128)(2,1)S(1)}, bf16[384,2048]{1,0:T(8,128)(2,1)}, u32[]{:S(2)}) copy-start(bf16[384,2048]{1,0:T(8,128)(2,1)} %param.15) | copy-start | bytes 4718596
  144.4 10.3 %copy-start.68 = (bf16[2048,16]{0,1:T(8,128)(2,1)S(1)}, bf16[2048,16]{0,1:T(8,128)(2,1)}, u32[]{:S(2)}) copy-start(bf16[2048,16]{0,1:T(8,128)(2,1)} %param.23) | copy-start | bytes 196612
  144.5 280.9 %reduce-scatter.5.cloned.1.call-start = ((), (), s32[]{:S(2)}) async-start(), calls=%async_computation.5 | async-start | bytes 2359296 | tf_op jit(solution)/shard_map/reduce_scatter | solution.py:1039
  370.8 138.1 %reduce-scatter.3.cloned.1.call-start = ((), (), s32[]{:S(2)}) async-start(), calls=%async_computation.3 | async-start | bytes 14155776 | tf_op jit(solution)/shard_map/reduce_scatter | solution.py:936
  371.4 275.1 %all-reduce.7.cloned.1.call-start = ((), (), s32[]{:S(2)}) async-start(), calls=%async_computation.4 | async-start | bytes 3145728 | tf_op jit(solution)/shard_map/psum | solution.py:935
  384.1 16.8 %slice-start.1 = ((s8[12582912]{0:T(1024)(128)(4,1)}), s8[4194304]{0:T(1024)(128)(4,1)S(1)}, s32[]{:S(2)}) async-start(s8[12582912]{0:T(1024)(128)(4,1)} %bitcast.138), calls=%async_computation.8 | async-start | bytes 8388608
  384.1 16.8 %slice-start.2 = ((s8[12582912]{0:T(1024)(128)(4,1)}), s8[4194304]{0:T(1024)(128)(4,1)S(1)}, s32[]{:S(2)}) async-start(s8[12582912]{0:T(1024)(128)(4,1)} %bitcast.138), calls=%async_computation.9 | async-start | bytes 8388608
  391.2 9.7 %slice-start.3 = ((s8[12582912]{0:T(1024)(128)(4,1)}), s8[4194304]{0:T(1024)(128)(4,1)S(1)}, s32[]{:S(2)}) async-start(s8[12582912]{0:T(1024)(128)(4,1)} %bitcast.138), calls=%async_computation.10 | async-start | bytes 8388608
  435.1 13.9 %copy-start.64 = (bf16[256,512]{1,0:T(8,128)(2,1)S(1)}, bf16[256,512]{1,0:T(8,128)(2,1)}, u32[]{:S(2)}) copy-start(bf16[256,512]{1,0:T(8,128)(2,1)} %maximum_convert_fusion.1) | copy-start | bytes 786436
  435.8 73.1 %copy-start.113 = (f32[384]{0:T(512)S(1)}, f32[384]{0:T(512)}, u32[]{:S(2)}) copy-start(f32[384]{0:T(512)} %get-tuple-element.105) | copy-start | bytes 4612
  449.8 61.5 %copy-start.112 = (f32[384]{0:T(512)S(1)}, f32[384]{0:T(512)}, u32[]{:S(2)}) copy-start(f32[384]{0:T(512)} %get-tuple-element.104) | copy-start | bytes 4612
  628.5 18.0 %copy-start.89 = (f32[384]{0:T(512)S(1)}, f32[384]{0:T(512)}, u32[]{:S(2)}) copy-start(f32[384]{0:T(512)} %copy-done.87) | copy-start | bytes 4612
  628.5 18.0 %copy-start.93 = (f32[384]{0:T(512)S(1)}, f32[384]{0:T(512)}, u32[]{:S(2)}) copy-start(f32[384]{0:T(512)} %get-tuple-element.140) | copy-start | bytes 4612
  628.5 18.0 %copy-start.95 = (f32[384]{0:T(512)S(1)}, f32[384]{0:T(512)}, u32[]{:S(2)}) copy-start(f32[384]{0:T(512)} %get-tuple-element.138) | copy-start | bytes 4612
  628.5 18.0 %copy-start.115 = (f32[384]{0:T(512)S(1)}, f32[384]{0:T(512)}, u32[]{:S(2)}) copy-start(f32[384]{0:T(512)} %copy-done.114) | copy-start | bytes 4612
  (106 other events, 276.3 us)
Sparse Core Ops, SparseCore 0:
  35.4 26.0 all-gather.4
  144.6 69.8 all-gather.6
  370.9 41.7 reduce-scatter.4
  416.5 92.3 reduce-scatter.2
  511.3 94.1 all-reduce.6

commit v4 on v3

--- a/solution.py
+++ b/solution.py
@@ -175,7 +175,8 @@
 
 
 class Plane(Place):
-    def __init__(self, own, spare, paired, from_x, from_y, pair_sems, x_sems, y_sems):
+    def __init__(self, own, spare, paired, from_x, from_y, pair_sems, x_sems, y_sems, by_device=False):
+        self.by_device = by_device
         self.own, self.spare, self.paired, self.from_x, self.from_y = own, spare, paired, from_x, from_y
         self.pair_sems, self.x_sems, self.y_sems = pair_sems, x_sems, y_sems
         super().__init__()
@@ -192,8 +193,9 @@
         ]
 
     def pair_copy(self, chip):
+        place = self.block(chip, 1 - self.core) if self.by_device else chip
         return remote(
-            self.spare.at[chip], self.paired.at[chip],
+            self.spare.at[place], self.paired.at[chip],
             self.pair_sems.at[0, chip], self.pair_sems.at[1, chip], expert=self.sibling,
         )
 
@@ -626,84 +628,254 @@
 
 
 def closing_kernel(
-    normed, query_grad, key_grad, value_grad, attended, attention_grad, w_query, w_key, w_value, extras,
-    total, sums,
-    line_own, line_in, part, paired, from_x, from_y, line_sems, pair_sems, x_sems, y_sems,
+    normed, query_grad, key_grad, value_grad, attended, attention_grad, extras,
+    w_query, w_key, w_value, mixed, x_all, g_all, gated_all, gate_all, up_all,
+    total, sums, mixture, gate_out, up_out, down_out,
+    line_own, line_in, part, paired, from_x, from_y,
+    mix_own, mix_paired, mix_x, mix_y, mix_in, tiles, factors, results, downs,
+    line_sems, pair_sems, x_sems, y_sems, mix_line_sems, mix_pair_sems, mix_x_sems, mix_y_sems,
+    load_sems, weight_sems, factor_sems, tile_sems, out_sems,
 ):
-    rows, width = normed.shape
+    width = normed.shape[1]
     heads = query_grad.shape[1]
     share = part.shape[2]
-    tile = min(512, width)
+    experts, _, hidden = gate_out.shape
+    column_tile = min(512, width // 2)
+    tile = tiles.shape[2]
+    count = width // tile
     line = Line(line_own, line_in, total, line_sems)
     plane = Plane(part.at[1], part.at[0], paired, from_x, from_y, pair_sems, x_sems, y_sems)
+    mix = Plane(mix_own, mixed, mix_paired, mix_x, mix_y, mix_pair_sems, mix_x_sems, mix_y_sems, by_device=True)
+    mix_line = Line(mix_own.at[3], mix_in, mixture, mix_line_sems)
+    half = width // 2
+
+    def load_own(chip):
+        return pltpu.make_async_copy(mixed.at[mix.block(chip, mix.core)], mix_own.at[chip], load_sems.at[chip])
+
+    weight_loads = [
+        pltpu.make_async_copy(w_query, factors.at[0, 0:width], weight_sems.at[0]),
+        pltpu.make_async_copy(w_key, factors.at[1, 0:width], weight_sems.at[1]),
+        pltpu.make_async_copy(w_value.at[0:half], factors.at[0, width : width + half], weight_sems.at[2]),
+        pltpu.make_async_copy(w_value.at[half:], factors.at[1, width : width + half], weight_sems.at[3]),
+    ]
+
+    def factor_load(matrix):
+        return pltpu.make_async_copy(
+            (gate_all, up_all, gated_all)[matrix], factors.at[matrix % 2], factor_sems.at[matrix]
+        )
+
+    def tile_copy(source, s):
+        columns = pl.ds(pl.multiple_of(s % count * tile, tile), tile)
+        return pltpu.make_async_copy(source.at[:, columns], tiles.at[s % 2], tile_sems.at[s % 2])
+
+    def start_tile(s):
+        @pl.when(s < 2 * count)
+        def _():
+            tile_copy(x_all, s).start()
+
+        @pl.when(s >= 2 * count)
+        def _():
+            tile_copy(g_all, s).start()
+
+    def across(target, s):
+        rows = pl.ds(pl.multiple_of(s % count * tile, tile), tile)
+        return [
+            pltpu.make_async_copy(
+                results.at[s % 2, :, j * hidden : (j + 1) * hidden], target.at[j, rows], out_sems.at[0, s % 2, j]
+            )
+            for j in range(experts)
+        ]
+
+    def down(s):
+        columns = pl.ds(pl.multiple_of(s % count * tile, tile), tile)
+        return [
+            pltpu.make_async_copy(
+                downs.at[s % 2, j * hidden : (j + 1) * hidden], down_out.at[j, :, columns], out_sems.at[1, s % 2, j]
+            )
+            for j in range(experts)
+        ]
+
+    def expert_tile(s):
+        @pl.when(s + 1 < 3 * count)
+        def _():
+            start_tile(s + 1)
+
+        for matrix in range(3):
+
+            @pl.when(s == matrix * count)
+            def _():
+                factor_load(matrix).wait()
+
+        tile_copy(x_all, s).wait()
+
+        @pl.when(s < 2 * count)
+        def _():
+            @pl.when(s >= 2)
+            def _():
+                for copy in across(gate_out, s):
+                    copy.wait()
+
+            results[s % 2] = crossed_dot(tiles[s % 2], factors[s // count])
+
+            @pl.when(s < count)
+            def _():
+                for copy in across(gate_out, s):
+                    copy.start()
+
+            @pl.when(s >= count)
+            def _():
+                for copy in across(up_out, s):
+                    copy.start()
+
+        @pl.when(s >= 2 * count)
+        def _():
+            @pl.when(s >= 2 * count + 2)
+            def _():
+                for copy in down(s):
+                    copy.wait()
+
+            downs[s % 2] = crossed_dot(factors[0], tiles[s % 2])
+            for copy in down(s):
+                copy.start()
+
+        @pl.when(s == count - 1)
+        def _():
+            factor_load(2).start()
+
+    def dense_block(i):
+        chip, sub = i // 2, i % 2
+        block = plane.block(chip, (plane.core + 1 - sub) % 2)
+        columns = pl.ds(pl.multiple_of(block * share, share), share)
+        source = normed[:, columns]
+        part[sub, chip, :, 0:heads] = crossed_dot(source, query_grad[...]).astype(jnp.bfloat16)
+        part[sub, chip, :, heads : 2 * heads] = crossed_dot(source, key_grad[...]).astype(jnp.bfloat16)
+        part[sub, chip, :, 2 * heads : 3 * heads] = crossed_dot(source, value_grad[...]).astype(jnp.bfloat16)
+        part[sub, chip, :, 3 * heads : 4 * heads] = crossed_dot(
+            attention_grad[:, columns], attended[...]
+        ).astype(jnp.bfloat16)
+        part[sub, chip, :, 4 * heads :] = extras[block]
+
+        @pl.when(sub == 0)
+        def _():
+            plane.pair_copy(chip).start()
+
+    for copy in weight_loads:
+        copy.start()
+    for chip in range(4):
+        load_own(chip).start()
     greet(plane.neighbours() + line.neighbours())
-    for start in range(0, width, tile):
-        columns = slice(start, start + tile)
+    for chip in range(4):
+        mix.pair_copy(chip).start()
+    for copy in weight_loads:
+        copy.wait()
+    for start in range(0, width, column_tile):
+        columns = slice(start, start + column_tile)
+        later = width + start % half
         line_own[:, columns] = (
-            turned_dot(query_grad[...], w_query[columns])
-            + turned_dot(key_grad[...], w_key[columns])
-            + turned_dot(value_grad[...], w_value[columns])
+            turned_dot(query_grad[...], factors[0, columns])
+            + turned_dot(key_grad[...], factors[1, columns])
+            + turned_dot(value_grad[...], factors[start // half, later : later + column_tile])
         ).astype(jnp.bfloat16)
-
-    def pair(chip, carry):
-        for sub in range(2):
-            block = plane.block(chip, (plane.core + 1 - sub) % 2)
-            columns = pl.ds(pl.multiple_of(block * share, share), share)
-            source = normed[:, columns]
-            part[sub, chip, :, 0:heads] = crossed_dot(source, query_grad[...]).astype(jnp.bfloat16)
-            part[sub, chip, :, heads : 2 * heads] = crossed_dot(source, key_grad[...]).astype(jnp.bfloat16)
-            part[sub, chip, :, 2 * heads : 3 * heads] = crossed_dot(source, value_grad[...]).astype(jnp.bfloat16)
-            part[sub, chip, :, 3 * heads : 4 * heads] = crossed_dot(
-                attention_grad[:, columns], attended[...]
-            ).astype(jnp.bfloat16)
-            part[sub, chip, :, 4 * heads :] = extras[block]
-            if sub == 0:
-                plane.pair_copy(chip).start()
-        line.advance(chip)
-        return carry
-
-    lax.fori_loop(0, 4, pair, 0)
-    for chip in range(4):
-        plane.pair_copy(chip).wait_recv()
-    for chip in range(3):
-        plane.send_first(chip)
-    late = plane.pieces + 2
+    factor_load(0).start()
+    factor_load(1).start()
+    start_tile(0)
+    mix_last = mix.pieces + 1
+    dense_first = 8 + 5
+    dense_second = dense_first + plane.pieces // 2 + 2
+    dense_last = dense_second + plane.pieces // 2 + 1
 
     def step(s, carry):
         line.advance(s)
-
-        @pl.when(s - 4 < plane.pieces)
-        def _():
-            plane.second_piece(s - 4)
-
-        @pl.when((s >= 4 + late) & (s - 4 - late < plane.pieces))
-        def _():
-            piece = s - 4 - late
+        for chip in range(4):
+
+            @pl.when(s == chip)
+            def _():
+                load_own(chip).wait()
+                mix.pair_copy(chip).wait_recv()
+                if chip < 3:
+                    mix.send_first(chip)
+
+        @pl.when((s >= 3) & (s - 3 < mix.pieces))
+        def _():
+            mix.second_piece(s - 3)
+
+        @pl.when((s >= mix_last) & (s - mix_last < mix.pieces))
+        def _():
+            piece = s - mix_last
+            for side, summed in enumerate(mix.last_sum(piece)):
+                mix_own[3, mix.rows(side, piece)] = summed.astype(jnp.bfloat16)
+
+        mix_line.advance(s - mix_last)
+
+        @pl.when((s >= 4) & (s < 12))
+        def _():
+            dense_block(s - 4)
+
+        @pl.when(s == dense_first)
+        def _():
+            for chip in range(4):
+                plane.pair_copy(chip).wait_recv()
+            for chip in range(3):
+                plane.send_first(chip)
+
+        @pl.when((s >= dense_second) & (s - dense_second < plane.pieces))
+        def _():
+            plane.second_piece(s - dense_second)
+
+        @pl.when((s >= dense_last) & (s - dense_last < plane.pieces))
+        def _():
+            piece = s - dense_last
             for side, summed in enumerate(plane.last_sum(piece)):
                 sums[plane.rows(side, piece)] = summed
 
+        @pl.when(s < 3 * count)
+        def _():
+            expert_tile(s)
+
         return carry
 
-    lax.fori_loop(4, jnp.maximum(line.steps(), 4 + late + plane.pieces), step, 0)
-    plane.finish()
-    line.finish()
-
-
-def closing(normed, query_grad, key_grad, value_grad, attended, attention_grad, w_query, w_key, w_value, extras):
+    steps = jnp.maximum(mix_last + mix_line.steps(), jnp.maximum(3 * count, dense_last + plane.pieces))
+    lax.fori_loop(0, steps, step, 0)
+    for s in (2 * count - 2, 2 * count - 1):
+        for copy in across(up_out, s):
+            copy.wait()
+    for s in (3 * count - 2, 3 * count - 1):
+        for copy in down(s):
+            copy.wait()
+    for each in (plane, line, mix, mix_line):
+        each.finish()
+
+
+TILE = 256
+
+
+def closing(
+    normed, query_grad, key_grad, value_grad, attended, attention_grad, extras, w_query, w_key, w_value,
+    mixed, arrived, arrived_grad, gated, gate_grad, up_grad, experts,
+):
     rows, width = normed.shape
     heads = query_grad.shape[1]
     ranks, share, more = extras.shape
     wide = 4 * heads + more
+    inner = gated.shape[2]
+    hidden = inner // experts
     low = jnp.bfloat16
+    tile = min(TILE, width // 2)
     vmem = pl.BlockSpec(memory_space=pltpu.VMEM)
+    any_space = pl.BlockSpec(memory_space=pl.ANY)
+    every = ranks * rows
     return pl.pallas_call(
         closing_kernel,
         out_shape=(
             jax.ShapeDtypeStruct((rows, width), low),
             jax.ShapeDtypeStruct((share, wide), jnp.float32),
+            jax.ShapeDtypeStruct((rows, width), low),
+            jax.ShapeDtypeStruct((experts, width, hidden), jnp.float32),
+            jax.ShapeDtypeStruct((experts, width, hidden), jnp.float32),
+            jax.ShapeDtypeStruct((experts, hidden, width), jnp.float32),
         ),
-        in_specs=[vmem] * 10,
-        out_specs=(vmem, vmem),
+        in_specs=[vmem] * 7 + [any_space] * 9,
+        out_specs=(vmem,) * 3 + (any_space,) * 3,
         scratch_shapes=[
             pltpu.VMEM((rows, width), low),
             pltpu.VMEM((rows, width), low),
@@ -711,13 +883,33 @@
             pltpu.VMEM((4, share, wide), low),
             pltpu.VMEM((3, share // 2, wide), low),
             pltpu.VMEM((3, share // 2, wide), low),
+            pltpu.VMEM((4, rows, width), low),
+            pltpu.VMEM((4, rows, width), low),
+            pltpu.VMEM((3, rows // 2, width), low),
+            pltpu.VMEM((3, rows // 2, width), low),
+            pltpu.VMEM((rows, width), low),
+            pltpu.VMEM((2, every, tile), low),
+            pltpu.VMEM((2, every, inner), low),
+            pltpu.VMEM((2, tile, inner), jnp.float32),
+            pltpu.VMEM((2, inner, tile), jnp.float32),
             Line.semaphores(rows),
             *Plane.semaphores(share),
+            Line.semaphores(rows),
+            *Plane.semaphores(rows),
+            pltpu.SemaphoreType.DMA((4,)),
+            pltpu.SemaphoreType.DMA((4,)),
+            pltpu.SemaphoreType.DMA((3,)),
+            pltpu.SemaphoreType.DMA((2,)),
+            pltpu.SemaphoreType.DMA((2, 2, experts)),
         ],
         compiler_params=pltpu.CompilerParams(
-            collective_id=2, has_side_effects=True, vmem_limit_bytes=58 * 2**20
+            collective_id=2, has_side_effects=True, vmem_limit_bytes=63 * 2**20
         ),
-    )(normed, query_grad, key_grad, value_grad, attended, attention_grad, w_query, w_key, w_value, extras)
+    )(
+        normed, query_grad, key_grad, value_grad, attended, attention_grad, extras, w_query, w_key, w_value,
+        mixed, arrived.reshape(every, width), arrived_grad.reshape(every, width),
+        gated.reshape(every, inner), gate_grad.reshape(every, inner), up_grad.reshape(every, inner),
+    )
 
 
 epsilon = 1e-05
@@ -833,6 +1025,15 @@
     angle = position.astype(jnp.float32)[:, None] * frequency[None, :]
     cosine = jnp.cos(angle)[:, None, :]
     sine = jnp.sin(angle)[:, None, :]
+    if compact:
+        routes_all = lax.all_gather(routes, "expert", axis=0)
+        own_expert = device * local_experts + jnp.arange(local_experts, dtype=jnp.int32)
+        expert_mask = jnp.any(routes_all[:, :, :, None] == own_expert, axis=2).astype(jnp.float32)
+        expert_mask = jnp.pad(expert_mask, ((0, 0), (0, 0), (0, LANE - local_experts)))
+        own_first = jnp.roll(router, -device * local_experts, axis=1)
+        own_first = jnp.pad(own_first, ((0, 0), (0, LANE - experts_total)))
+        bias = jnp.where(jnp.arange(LANE) < experts_total, 0.0, masked_value)
+        bias = bias.astype(jnp.float32)[None]
     source = tokens.astype(jnp.float32)
     scale_one = lax.rsqrt(jnp.mean(source * source, axis=1, keepdims=True) + epsilon)
     normed = (source * scale_one * attn_gain).astype(jnp.bfloat16)
@@ -918,39 +1119,12 @@
     rows_mask = jnp.sum(hits, axis=1)
     grad_out = cotangent.astype(jnp.float32)
     if compact:
-        routes_all = lax.all_gather(routes, "expert", axis=0)
-        own_expert = device * local_experts + jnp.arange(local_experts, dtype=jnp.int32)
-        own_mask = jnp.any(routes_all[:, :, :, None] == own_expert, axis=2).astype(jnp.float32)
-        own_mask = jnp.pad(own_mask, ((0, 0), (0, 0), (0, LANE - local_experts)))
-        own_first = jnp.roll(router, -device * local_experts, axis=1)
-        own_first = jnp.pad(own_first, ((0, 0), (0, LANE - experts_total)))
-        bias = jnp.where(jnp.arange(LANE) < experts_total, 0.0, masked_value)
-        bias = bias.astype(jnp.float32)[None]
         arrived = lax.all_gather(normed_two, "expert", axis=0)
         reduced, gated, gate_grad, up_grad, mixed_part = experts_fused(
-            arrived, arrived_grad, own_mask, own_first, bias, w_gate, w_up, w_down
+            arrived, arrived_grad, expert_mask, own_first, bias, w_gate, w_up, w_down
         )
         moe_input_grad = reduced[:, :width].astype(jnp.float32)
         chance_grad = reduced[:, width : width + experts_total].astype(jnp.float32)
-        mixture = lax.psum(
-            lax.psum_scatter(
-                mixed_part.reshape(ranks * rows, width), "expert", scatter_dimension=0, tiled=True
-            ),
-            "tensor",
-        ).astype(jnp.float32)
-        hidden_units = w_gate.shape[2]
-
-        def per_expert(j):
-            span = slice(j * hidden_units, (j + 1) * hidden_units)
-            return (
-                jnp.einsum("nrd,nrf->df", arrived, gate_grad[:, :, span], preferred_element_type=jnp.float32),
-                jnp.einsum("nrd,nrf->df", arrived, up_grad[:, :, span], preferred_element_type=jnp.float32),
-                jnp.einsum("nrf,nrd->fd", gated[:, :, span], arrived_grad, preferred_element_type=jnp.float32),
-            )
-
-        grad_w_gate, grad_w_up, grad_w_down = (
-            jnp.stack(list(parts)) for parts in zip(*(per_expert(j) for j in range(local_experts)))
-        )
     else:
         routed = lax.all_gather(
             (rows_mask * chances).astype(jnp.float32), "expert", axis=0, tiled=True
@@ -983,7 +1157,6 @@
         )
         grad_w_gate, grad_w_up, grad_w_down = weight_grads
     chance_grad = rows_mask * chance_grad
-    output = (hidden + mixture).astype(jnp.bfloat16)
     logit_grad = (
         chances * (chance_grad - jnp.sum(chances * chance_grad, axis=1, keepdims=True))
     ).astype(jnp.bfloat16)
@@ -1091,18 +1264,26 @@
             axis=2,
         ).astype(jnp.bfloat16)
         extras = jnp.pad(extras, ((0, 0), (0, 0), (0, LANE - experts_total - 3)))
-        normed_grad, sums = closing(
+        normed_grad, sums, mixture, grad_w_gate, grad_w_up, grad_w_down = closing(
             normed,
             query_raw_grad,
             key_raw_grad,
             value_raw_grad,
             attended,
             attention_grad,
+            extras,
             w_query,
             w_key,
             w_value,
-            extras,
-        )
+            mixed_part,
+            arrived,
+            arrived_grad,
+            gated,
+            gate_grad,
+            up_grad,
+            local_experts,
+        )
+        mixture = mixture.astype(jnp.float32)
         normed_grad = normed_grad.astype(jnp.float32)
     else:
         grad_w_out = jnp.einsum(
@@ -1173,6 +1354,7 @@
                 grad_router.astype(jnp.bfloat16), "expert", scatter_dimension=0, tiled=True
             ).astype(jnp.float32),
         )
+    output = (hidden + mixture).astype(jnp.bfloat16)
     return (
         output,
         input_grad,

time: 666 us -> 626 us (0.940)
  matrix products: 58.5 us -> 23.6 us
  waiting for transfers between devices: 134 us -> 104 us
  Pallas kernels: 307 us -> 323 us
  local copies, waits for them, and re-layouts: 41.1 us -> 56.1 us
  other arithmetic: 56 us -> 49.1 us
    reduce_scatter x1 -> x0, waiting for transfers between devices: 59.1 us -> none  [body(): lax.psum_scatter(mixed_part.reshape(ranks * rows, width), 'expert', scatt...]
    dot_general x6 -> x0, matrix products: 32.9 us -> none  [the longest x2 14.2 us: per_expert(): jnp.einsum('nrf,nrd->fd', gated[:, :, span], arrived_grad, preferred_elem...]
    reduce_scatter x1, waiting for transfers between devices: 0.01 us -> 30 us  [body(): lax.psum_scatter(jnp.concatenate([key_grad_all[:prompt_count], value_grad...]
    pallas_call x1, Pallas kernels: 109 us -> 125 us  [closing(): pl.pallas_call(closing_kernel, out_shape=(jax.ShapeDtypeStruct((rows, wid...]
    unnamed x259 -> x256, local copies, waits for them, and re-layouts: 22.6 us -> 31 us
    another operation x4 -> x2, other arithmetic: 8.85 us -> 1.94 us  [the longest x2 7.57 us: body(): jnp.stack(list(parts))]
  transfers between devices with their start and end apart: 5 -> 3, of which waited for: 3 -> 3; matrix products, arithmetic and copies ran while one was open for 14% -> 4% of each run, Pallas kernels for 17% -> 0%
where the time goes in v4:
time: 626 us; the launch traced here: 619 us
  Pallas kernels  323 us (52%)
  waiting for transfers between devices  104 us (17%)
  local copies, waits for them, and re-layouts  56.1 us (9%)
  other arithmetic  49.1 us (8%)
  blocking collectives  45.9 us (7%)
  matrix products  23.6 us (4%)
  between operations  17.2 us (3%)
    pallas_call x1, Pallas kernels, experts_fused(): pl.pallas_call(expert_kernel, out_shape=(jax.ShapeDtypeStruct((rows, wide...  128 us
    pallas_call x1, Pallas kernels, closing(): pl.pallas_call(closing_kernel, out_shape=(jax.ShapeDtypeStruct((rows, wid...  125 us
    pallas_call x1, Pallas kernels, summed_product(): pl.pallas_call(product_kernel, out_shape=(jax.ShapeDtypeStruct((rows, wid...  69.6 us
    all_gather x1, waiting for transfers between devices, body(): arrived = lax.all_gather(normed_two, 'expert', axis=0)  50.6 us
    unnamed x256, local copies, waits for them, and re-layouts  31 us
    reduce_scatter x1, waiting for transfers between devices, body(): lax.psum_scatter(jnp.concatenate([key_grad_all[:prompt_count], value_grad...  30 us
    all_gather x1, waiting for transfers between devices, body(): lax.all_gather(jnp.concatenate([key_rot[:PROMPT_DEV], value_low[:PROMPT_D...  23.3 us
    psum x1, blocking collectives, body(): lax.psum(jnp.stack([jnp.sum(query_raw * query_raw, axis=1), jnp.sum(key_r...  13.5 us
  transfers between devices with their start and end apart: 3, of which 3 were waited for; matrix products, arithmetic and copies ran while one was open for 4% of the time, Pallas kernels for 0%

profile of v4, /device:TPU:0, one launch (start us, length us, event | category | flops | bytes accessed | tf_op | source)
XLA Modules:
  0.0 619.1 jit_solution(15656129475814603889)
XLA Ops:
  7.3 1.9 fusion.3
  14.5 13.5 %psum.14 = f32[384,2]{0,1:T(2,128)S(1)} all-reduce(f32[384,2]{0,1:T(2,128)S(1)} %pad_maximum_fusion.13), channel_id=1, replica_groups=mesh['expert'=8,'tensor'=4] {'tensor'}, use_global_device_ids=true, to_apply=%region_3.4 | all-reduce | flops 768 | bytes 6144 | tf_op jit(solution)/shard_map/psum | solution.py:1043
  39.9 23.3 %all-gather.5.cloned.1.call-done = bf16[1024,1024]{1,0:T(8,128)(2,1)} async-done(((bf16[128,1024]{1,0:T(8,128)(2,1)}), bf16[1024,1024]{1,0:T(8,128)(2,1)}) %all-gather.5.cloned.1.call-update) | async-done | bytes 2097168 | tf_op jit(solution)/shard_map/all_gather | solution.py:1062
  73.4 69.6 %shard_map.246 = (bf16[384,2048]{1,0:T(8,128)(2,1)S(1)}, bf16[8,384,2048]{2,1,0:T(8,128)(2,1)}) custom-call(bf16[384,512]{1,0:T(8,128)(2,1)S(1)} %pad_maximum_fusion.6.left.attended, bf16[512,2048]{1,0:T(8,128)(2,1)S(1)} %copy-done.6, bf16[384,2048]{1,0:T(8,128)(2,1)S(1)} %copy-done.2), custom_call_target="tpu_custom_call" | custom-call | tf_op jit(solution)/shard_map/pallas_call | solution.py:606
  144.2 1.9 multiply_convert_fusion
  147.3 8.3 %all-gather.1 = s32[3072,8]{0,1:T(8,128)S(1)} all-gather(s32[384,8]{0,1:T(8,128)S(1)} %copy-done.78), channel_id=3, replica_groups=mesh['expert'=8,'tensor'=4] {'expert'}, dimensions={0}, use_global_device_ids=true | all-gather | bytes 110592 | tf_op jit(solution)/shard_map/all_gather | solution.py:1029
  157.3 2.1 pad.21.router
  165.5 50.6 %all-gather.7.cloned.1.call-done.x_all = bf16[3072,2048]{1,0:T(8,128)(2,1)} async-done(((bf16[384,2048]{1,0:T(8,128)(2,1)}), bf16[3072,2048]{1,0:T(8,128)(2,1)}) %all-gather.7.cloned.1.call-update) | async-done | bytes 12582928 | tf_op jit(solution)/shard_map/all_gather | solution.py:1122
  216.1 128.2 %shard_map.247 = (bf16[384,2176]{1,0:T(8,128)(2,1)}, bf16[8,384,512]{2,1,0:T(8,128)(2,1)}, bf16[8,384,512]{2,1,0:T(8,128)(2,1)}, bf16[8,384,512]{2,1,0:T(8,128)(2,1)}, bf16[8,384,2048]{2,1,0:T(8,128)(2,1)}) custom-call(bf16[8,384,2048]{2,1,0:T(8,128)(2,1)} %bitcast.83, bf16[8,384,2048]{2,1,0:T(8,128)(2,1)} %get-tuple-element.27.g_all, ...), custom_call_target="tpu_custom_call" | custom-call | flops 38654705664 | bytes 50331648 | tf_op jit(solution)/shard_map/pallas_call | solution.py:539
  345.7 4.2 multiply_reduce_fusion
  377.8 2.3 copy.158
  382.4 30.0 %reduce-scatter.2.cloned.1.call-done = bf16[128,1024]{1,0:T(8,128)(2,1)} async-done(((bf16[1024,1024]{1,0:T(8,128)(2,1)}), bf16[128,1024]{1,0:T(8,128)(2,1)}) %reduce-scatter.2.cloned.1.call-update) | async-done | bytes 262160 | tf_op jit(solution)/shard_map/reduce_scatter | solution.py:1212
  415.9 1.8 multiply_add_fusion
  425.0 1.9 copy.140
  427.0 2.0 pad.23.extras
  430.9 12.4 %psum.15 = f32[384,2]{0,1:T(2,128)} all-reduce(f32[384,2]{0,1:T(2,128)} %pad_maximum_fusion.14), channel_id=1, replica_groups=mesh['expert'=8,'tensor'=4] {'tensor'}, use_global_device_ids=true, to_apply=%region_26.27 | all-reduce | flops 768 | bytes 6144 | tf_op jit(solution)/shard_map/psum | solution.py:1238
  448.1 124.8 %shard_map.248 = (bf16[384,2048]{1,0:T(8,128)(2,1)}, f32[256,2176]{1,0:T(8,128)}, bf16[384,2048]{1,0:T(8,128)(2,1)}, f32[2,2048,256]{2,1,0:T(8,128)}, f32[2,2048,256]{2,1,0:T(8,128)}, /*index=5*/f32[2,256,2048]{2,1,0:T(8,128)}) custom-call(bf16[384,2048]{1,0:T(8,128)(2,1)} %copy-done.40, bf16[384,512]{1,0:T(8,128)(2,1)} %subtract_convert_fusion.1.query_grad, ...), custom_call_target="tpu_custom_call" | custom-call | tf_op jit(solution)/shard_map/pallas_call | solution.py:867
  572.9 3.0 slice_bitcast_fusion
  580.4 2.0 copy.141
  583.8 11.8 %all-reduce.4 = bf16[2048]{0:T(1024)(128)(2,1)S(1)} all-reduce(bf16[2048]{0:T(1024)(128)(2,1)S(1)} %get-tuple-element.106), channel_id=5, replica_groups=mesh['expert'=8,'tensor'=4] {'expert'}, use_global_device_ids=true, to_apply=%region_32.33.clone | all-reduce | flops 2048 | bytes 8192
  596.2 6.4 %fusion.2 = (f32[384,2048]{1,0:T(8,128)}, bf16[384,2048]{1,0:T(8,128)(2,1)}) fusion(bf16[384,2048]{1,0:T(8,128)(2,1)} %get-tuple-element.34, bf16[384,2048]{1,0:T(8,128)(2,1)} %param.15, f32[384]{0:T(512)S(1)} %get-tuple-element.107, f32[384]{0:T(512)S(1)} %copy-done.101, f32[2048]{0:T(1024)S(1)} %copy-done.74, f32[384]{0:T(512)S(1)} %copy-done.81, ...), kind=kLoop, calls=%fused_computation.9 | loop fusion | flops 15728640 | bytes 15754240 | tf_op jit(solution)/shard_map/sub | solution.py:1312
  602.7 2.1 copy.191
  606.4 2.1 copy.192
  610.1 2.0 copy.193
  (378 shorter events, 93.7 us)
Async XLA Ops:
  7.2 55.9 %all-gather.5.cloned.1.call-start = ((), (), s32[]{:S(2)}) async-start(), calls=%async_computation.1 | async-start | bytes 2359296 | tf_op jit(solution)/shard_map/all_gather | solution.py:1062
  12.0 17.5 %copy-start.33 = (f32[384,512]{1,0:T(8,128)}, f32[384,512]{1,0:T(8,128)S(1)}, u32[]{:S(2)}) copy-start(f32[384,512]{1,0:T(8,128)S(1)} %get-tuple-element.153) | copy-start | bytes 2359300
  13.4 15.2 %copy-start.118 = (f32[2,512]{1,0:T(2,128)S(1)}, f32[2,512]{1,0:T(2,128)}, u32[]{:S(2)}) copy-start(f32[2,512]{1,0:T(2,128)} %param.22) | copy-start | bytes 12292
  14.4 16.1 %copy-start.35 = (f32[384,512]{1,0:T(8,128)}, f32[384,512]{1,0:T(8,128)S(1)}, u32[]{:S(2)}) copy-start(f32[384,512]{1,0:T(8,128)S(1)} %get-tuple-element.151) | copy-start | bytes 2359300
  36.9 179.3 %all-gather.7.cloned.1.call-start = ((), (), s32[]{:S(2)}) async-start(), calls=%async_computation.3 | async-start | bytes 14155776 | tf_op jit(solution)/shard_map/all_gather | solution.py:1122
  37.5 32.0 %copy-start.37 = (bf16[256,512]{1,0:T(8,128)(2,1)}, bf16[256,512]{1,0:T(8,128)(2,1)S(1)}, u32[]{:S(2)}) copy-start(bf16[256,512]{1,0:T(8,128)(2,1)S(1)} %slice.254) | copy-start | bytes 786436
  38.1 31.9 %copy-start.65 = (bf16[48,8,4,128]{3,1,2,0:T(8,128)(2,1)}, bf16[48,8,4,128]{3,1,2,0:T(8,128)(2,1)S(1)}, u32[]{:S(2)}) copy-start(bf16[48,8,4,128]{3,1,2,0:T(8,128)(2,1)S(1)} %copy.174) | copy-start | bytes 1179652
  73.4 69.6 %copy-start.5 = (bf16[384,512]{1,0:T(8,128)(2,1)}, bf16[384,512]{1,0:T(8,128)(2,1)S(1)}, u32[]{:S(2)}) copy-start(bf16[384,512]{1,0:T(8,128)(2,1)S(1)} %pad_maximum_fusion.6.left.attended) | copy-start | bytes 1179652
  73.4 69.7 %copy-start.9 = (bf16[384,2048]{1,0:T(8,128)(2,1)S(1)}, bf16[384,2048]{1,0:T(8,128)(2,1)}, u32[]{:S(2)}) copy-start(bf16[384,2048]{1,0:T(8,128)(2,1)} %param.15) | copy-start | bytes 4718596
  143.0 206.9 %copy-start = (bf16[384,2048]{1,0:T(8,128)(2,1)}, bf16[384,2048]{1,0:T(8,128)(2,1)S(1)}, u32[]{:S(2)}) copy-start(bf16[384,2048]{1,0:T(8,128)(2,1)S(1)} %get-tuple-element.26) | copy-start | bytes 4718596
  146.2 266.2 %reduce-scatter.2.cloned.1.call-start = ((), (), s32[]{:S(2)}) async-start(), calls=%async_computation.2 | async-start | bytes 2359296 | tf_op jit(solution)/shard_map/reduce_scatter | solution.py:1212
  357.1 10.7 %copy-start.55 = (bf16[1280,128]{1,0:T(8,128)(2,1)}, bf16[1280,128]{1,0:T(8,128)(2,1)S(1)}, u32[]{:S(2)}) copy-start(bf16[1280,128]{1,0:T(8,128)(2,1)S(1)} %fusion.28) | copy-start | bytes 983044
  377.8 35.6 %copy-start.44 = (f32[1280,128]{1,0:T(8,128)S(1)}, f32[1280,128]{1,0:T(8,128)}, u32[]{:S(2)}) copy-start(f32[1280,128]{1,0:T(8,128)} %copy-done.43) | copy-start | bytes 1966084
  377.8 35.6 %copy-start.46 = (f32[1280,128]{1,0:T(8,128)S(1)}, f32[1280,128]{1,0:T(8,128)}, u32[]{:S(2)}) copy-start(f32[1280,128]{1,0:T(8,128)} %copy-done.45) | copy-start | bytes 1966084
  377.8 35.6 %copy-start.48 = (f32[1280,128]{1,0:T(8,128)S(1)}, f32[1280,128]{1,0:T(8,128)}, u32[]{:S(2)}) copy-start(f32[1280,128]{1,0:T(8,128)} %copy-done.47) | copy-start | bytes 1966084
  377.8 35.6 %copy-start.50 = (f32[1280,128]{1,0:T(8,128)S(1)}, f32[1280,128]{1,0:T(8,128)}, u32[]{:S(2)}) copy-start(f32[1280,128]{1,0:T(8,128)} %copy-done.49) | copy-start | bytes 1966084
  419.1 25.0 %copy-start.71 = (bf16[256,512]{1,0:T(8,128)(2,1)S(1)}, bf16[256,512]{1,0:T(8,128)(2,1)}, u32[]{:S(2)}) copy-start(bf16[256,512]{1,0:T(8,128)(2,1)} %maximum_convert_fusion.1) | copy-start | bytes 786436
  579.3 16.9 %copy-start.1 = (bf16[384,2048]{1,0:T(8,128)(2,1)S(1)}, bf16[384,2048]{1,0:T(8,128)(2,1)}, u32[]{:S(2)}) copy-start(bf16[384,2048]{1,0:T(8,128)(2,1)} %copy-done) | copy-start | bytes 4718596
  579.3 16.9 %copy-start.4 = (bf16[384,2048]{1,0:T(8,128)(2,1)S(1)}, bf16[384,2048]{1,0:T(8,128)(2,1)}, u32[]{:S(2)}) copy-start(bf16[384,2048]{1,0:T(8,128)(2,1)} %spread.1) | copy-start | bytes 4718596
  579.3 16.8 %copy-start.77 = (f32[2048]{0:T(1024)S(1)}, f32[2048]{0:T(1024)}, u32[]{:S(2)}) copy-start(f32[2048]{0:T(1024)} %param.21) | copy-start | bytes 24580
  579.4 16.8 %copy-start.95 = (f32[384]{0:T(512)S(1)}, f32[384]{0:T(512)}, u32[]{:S(2)}) copy-start(f32[384]{0:T(512)} %copy-done.93) | copy-start | bytes 4612
  579.4 16.8 %copy-start.99 = (f32[384]{0:T(512)S(1)}, f32[384]{0:T(512)}, u32[]{:S(2)}) copy-start(f32[384]{0:T(512)} %get-tuple-element.148) | copy-start | bytes 4612
  579.4 16.8 %copy-start.101 = (f32[384]{0:T(512)S(1)}, f32[384]{0:T(512)}, u32[]{:S(2)}) copy-start(f32[384]{0:T(512)} %get-tuple-element.146) | copy-start | bytes 4612
  579.4 16.8 %copy-start.117 = (f32[384]{0:T(512)S(1)}, f32[384]{0:T(512)}, u32[]{:S(2)}) copy-start(f32[384]{0:T(512)} %copy-done.116) | copy-start | bytes 4612
  (100 other events, 245.9 us)
Sparse Core Ops, SparseCore 0:
  37.0 26.0 all-gather.4
  146.3 69.7 all-gather.6
  370.4 41.9 reduce-scatter.1

commit v5 on v4

--- a/solution.py
+++ b/solution.py
@@ -9,6 +9,10 @@
 PROMPT_DEV = 128
 CLEN = 256
 CONT_DEV = 1
+
+
+epsilon = 1e-05
+masked_value = -1e30
 
 
 MESH = pl.DeviceIdType.MESH
@@ -351,12 +355,15 @@
             self.pair_sems.at[0, kind, piece], self.pair_sems.at[1, kind, piece], expert=self.place.sibling,
         )
 
+    def start_piece(self, piece):
+        self.x_copy(piece).start()
+        self.y_copy(piece).start()
+        self.pair_copy(3, piece).start()
+
     def start(self):
+        self.own_copy().start()
         for piece in range(self.pieces):
-            self.x_copy(piece).start()
-            self.y_copy(piece).start()
-            self.pair_copy(3, piece).start()
-        self.own_copy().start()
+            self.start_piece(piece)
 
     def near(self, piece):
         self.x_copy(piece).wait_recv()
@@ -375,8 +382,7 @@
     def paired(self, kind, piece):
         self.pair_copy(kind, piece).wait_recv()
 
-    def finish_sends(self):
-        self.own_copy().wait()
+    def finish(self):
         for piece in range(self.pieces):
             self.x_copy(piece).wait_send()
             self.y_copy(piece).wait_send()
@@ -568,59 +574,7 @@
     )(arrived, arrived_grad, mask, router, bias, w_gate, w_up, w_down)
 
 
-def product_kernel(left, right, spread, total, gathered, own, arrived, sems, *gather_sems):
-    line = Line(own, arrived, total, sems)
-    place = Place()
-    gather = Gather(spread, gathered, place, *gather_sems, pieces=GATHER_PIECES)
-    greet(place.neighbours() + line.neighbours())
-    gather.start()
-    width = right.shape[1]
-    tile = min(512, width)
-    for start in range(0, width, tile):
-        columns = slice(start, start + tile)
-        own[:, columns] = wide_dot(left[...], right[:, columns]).astype(jnp.bfloat16)
-    steps = line.pieces + 2 * (line.size - 1)
-    done = 0
-    for piece in range(GATHER_PIECES):
-        upto = steps * (piece + 1) * 2 // (3 * GATHER_PIECES)
-        lax.fori_loop(done, upto, line.step_body, 0)
-        done = upto
-        gather.near(piece)
-    lax.fori_loop(done, steps, line.step_body, 0)
-    for piece in range(GATHER_PIECES):
-        gather.far(piece)
-    for kind in range(4):
-        for piece in range(GATHER_PIECES):
-            gather.paired(kind, piece)
-    gather.finish_sends()
-    line.finish()
-
-
 GATHER_PIECES = 4
-
-
-def summed_product(left, right, spread, collective_id):
-    rows, width = left.shape[0], right.shape[1]
-    vmem = pl.BlockSpec(memory_space=pltpu.VMEM)
-    any_space = pl.BlockSpec(memory_space=pl.ANY)
-    return pl.pallas_call(
-        product_kernel,
-        out_shape=(
-            jax.ShapeDtypeStruct((rows, width), jnp.bfloat16),
-            jax.ShapeDtypeStruct((lax.axis_size("expert"),) + spread.shape, spread.dtype),
-        ),
-        in_specs=[vmem, vmem, any_space],
-        out_specs=(vmem, any_space),
-        scratch_shapes=[
-            pltpu.VMEM((rows, width), jnp.bfloat16),
-            pltpu.VMEM((rows, width), jnp.bfloat16),
-            Line.semaphores(rows),
-            *Gather.semaphores(GATHER_PIECES),
-        ],
-        compiler_params=pltpu.CompilerParams(
-            collective_id=collective_id, has_side_effects=True, vmem_limit_bytes=40 * 2**20
-        ),
-    )(left, right, spread)
 
 
 def crossed_dot(left, right):
@@ -912,8 +866,332 @@
     )
 
 
-epsilon = 1e-05
-masked_value = -1e30
+class Peers:
+    def __init__(self, mine, theirs, sent, got):
+        self.mine, self.theirs, self.sent, self.got = mine, theirs, sent, got
+        self.size = lax.axis_size("tensor")
+        self.here = lax.axis_index("tensor")
+
+    def neighbours(self):
+        return [(None, {"tensor": (self.here + d) % self.size}) for d in range(1, self.size)]
+
+    def copies(self):
+        return [
+            remote(
+                self.mine, self.theirs.at[d - 1], self.sent.at[d - 1], self.got.at[d - 1],
+                tensor=(self.here + d) % self.size,
+            )
+            for d in range(1, self.size)
+        ]
+
+    def start(self):
+        for copy in self.copies():
+            copy.start()
+
+    def total(self):
+        result = self.mine[...]
+        for d, copy in enumerate(self.copies()):
+            copy.wait_recv()
+            result = result + self.theirs[d]
+        return result
+
+    def finish(self):
+        for copy in self.copies():
+            copy.wait_send()
+
+
+def to_rows(columns, rows):
+    lane = lax.broadcasted_iota(jnp.int32, (rows, LANE), 1)
+    field = jnp.zeros((rows, LANE), jnp.float32)
+    for i, column in enumerate(columns):
+        field = jnp.where(lane == i, column, field)
+    return field.T[:8]
+
+
+def to_columns(sums):
+    padded = jnp.concatenate([sums, jnp.zeros((LANE - 8, sums.shape[1]), jnp.float32)], axis=0)
+    return padded.T
+
+
+def swapped(field):
+    half = HD // 2
+    return jnp.concatenate([field[:, half:], field[:, :half]], axis=1)
+
+
+def front_kernel(
+    tokens, attn_gain, ffn_gain, w_query, w_key, w_value, w_out, qk_gain, cosine, sine, bias, routes, cotangent,
+    total, normed, normed_two, attended, query_rot, keys_values, query_raw, key_raw, stats, routes_all, spread_all,
+    line_own, line_in, prompt, mine, theirs,
+    line_sems, peer_sent, peer_got, *gather_sems,
+):
+    rows, width = tokens.shape
+    local = w_query.shape[1]
+    heads = local // HD
+    factor = HD ** (-0.5)
+    own_blocks = rows // PROMPT_DEV - 1
+    devices = keys_values.shape[0] - own_blocks
+    place = Place()
+    line = Line(line_own, line_in, total, line_sems)
+    peers = Peers(mine, theirs, peer_sent, peer_got)
+    spread = Gather(cotangent, spread_all, place, *gather_sems[0:5], pieces=GATHER_PIECES)
+    names = Gather(routes, routes_all, place, *gather_sems[5:10], pieces=2)
+    prompts = Gather(prompt, keys_values, place, *gather_sems[10:15], pieces=2)
+    greet(place.neighbours() + peers.neighbours())
+    names.start()
+    spread.own_copy().start()
+    spread.start_piece(0)
+    source = tokens[...].astype(jnp.float32)
+    scale_one = lax.rsqrt(jnp.sum(source * source, axis=1, keepdims=True) / width + epsilon)
+    normed[...] = (source * scale_one * attn_gain[...]).astype(jnp.bfloat16)
+    query_raw[...] = wide_dot(normed[...], w_query[...])
+    key_raw[...] = wide_dot(normed[...], w_key[...])
+    mine[...] = to_rows(
+        [
+            jnp.sum(query_raw[...] * query_raw[...], axis=1, keepdims=True),
+            jnp.sum(key_raw[...] * key_raw[...], axis=1, keepdims=True),
+        ],
+        rows,
+    )
+    peers.start()
+    value = wide_dot(normed[...], w_value[...]).astype(jnp.bfloat16)
+    prompt[:, local:] = value[:PROMPT_DEV]
+    for i in range(own_blocks):
+        keys_values[devices + i, :, local:] = value[(i + 1) * PROMPT_DEV : (i + 2) * PROMPT_DEV]
+    squares = to_columns(peers.total())
+    scale_query = lax.rsqrt(squares[:, 0:1] / width + epsilon)
+    scale_key = lax.rsqrt(squares[:, 1:2] / width + epsilon)
+    for head in range(heads):
+        columns = slice(head * HD, (head + 1) * HD)
+        turned = key_raw[:, columns] * scale_key * qk_gain[1:2, columns]
+        turned = (turned * cosine[...] + swapped(turned) * sine[...]).astype(jnp.bfloat16)
+        prompt[:, columns] = turned[:PROMPT_DEV]
+        for i in range(own_blocks):
+            keys_values[devices + i, :, columns] = turned[(i + 1) * PROMPT_DEV : (i + 2) * PROMPT_DEV]
+    prompts.own_copy().start()
+    for piece in range(2):
+        prompts.start_piece(piece)
+    for piece in range(1, GATHER_PIECES):
+        spread.start_piece(piece)
+    for head in range(heads):
+        columns = slice(head * HD, (head + 1) * HD)
+        turned = query_raw[:, columns] * scale_query * qk_gain[0:1, columns]
+        turned = turned * cosine[...] + swapped(turned) * sine[...]
+        query_rot[:, columns] = turned.astype(jnp.bfloat16)
+    for piece in range(2):
+        prompts.near(piece)
+    for piece in range(2):
+        names.near(piece)
+    for piece in range(2):
+        prompts.far(piece)
+        names.far(piece)
+    prompts.own_copy().wait()
+    for kind in range(4):
+        for piece in range(2):
+            prompts.paired(kind, piece)
+            names.paired(kind, piece)
+    lane = lax.broadcasted_iota(jnp.int32, (rows, LANE), 1)
+    kept = jnp.where(lane == 0, scale_one, 0.0)
+    kept = jnp.where(lane == 1, scale_query, kept)
+    kept = jnp.where(lane == 2, scale_key, kept)
+    count = keys_values.shape[0] * PROMPT_DEV
+    for head in range(heads):
+        columns = slice(head * HD, (head + 1) * HD)
+        keys = keys_values[:, :, columns].reshape(count, HD)
+        values = keys_values[:, :, local + head * HD : local + (head + 1) * HD].reshape(count, HD)
+        scores = turned_dot(query_rot[:, columns], keys) * factor + bias[...]
+        top = jnp.max(scores, axis=1, keepdims=True)
+        weights = jnp.exp(scores - top)
+        whole = jnp.sum(weights, axis=1, keepdims=True)
+        shares = (weights / whole).astype(jnp.bfloat16)
+        attended[:, columns] = wide_dot(shares, values).astype(jnp.bfloat16)
+        kept = jnp.where(lane == 8 + head, top + jnp.log(whole), kept)
+    tile = min(512, width)
+    for start in range(0, width, tile):
+        columns = slice(start, start + tile)
+        line_own[:, columns] = wide_dot(attended[...], w_out[:, columns]).astype(jnp.bfloat16)
+    steps = line.pieces + 2 * (line.size - 1)
+    done = 0
+    for piece in range(GATHER_PIECES):
+        upto = steps * (piece + 1) // (2 * GATHER_PIECES)
+        lax.fori_loop(done, upto, line.step_body, 0)
+        done = upto
+        spread.near(piece)
+    for piece in range(GATHER_PIECES):
+        upto = done + (steps - done) * (piece + 1) // GATHER_PIECES
+        lax.fori_loop(done, upto, line.step_body, 0)
+        done = upto
+        spread.far(piece)
+    hidden = tokens[...].astype(jnp.float32) + total[...].astype(jnp.float32)
+    scale_two = lax.rsqrt(jnp.sum(hidden * hidden, axis=1, keepdims=True) / width + epsilon)
+    normed_two[...] = (hidden * scale_two * ffn_gain[...]).astype(jnp.bfloat16)
+    stats[...] = jnp.where(lane == 3, scale_two, kept)
+    for kind in range(4):
+        for piece in range(GATHER_PIECES):
+            spread.paired(kind, piece)
+    names.own_copy().wait()
+    spread.own_copy().wait()
+    for each in (names, prompts, spread, line, peers):
+        each.finish()
+
+
+def front(tokens, attn_gain, ffn_gain, w_query, w_key, w_value, w_out, qk_gain, cosine, sine, bias, routes, cotangent):
+    rows, width = tokens.shape
+    local = w_query.shape[1]
+    ranks = lax.axis_size("expert")
+    size = lax.axis_size("tensor")
+    low, full = jnp.bfloat16, jnp.float32
+    vmem = pl.BlockSpec(memory_space=pltpu.VMEM)
+    any_space = pl.BlockSpec(memory_space=pl.ANY)
+    blocks = ranks + rows // PROMPT_DEV - 1
+    return pl.pallas_call(
+        front_kernel,
+        out_shape=(
+            jax.ShapeDtypeStruct((rows, width), low),
+            jax.ShapeDtypeStruct((rows, width), low),
+            jax.ShapeDtypeStruct((rows, width), low),
+            jax.ShapeDtypeStruct((rows, local), low),
+            jax.ShapeDtypeStruct((rows, local), low),
+            jax.ShapeDtypeStruct((blocks, PROMPT_DEV, 2 * local), low),
+            jax.ShapeDtypeStruct((rows, local), full),
+            jax.ShapeDtypeStruct((rows, local), full),
+            jax.ShapeDtypeStruct((rows, LANE), full),
+            jax.ShapeDtypeStruct((ranks,) + routes.shape, jnp.int32),
+            jax.ShapeDtypeStruct((ranks, rows, width), low),
+        ),
+        in_specs=[vmem] * 12 + [any_space],
+        out_specs=(vmem,) * 10 + (any_space,),
+        scratch_shapes=[
+            pltpu.VMEM((rows, width), low),
+            pltpu.VMEM((rows, width), low),
+            pltpu.VMEM((PROMPT_DEV, 2 * local), low),
+            pltpu.VMEM((8, rows), full),
+            pltpu.VMEM((size - 1, 8, rows), full),
+            Line.semaphores(rows),
+            pltpu.SemaphoreType.DMA((size - 1,)),
+            pltpu.SemaphoreType.DMA((size - 1,)),
+            *Gather.semaphores(GATHER_PIECES),
+            *Gather.semaphores(2),
+            *Gather.semaphores(2),
+        ],
+        compiler_params=pltpu.CompilerParams(
+            collective_id=1, has_side_effects=True, vmem_limit_bytes=60 * 2**20
+        ),
+    )(tokens, attn_gain, ffn_gain, w_query, w_key, w_value, w_out, qk_gain, cosine, sine, bias, routes, cotangent)
+
+
+def backward_kernel(
+    attention_grad, w_out, query_rot, keys_values, bias, stats, query_raw, key_raw, cosine, sine, qk_gain,
+    query_out, key_out, value_out, gain_out,
+    out_grad, query_grad, prompt_grads, own_grads, own, paired, from_x, from_y, mine, theirs,
+    pair_sems, x_sems, y_sems, peer_sent, peer_got,
+):
+    rows, local = query_rot.shape
+    width = attention_grad.shape[1]
+    heads = local // HD
+    factor = HD ** (-0.5)
+    own_blocks = rows // PROMPT_DEV - 1
+    devices = keys_values.shape[0] - own_blocks
+    count = keys_values.shape[0] * PROMPT_DEV
+    reach = devices * PROMPT_DEV
+    plane = Plane(own, prompt_grads, paired, from_x, from_y, pair_sems, x_sems, y_sems, by_device=True)
+    peers = Peers(mine, theirs, peer_sent, peer_got)
+    greet(plane.neighbours() + peers.neighbours())
+    out_grad[...] = turned_dot(attention_grad[...], w_out[...]).astype(jnp.bfloat16)
+    for head in range(heads):
+        columns = slice(head * HD, (head + 1) * HD)
+        other = slice(local + head * HD, local + (head + 1) * HD)
+        keys = keys_values[:, :, columns].reshape(count, HD)
+        values = keys_values[:, :, other].reshape(count, HD)
+        query, above = query_rot[:, columns], out_grad[:, columns]
+        scores = turned_dot(query, keys) * factor + bias[...]
+        shares = jnp.exp(scores - stats[:, 8 + head : 9 + head])
+        share_grad = turned_dot(above, values)
+        delta = jnp.sum(shares * share_grad, axis=1, keepdims=True)
+        score_grad = (shares * (share_grad - delta)).astype(jnp.bfloat16)
+        query_grad[:, columns] = wide_dot(score_grad, keys) * factor
+        key_grad = crossed_dot(score_grad, query) * factor
+        value_grad = crossed_dot(shares.astype(jnp.bfloat16), above)
+        prompt_grads[:, :, columns] = key_grad[:reach].astype(jnp.bfloat16).reshape(devices, PROMPT_DEV, HD)
+        prompt_grads[:, :, other] = value_grad[:reach].astype(jnp.bfloat16).reshape(devices, PROMPT_DEV, HD)
+        own_grads[PROMPT_DEV:, columns] = key_grad[reach:]
+        own_grads[PROMPT_DEV:, other] = value_grad[reach:]
+    for chip in range(4):
+        plane.pair_copy(chip).start()
+    for chip in range(4):
+        own[chip] = prompt_grads[plane.block(chip, plane.core)]
+    for chip in range(4):
+        plane.pair_copy(chip).wait_recv()
+        if chip < 3:
+            plane.send_first(chip)
+
+    def normed_part(source, raw, row, scale):
+        inner = jnp.zeros((rows, 1), jnp.float32)
+        for head in range(heads):
+            columns = slice(head * HD, (head + 1) * HD)
+            grad = source[:, columns]
+            grad = grad * cosine[...] - swapped(grad) * sine[...]
+            gain_out[row : row + 1, columns] = jnp.sum(grad * raw[:, columns] * scale, axis=0, keepdims=True)
+            grad = qk_gain[row : row + 1, columns] * grad
+            source[:, columns] = grad
+            inner = inner + jnp.sum(grad * raw[:, columns], axis=1, keepdims=True)
+        return inner
+
+    scale_query, scale_key = stats[:, 1:2], stats[:, 2:3]
+    query_inner = normed_part(query_grad, query_raw, 0, scale_query)
+    plane.send_second()
+
+    def last(piece, carry):
+        for side, summed in enumerate(plane.last_sum(piece)):
+            own_grads[plane.rows(side, piece)] = summed
+        return carry
+
+    lax.fori_loop(0, plane.pieces, last, 0)
+    key_inner = normed_part(own_grads, key_raw, 1, scale_key)
+    mine[...] = to_rows([query_inner, key_inner], rows)
+    peers.start()
+    value_out[...] = own_grads[:, local:].astype(jnp.bfloat16)
+    inner = to_columns(peers.total())
+    for out, source, raw, scale, i in (
+        (query_out, query_grad, query_raw, scale_query, 0),
+        (key_out, own_grads, key_raw, scale_key, 1),
+    ):
+        pull = scale * scale * scale / width * inner[:, i : i + 1]
+        out[...] = (scale * source[:, :local] - raw[...] * pull).astype(jnp.bfloat16)
+    plane.finish()
+    peers.finish()
+
+
+def backward(attention_grad, w_out, query_rot, keys_values, bias, stats, query_raw, key_raw, cosine, sine, qk_gain):
+    rows, local = query_rot.shape
+    size = lax.axis_size("tensor")
+    ranks = lax.axis_size("expert")
+    low, full = jnp.bfloat16, jnp.float32
+    vmem = pl.BlockSpec(memory_space=pltpu.VMEM)
+    small = jax.ShapeDtypeStruct((rows, local), low)
+    return pl.pallas_call(
+        backward_kernel,
+        out_shape=(small, small, small, jax.ShapeDtypeStruct((2, local), full)),
+        in_specs=[vmem] * 11,
+        out_specs=(vmem,) * 4,
+        scratch_shapes=[
+            pltpu.VMEM((rows, local), low),
+            pltpu.VMEM((rows, local), full),
+            pltpu.VMEM((ranks, PROMPT_DEV, 2 * local), low),
+            pltpu.VMEM((rows, 2 * local), full),
+            pltpu.VMEM((4, PROMPT_DEV, 2 * local), low),
+            pltpu.VMEM((4, PROMPT_DEV, 2 * local), low),
+            pltpu.VMEM((3, PROMPT_DEV // 2, 2 * local), low),
+            pltpu.VMEM((3, PROMPT_DEV // 2, 2 * local), low),
+            pltpu.VMEM((8, rows), full),
+            pltpu.VMEM((size - 1, 8, rows), full),
+            *Plane.semaphores(PROMPT_DEV),
+            pltpu.SemaphoreType.DMA((size - 1,)),
+            pltpu.SemaphoreType.DMA((size - 1,)),
+        ],
+        compiler_params=pltpu.CompilerParams(
+            collective_id=3, has_side_effects=True, vmem_limit_bytes=60 * 2**20
+        ),
+    )(attention_grad, w_out, query_rot, keys_values, bias, stats, query_raw, key_raw, cosine, sine, qk_gain)
 
 
 def rotate(field, cosine, sine):
@@ -1003,7 +1281,6 @@
     ranks = lax.axis_size("expert")
     device = lax.axis_index("expert")
     span = ranks // 2
-    compact = ranks == 8
     prompt_len = PROMPT_DEV * span
     factor = HD ** (-0.5)
     local = jnp.arange(rows, dtype=jnp.int32)
@@ -1025,15 +1302,6 @@
     angle = position.astype(jnp.float32)[:, None] * frequency[None, :]
     cosine = jnp.cos(angle)[:, None, :]
     sine = jnp.sin(angle)[:, None, :]
-    if compact:
-        routes_all = lax.all_gather(routes, "expert", axis=0)
-        own_expert = device * local_experts + jnp.arange(local_experts, dtype=jnp.int32)
-        expert_mask = jnp.any(routes_all[:, :, :, None] == own_expert, axis=2).astype(jnp.float32)
-        expert_mask = jnp.pad(expert_mask, ((0, 0), (0, 0), (0, LANE - local_experts)))
-        own_first = jnp.roll(router, -device * local_experts, axis=1)
-        own_first = jnp.pad(own_first, ((0, 0), (0, LANE - experts_total)))
-        bias = jnp.where(jnp.arange(LANE) < experts_total, 0.0, masked_value)
-        bias = bias.astype(jnp.float32)[None]
     source = tokens.astype(jnp.float32)
     scale_one = lax.rsqrt(jnp.mean(source * source, axis=1, keepdims=True) + epsilon)
     normed = (source * scale_one * attn_gain).astype(jnp.bfloat16)
@@ -1059,13 +1327,10 @@
         .astype(jnp.bfloat16)
     )
     value_low = value_raw.astype(jnp.bfloat16)
-    prompts = lax.all_gather(
-        jnp.concatenate([key_rot[:PROMPT_DEV], value_low[:PROMPT_DEV]], axis=1),
-        "expert",
-        axis=0,
-        tiled=True,
-    )
-    prompt_keys, prompt_values = prompts[:, :local_width], prompts[:, local_width:]
+    prompt_keys, prompt_values = (
+        lax.all_gather(key_rot[:PROMPT_DEV], "expert", axis=0, tiled=True),
+        lax.all_gather(value_low[:PROMPT_DEV], "expert", axis=0, tiled=True),
+    )
     prompt_count = prompt_keys.shape[0]
     all_keys = jnp.concatenate([prompt_keys, key_rot[PROMPT_DEV:]], axis=0)
     all_values = jnp.concatenate([prompt_values, value_low[PROMPT_DEV:]], axis=0)
@@ -1099,13 +1364,7 @@
         )
         log_totals.append(top + jnp.log(total))
     attended = jnp.concatenate(outputs, axis=1).astype(jnp.bfloat16)
-    if compact:
-        attention, arrived_grad = summed_product(attended, w_out, cotangent, 1)
-        attention = attention.astype(jnp.float32)
-    else:
-        attention = lax.psum(
-            jnp.dot(attended, w_out, preferred_element_type=jnp.float32), "tensor"
-        )
+    attention = lax.psum(jnp.dot(attended, w_out, preferred_element_type=jnp.float32), "tensor")
     hidden = source + attention
     scale_two = lax.rsqrt(jnp.mean(hidden * hidden, axis=1, keepdims=True) + epsilon)
     normed_two = (hidden * scale_two * ffn_gain).astype(jnp.bfloat16)
@@ -1117,46 +1376,39 @@
         jnp.float32
     )
     rows_mask = jnp.sum(hits, axis=1)
+    routed = lax.all_gather(
+        (rows_mask * chances).astype(jnp.float32), "expert", axis=0, tiled=True
+    )
+    gates = lax.dynamic_slice_in_dim(routed, device * local_experts, local_experts, 1).T
     grad_out = cotangent.astype(jnp.float32)
-    if compact:
-        arrived = lax.all_gather(normed_two, "expert", axis=0)
-        reduced, gated, gate_grad, up_grad, mixed_part = experts_fused(
-            arrived, arrived_grad, expert_mask, own_first, bias, w_gate, w_up, w_down
-        )
-        moe_input_grad = reduced[:, :width].astype(jnp.float32)
-        chance_grad = reduced[:, width : width + experts_total].astype(jnp.float32)
-    else:
-        routed = lax.all_gather(
-            (rows_mask * chances).astype(jnp.float32), "expert", axis=0, tiled=True
-        )
-        gates = lax.dynamic_slice_in_dim(routed, device * local_experts, local_experts, 1).T
-        pieces = max(1, ranks * rows // 4096)
-        piece = rows // pieces
-        split_gates = gates.reshape(local_experts, ranks, rows)
-        results = []
-        weight_grads = None
-        for number in range(pieces):
-            part = slice(number * piece, (number + 1) * piece)
-            sources = (normed_two[part], cotangent[part])
-            if results:
-                sources, results, weight_grads = lax.optimization_barrier(
-                    (sources, results, weight_grads)
-                )
-            *result, grads = experts(
-                *sources,
-                split_gates[:, :, part].reshape(local_experts, ranks * piece),
-                w_gate,
-                w_up,
-                w_down,
-                experts_total,
+    pieces = max(1, ranks * rows // 4096)
+    piece = rows // pieces
+    split_gates = gates.reshape(local_experts, ranks, rows)
+    results = []
+    weight_grads = None
+    for number in range(pieces):
+        part = slice(number * piece, (number + 1) * piece)
+        sources = (normed_two[part], cotangent[part])
+        if results:
+            sources, results, weight_grads = lax.optimization_barrier(
+                (sources, results, weight_grads)
             )
-            results.append(result)
-            weight_grads = grads if weight_grads is None else [a + b for a, b in zip(weight_grads, grads)]
-        mixture, moe_input_grad, chance_grad = (
-            jnp.concatenate(list(group_of), axis=0) for group_of in zip(*results)
-        )
-        grad_w_gate, grad_w_up, grad_w_down = weight_grads
+        *result, grads = experts(
+            *sources,
+            split_gates[:, :, part].reshape(local_experts, ranks * piece),
+            w_gate,
+            w_up,
+            w_down,
+            experts_total,
+        )
+        results.append(result)
+        weight_grads = grads if weight_grads is None else [a + b for a, b in zip(weight_grads, grads)]
+    mixture, moe_input_grad, chance_grad = (
+        jnp.concatenate(list(group_of), axis=0) for group_of in zip(*results)
+    )
+    grad_w_gate, grad_w_up, grad_w_down = weight_grads
     chance_grad = rows_mask * chance_grad
+    output = (hidden + mixture).astype(jnp.bfloat16)
     logit_grad = (
         chances * (chance_grad - jnp.sum(chances * chance_grad, axis=1, keepdims=True))
     ).astype(jnp.bfloat16)
@@ -1174,6 +1426,9 @@
         - hidden * (scale_two**3 / width) * jnp.sum(weighted_two * hidden, axis=1, keepdims=True)
     )
     attention_grad = hidden_grad.astype(jnp.bfloat16)
+    grad_w_out = jnp.einsum(
+        "td,te->de", attended, attention_grad, preferred_element_type=jnp.float32
+    )
     attended_grad = jnp.einsum(
         "te,de->td", attention_grad, w_out, preferred_element_type=jnp.float32
     ).astype(jnp.bfloat16)
@@ -1209,15 +1464,20 @@
         )
     key_grad_all = jnp.concatenate(key_grads, axis=1)
     value_grad_all = jnp.concatenate(value_grads, axis=1)
-    prompt_grads = lax.psum_scatter(
-        jnp.concatenate(
-            [key_grad_all[:prompt_count], value_grad_all[:prompt_count]], axis=1
-        ).astype(jnp.bfloat16),
-        "expert",
-        scatter_dimension=0,
-        tiled=True,
-    ).astype(jnp.float32)
-    prompt_key_grad, prompt_value_grad = prompt_grads[:, :local_width], prompt_grads[:, local_width:]
+    prompt_key_grad, prompt_value_grad = (
+        lax.psum_scatter(
+            key_grad_all[:prompt_count].astype(jnp.bfloat16),
+            "expert",
+            scatter_dimension=0,
+            tiled=True,
+        ).astype(jnp.float32),
+        lax.psum_scatter(
+            value_grad_all[:prompt_count].astype(jnp.bfloat16),
+            "expert",
+            scatter_dimension=0,
+            tiled=True,
+        ).astype(jnp.float32),
+    )
     key_grad = jnp.concatenate([prompt_key_grad, key_grad_all[prompt_count:]], axis=0)
     value_grad = jnp.concatenate([prompt_value_grad, value_grad_all[prompt_count:]], axis=0)
     query_grad = unrotate(
@@ -1249,63 +1509,23 @@
         scale_key * weighted_key - key_raw * (scale_key**3 / width) * inner_sums[:, 1:2]
     ).astype(jnp.bfloat16)
     value_raw_grad = value_grad.astype(jnp.bfloat16)
-    if compact:
-        small_part = local_width // ranks
-        gains = jnp.pad(
-            grad_qk_gain.reshape(2, ranks, small_part).transpose(1, 2, 0),
-            ((0, 0), (0, width // ranks - small_part), (0, 0)),
-        )
-        extras = jnp.concatenate(
-            [
-                grad_router.reshape(ranks, width // ranks, experts_total),
-                grad_ffn_gain.reshape(ranks, width // ranks, 1),
-                gains,
-            ],
-            axis=2,
-        ).astype(jnp.bfloat16)
-        extras = jnp.pad(extras, ((0, 0), (0, 0), (0, LANE - experts_total - 3)))
-        normed_grad, sums, mixture, grad_w_gate, grad_w_up, grad_w_down = closing(
-            normed,
-            query_raw_grad,
-            key_raw_grad,
-            value_raw_grad,
-            attended,
-            attention_grad,
-            extras,
-            w_query,
-            w_key,
-            w_value,
-            mixed_part,
-            arrived,
-            arrived_grad,
-            gated,
-            gate_grad,
-            up_grad,
-            local_experts,
-        )
-        mixture = mixture.astype(jnp.float32)
-        normed_grad = normed_grad.astype(jnp.float32)
-    else:
-        grad_w_out = jnp.einsum(
-            "td,te->de", attended, attention_grad, preferred_element_type=jnp.float32
-        )
-        grad_w_query = jnp.einsum(
-            "td,te->de", normed, query_raw_grad, preferred_element_type=jnp.float32
-        )
-        grad_w_key = jnp.einsum("td,te->de", normed, key_raw_grad, preferred_element_type=jnp.float32)
-        grad_w_value = jnp.einsum(
-            "td,te->de", normed, value_raw_grad, preferred_element_type=jnp.float32
-        )
-        normed_part = jnp.einsum(
-            "te,de->td", query_raw_grad, w_query, preferred_element_type=jnp.float32
-        )
-        normed_part = normed_part + jnp.einsum(
-            "te,de->td", key_raw_grad, w_key, preferred_element_type=jnp.float32
-        )
-        normed_part = normed_part + jnp.einsum(
-            "te,de->td", value_raw_grad, w_value, preferred_element_type=jnp.float32
-        )
-        normed_grad = lax.psum(normed_part.astype(jnp.bfloat16), "tensor").astype(jnp.float32)
+    grad_w_query = jnp.einsum(
+        "td,te->de", normed, query_raw_grad, preferred_element_type=jnp.float32
+    )
+    grad_w_key = jnp.einsum("td,te->de", normed, key_raw_grad, preferred_element_type=jnp.float32)
+    grad_w_value = jnp.einsum(
+        "td,te->de", normed, value_raw_grad, preferred_element_type=jnp.float32
+    )
+    normed_part = jnp.einsum(
+        "te,de->td", query_raw_grad, w_query, preferred_element_type=jnp.float32
+    )
+    normed_part = normed_part + jnp.einsum(
+        "te,de->td", key_raw_grad, w_key, preferred_element_type=jnp.float32
+    )
+    normed_part = normed_part + jnp.einsum(
+        "te,de->td", value_raw_grad, w_value, preferred_element_type=jnp.float32
+    )
+    normed_grad = lax.psum(normed_part.astype(jnp.bfloat16), "tensor").astype(jnp.float32)
     weighted_one = attn_gain * normed_grad
     grad_attn_gain = jnp.sum(normed_grad * source * scale_one, axis=0)
     input_grad = (
@@ -1313,48 +1533,32 @@
         + scale_one * weighted_one
         - source * (scale_one**3 / width) * jnp.sum(weighted_one * source, axis=1, keepdims=True)
     )
-    if compact:
-        edge = 4 * local_width
-        summed = (
-            sums[:, :local_width],
-            sums[:, local_width : 2 * local_width],
-            sums[:, 2 * local_width : 3 * local_width],
-            sums[:, 3 * local_width : edge].T,
-            lax.psum_scatter(
-                grad_attn_gain.astype(jnp.bfloat16), "expert", scatter_dimension=0, tiled=True
-            ).astype(jnp.float32),
-            sums[:, edge + experts_total],
-            sums[:small_part, edge + experts_total + 1 : edge + experts_total + 3].T,
-            sums[:, edge : edge + experts_total],
-        )
-    else:
-        summed = (
-            lax.psum_scatter(
-                grad_w_query.astype(jnp.bfloat16), "expert", scatter_dimension=0, tiled=True
-            ).astype(jnp.float32),
-            lax.psum_scatter(
-                grad_w_key.astype(jnp.bfloat16), "expert", scatter_dimension=0, tiled=True
-            ).astype(jnp.float32),
-            lax.psum_scatter(
-                grad_w_value.astype(jnp.bfloat16), "expert", scatter_dimension=0, tiled=True
-            ).astype(jnp.float32),
-            lax.psum_scatter(
-                grad_w_out.astype(jnp.bfloat16), "expert", scatter_dimension=1, tiled=True
-            ).astype(jnp.float32),
-            lax.psum_scatter(
-                grad_attn_gain.astype(jnp.bfloat16), "expert", scatter_dimension=0, tiled=True
-            ).astype(jnp.float32),
-            lax.psum_scatter(
-                grad_ffn_gain.astype(jnp.bfloat16), "expert", scatter_dimension=0, tiled=True
-            ).astype(jnp.float32),
-            lax.psum_scatter(
-                grad_qk_gain.astype(jnp.bfloat16), "expert", scatter_dimension=1, tiled=True
-            ).astype(jnp.float32),
-            lax.psum_scatter(
-                grad_router.astype(jnp.bfloat16), "expert", scatter_dimension=0, tiled=True
-            ).astype(jnp.float32),
-        )
-    output = (hidden + mixture).astype(jnp.bfloat16)
+    summed = (
+        lax.psum_scatter(
+            grad_w_query.astype(jnp.bfloat16), "expert", scatter_dimension=0, tiled=True
+        ).astype(jnp.float32),
+        lax.psum_scatter(
+            grad_w_key.astype(jnp.bfloat16), "expert", scatter_dimension=0, tiled=True
+        ).astype(jnp.float32),
+        lax.psum_scatter(
+            grad_w_value.astype(jnp.bfloat16), "expert", scatter_dimension=0, tiled=True
+        ).astype(jnp.float32),
+        lax.psum_scatter(
+            grad_w_out.astype(jnp.bfloat16), "expert", scatter_dimension=1, tiled=True
+        ).astype(jnp.float32),
+        lax.psum_scatter(
+            grad_attn_gain.astype(jnp.bfloat16), "expert", scatter_dimension=0, tiled=True
+        ).astype(jnp.float32),
+        lax.psum_scatter(
+            grad_ffn_gain.astype(jnp.bfloat16), "expert", scatter_dimension=0, tiled=True
+        ).astype(jnp.float32),
+        lax.psum_scatter(
+            grad_qk_gain.astype(jnp.bfloat16), "expert", scatter_dimension=1, tiled=True
+        ).astype(jnp.float32),
+        lax.psum_scatter(
+            grad_router.astype(jnp.bfloat16), "expert", scatter_dimension=0, tiled=True
+        ).astype(jnp.float32),
+    )
     return (
         output,
         input_grad,
@@ -1372,9 +1576,148 @@
     )
 
 
+def compact(
+    tokens, w_query, w_key, w_value, w_out, attn_gain, ffn_gain, qk_gain, router, w_gate, w_up, w_down,
+    routes, cont_group, cotangent,
+):
+    rows, width = tokens.shape
+    local_width = w_query.shape[1]
+    head_count = local_width // HD
+    experts_total = router.shape[1]
+    local_experts = w_gate.shape[0]
+    ranks = lax.axis_size("expert")
+    device = lax.axis_index("expert")
+    full = jnp.float32
+    group, position, tag = layout(rows, ranks, device, cont_group)
+    frequency = 10000.0 ** (-jnp.arange(HD // 2, dtype=full) * 2.0 / HD)
+    angle = position.astype(full)[:, None] * frequency[None, :]
+    cosine, sine = jnp.cos(angle), jnp.sin(angle)
+    cosine = jnp.concatenate([cosine, cosine], axis=1)
+    sine = jnp.concatenate([-sine, sine], axis=1)
+    bias = jnp.where(attention_mask(group, position, tag, ranks), 0.0, masked_value).astype(full)
+    own_first = jnp.roll(router, -device * local_experts, axis=1)
+    own_first = jnp.pad(own_first, ((0, 0), (0, LANE - experts_total)))
+    expert_bias = jnp.where(jnp.arange(LANE) < experts_total, 0.0, masked_value).astype(full)[None]
+    turned_routes = jnp.tile(jnp.pad(routes.T, ((0, -routes.shape[1] % 8), (0, 0)), constant_values=-1), (2, 1))
+    hits = routes[:, :, None] == jnp.arange(experts_total, dtype=jnp.int32)
+    routed = jnp.any(hits, axis=1).astype(full)
+    (
+        attention, normed, normed_two, attended, query_rot, keys_values, query_raw, key_raw, stats, routes_all, arrived_grad,
+    ) = front(
+        tokens, attn_gain[None], ffn_gain[None], w_query, w_key, w_value, w_out, qk_gain, cosine, sine, bias,
+        turned_routes, cotangent,
+    )
+    own_expert = device * local_experts + jnp.arange(local_experts, dtype=jnp.int32)
+    names = routes_all[:, : turned_routes.shape[0] // 2]
+    expert_mask = jnp.any(names[:, :, :, None] == own_expert, axis=1).astype(full)
+    expert_mask = jnp.pad(expert_mask, ((0, 0), (0, 0), (0, LANE - local_experts)))
+    arrived = lax.all_gather(normed_two, "expert", axis=0)
+    reduced, gated, gate_grad, up_grad, mixed_part = experts_fused(
+        arrived, arrived_grad, expert_mask, own_first, expert_bias, w_gate, w_up, w_down
+    )
+    source = tokens.astype(full)
+    hidden = source + attention.astype(full)
+    scale_one, scale_two = stats[:, 0:1], stats[:, 3:4]
+    logits = jnp.dot(normed_two, router, preferred_element_type=full)
+    weights = jnp.exp(logits - jnp.max(logits, axis=1, keepdims=True))
+    chances = weights / jnp.sum(weights, axis=1, keepdims=True)
+    chance_grad = routed * reduced[:, width : width + experts_total].astype(full)
+    logit_grad = (
+        chances * (chance_grad - jnp.sum(chances * chance_grad, axis=1, keepdims=True))
+    ).astype(jnp.bfloat16)
+    grad_router = jnp.einsum("td,te->de", normed_two, logit_grad, preferred_element_type=full)
+    normed_two_grad = reduced[:, :width].astype(full) + jnp.einsum(
+        "te,de->td", logit_grad, router, preferred_element_type=full
+    )
+    grad_out = cotangent.astype(full)
+    weighted_two = ffn_gain * normed_two_grad
+    grad_ffn_gain = jnp.sum(normed_two_grad * hidden * scale_two, axis=0)
+    hidden_grad = (
+        grad_out
+        + scale_two * weighted_two
+        - hidden * (scale_two**3 / width) * jnp.sum(weighted_two * hidden, axis=1, keepdims=True)
+    )
+    attention_grad = hidden_grad.astype(jnp.bfloat16)
+    query_raw_grad, key_raw_grad, value_raw_grad, grad_qk_gain = backward(
+        attention_grad, w_out, query_rot, keys_values, bias, stats, query_raw, key_raw, cosine, sine, qk_gain
+    )
+    small_part = local_width // ranks
+    share = width // ranks
+    gains = jnp.pad(
+        grad_qk_gain.reshape(2, ranks, small_part).transpose(1, 2, 0), ((0, 0), (0, share - small_part), (0, 0))
+    )
+    extras = jnp.concatenate(
+        [grad_router.reshape(ranks, share, experts_total), grad_ffn_gain.reshape(ranks, share, 1), gains], axis=2
+    ).astype(jnp.bfloat16)
+    extras = jnp.pad(extras, ((0, 0), (0, 0), (0, LANE - experts_total - 3)))
+    normed_grad, sums, mixture, grad_w_gate, grad_w_up, grad_w_down = closing(
+        normed, query_raw_grad, key_raw_grad, value_raw_grad, attended, attention_grad, extras, w_query, w_key, w_value,
+        mixed_part, arrived, arrived_grad, gated, gate_grad, up_grad, local_experts,
+    )
+    normed_grad = normed_grad.astype(full)
+    output = (hidden + mixture.astype(full)).astype(jnp.bfloat16)
+    weighted_one = attn_gain * normed_grad
+    grad_attn_gain = jnp.sum(normed_grad * source * scale_one, axis=0)
+    input_grad = (
+        hidden_grad
+        + scale_one * weighted_one
+        - source * (scale_one**3 / width) * jnp.sum(weighted_one * source, axis=1, keepdims=True)
+    )
+    edge = 4 * local_width
+    return (
+        output,
+        input_grad,
+        sums[:, :local_width],
+        sums[:, local_width : 2 * local_width],
+        sums[:, 2 * local_width : 3 * local_width],
+        sums[:, 3 * local_width : edge].T,
+        lax.psum_scatter(
+            grad_attn_gain.astype(jnp.bfloat16), "expert", scatter_dimension=0, tiled=True
+        ).astype(full),
+        sums[:, edge + experts_total],
+        sums[:small_part, edge + experts_total + 1 : edge + experts_total + 3].T,
+        sums[:, edge : edge + experts_total],
+        grad_w_gate,
+        grad_w_up,
+        grad_w_down,
+    )
+
+
+def layout(rows, ranks, device, cont_group):
+    span = ranks // 2
+    prompt_len = PROMPT_DEV * span
+    local = jnp.arange(rows, dtype=jnp.int32)
+    is_prompt = local < PROMPT_DEV
+    after = jnp.maximum(local - PROMPT_DEV, 0)
+    slot_cont = after // CLEN
+    cont_pick = jnp.sum(
+        jnp.where(
+            slot_cont[:, None] == jnp.arange(CONT_DEV, dtype=jnp.int32)[None, :], cont_group[None, :], 0
+        ),
+        axis=1,
+    )
+    group = jnp.where(is_prompt, device // span, cont_pick)
+    position = jnp.where(is_prompt, device % span * PROMPT_DEV + local, prompt_len + after % CLEN)
+    tag = jnp.where(is_prompt, -1, slot_cont)
+    return group, position, tag
+
+
+def attention_mask(group, position, tag, ranks):
+    prompt_len = PROMPT_DEV * (ranks // 2)
+    key_index = jnp.arange(ranks * PROMPT_DEV, dtype=jnp.int32)
+    prompt_mask = (group[:, None] == (key_index // prompt_len)[None, :]) & (
+        (key_index % prompt_len)[None, :] <= position[:, None]
+    )
+    own_mask = (tag[:, None] == tag[None, PROMPT_DEV:]) & (
+        position[None, PROMPT_DEV:] <= position[:, None]
+    )
+    return jnp.concatenate([prompt_mask, own_mask], axis=1)
+
+
 def solution(mesh):
+    small = mesh.shape["expert"] == 8
     return jax.shard_map(
-        body,
+        compact if small else body,
         mesh=mesh,
         in_specs=(
             P("expert", None),

time: 626 us -> 567 us (0.906)
  Pallas kernels: 323 us -> 415 us
  waiting for transfers between devices: 104 us -> 64 us
  blocking collectives: 45.9 us -> 11.8 us
  local copies, waits for them, and re-layouts: 56.1 us -> 25.7 us
  other arithmetic: 49.1 us -> 20.6 us
  matrix products: 23.6 us -> 5.92 us
    pallas_call x1 -> x2, Pallas kernels: 69.6 us -> 160 us  [the longest x1 127 us: front(): pl.pallas_call(front_kernel, out_shape=(jax.ShapeDtypeStruct((rows, width...]
    reduce_scatter x1 -> x0, waiting for transfers between devices: 30 us -> none  [body(): lax.psum_scatter(jnp.concatenate([key_grad_all[:prompt_count], value_grad...]
    psum x2 -> x0, blocking collectives: 25.8 us -> none  [the longest x1 13.5 us: body(): lax.psum(jnp.stack([jnp.sum(query_raw * query_raw, axis=1), jnp.sum(key_r...]
    dot_general x31 -> x3, matrix products: 23.6 us -> 5.92 us  [the longest x1 3.5 us: compact(): jnp.einsum('te,de->td', logit_grad, router, preferred_element_type=full)]
    unnamed x256 -> x41, local copies, waits for them, and re-layouts: 31 us -> 13.7 us
    all_gather x2 -> x1, waiting for transfers between devices: 73.9 us -> 64 us  [compact(): arrived = lax.all_gather(normed_two, 'expert', axis=0)]
    all_gather x1 -> x0, blocking collectives: 8.29 us -> none  [body(): routes_all = lax.all_gather(routes, 'expert', axis=0)]
    convert_element_type x11 -> x2, other arithmetic: 10 us -> 2.95 us  [the longest x1 2.32 us: compact(): attention_grad = hidden_grad.astype(jnp.bfloat16)]
  transfers between devices with their start and end apart: 3 -> 1, of which waited for: 3 -> 1; matrix products, arithmetic and copies ran while one was open for 4% -> 1% of each run, Pallas kernels for 0% -> 0%
where the time goes in v5:
time: 567 us; the launch traced here: 559 us
  Pallas kernels  415 us (73%)
  waiting for transfers between devices  64 us (11%)
  local copies, waits for them, and re-layouts  25.7 us (5%)
  other arithmetic  20.6 us (4%)
  between operations  16.2 us (3%)
  blocking collectives  11.8 us (2%)
  matrix products  5.92 us (1%)
    pallas_call x1, Pallas kernels, experts_fused(): pl.pallas_call(expert_kernel, out_shape=(jax.ShapeDtypeStruct((rows, wide...  128 us
    pallas_call x1, Pallas kernels, closing(): pl.pallas_call(closing_kernel, out_shape=(jax.ShapeDtypeStruct((rows, wid...  127 us
    pallas_call x1, Pallas kernels, front(): pl.pallas_call(front_kernel, out_shape=(jax.ShapeDtypeStruct((rows, width...  127 us
    all_gather x1, waiting for transfers between devices, compact(): arrived = lax.all_gather(normed_two, 'expert', axis=0)  64 us
    pallas_call x1, Pallas kernels, backward(): pl.pallas_call(backward_kernel, out_shape=(small, small, small, jax.Shape...  32.7 us
    unnamed x41, local copies, waits for them, and re-layouts  13.7 us
    unnamed x1, blocking collectives  11.8 us
  transfers between devices with their start and end apart: 1, of which 1 were waited for; matrix products, arithmetic and copies ran while one was open for 1% of the time, Pallas kernels for 0%

profile of v5, /device:TPU:0, one launch (start us, length us, event | category | flops | bytes accessed | tf_op | source)
XLA Modules:
  0.0 559.2 jit_solution(15120681568295673786)
XLA Ops:
  9.6 1.3 broadcast_bitcast_fusion.routes
  11.5 1.5 add_select_fusion.bias
  13.7 126.8 %shard_map.246 = (bf16[384,2048]{1,0:T(8,128)(2,1)}, bf16[384,2048]{1,0:T(8,128)(2,1)}, bf16[384,2048]{1,0:T(8,128)(2,1)}, bf16[384,512]{1,0:T(8,128)(2,1)}, bf1...) custom-call(bf16[384,2048]{1,0:T(8,128)(2,1)} %tokens.1, ...), custom_call_target="tpu_custom_call" | custom-call | tf_op jit(solution)/shard_map/pallas_call | solution.py:1046
  147.0 1.3 pad_convert_fusion.mask
  148.3 64.0 %all-gather.3.cloned.1.call-done.x_all = bf16[3072,2048]{1,0:T(8,128)(2,1)} async-done(((bf16[384,2048]{1,0:T(8,128)(2,1)}), bf16[3072,2048]{1,0:T(8,128)(2,1)}) %all-gather.3.cloned.1.call-update) | async-done | bytes 12582928 | tf_op jit(solution)/shard_map/all_gather | solution.py:1614
  212.3 128.3 %shard_map.247 = (bf16[384,2176]{1,0:T(8,128)(2,1)}, bf16[8,384,512]{2,1,0:T(8,128)(2,1)}, bf16[8,384,512]{2,1,0:T(8,128)(2,1)}, bf16[8,384,512]{2,1,0:T(8,128)(2,1)}, bf16[8,384,2048]{2,1,0:T(8,128)(2,1)}) custom-call(bf16[8,384,2048]{2,1,0:T(8,128)(2,1)} %bitcast.27, bf16[8,384,2048]{2,1,0:T(8,128)(2,1)} %get-tuple-element.43.g_all, ...), custom_call_target="tpu_custom_call" | custom-call | flops 38654705664 | bytes 50331648 | tf_op jit(solution)/shard_map/pallas_call | solution.py:545
  340.6 1.2 multiply_reduce_fusion.2
  341.8 1.9 convolution_convert_fusion
  343.8 3.5 multiply_reduce_fusion
  347.3 2.3 fusion.34.attention_grad
  349.6 32.7 %shard_map.248 = (bf16[384,512]{1,0:T(8,128)(2,1)}, bf16[384,512]{1,0:T(8,128)(2,1)}, bf16[384,512]{1,0:T(8,128)(2,1)}, f32[2,512]{1,0:T(2,128)}) custom-call(bf16[384,2048]{1,0:T(8,128)(2,1)} %fusion.34.attention_grad, bf16[512,2048]{1,0:T(8,128)(2,1)} %w_out.3, bf16[384,512]{1,0:T(8,128)(2,1)} %get-tuple-element.46.query_rot, ...), custom_call_target="tpu_custom_call" | custom-call | tf_op jit(solution)/shard_map/pallas_call | solution.py:1171
  384.3 127.1 %shard_map.249 = (bf16[384,2048]{1,0:T(8,128)(2,1)}, f32[256,2176]{1,0:T(8,128)}, bf16[384,2048]{1,0:T(8,128)(2,1)}, f32[2,2048,256]{2,1,0:T(8,128)}, f32[2,2048,256]{2,1,0:T(8,128)}, /*index=5*/f32[2,256,2048]{2,1,0:T(8,128)}) custom-call(bf16[384,2048]{1,0:T(8,128)(2,1)} %get-tuple-element.40.normed, bf16[384,512]{1,0:T(8,128)(2,1)} %get-tuple-element.50.query_grad, ...), custom_call_target="tpu_custom_call" | custom-call | tf_op jit(solution)/shard_map/pallas_call | solution.py:821
  511.4 3.0 slice_bitcast_fusion
  514.4 1.0 slice.55
  516.3 1.7 slice_reduce_fusion.2
  517.9 2.0 copy.59
  521.3 2.4 fusion.6
  523.7 11.8 %all-reduce.4 = bf16[2048]{0:T(1024)(128)(2,1)S(1)} all-reduce(bf16[2048]{0:T(1024)(128)(2,1)S(1)} %get-tuple-element.119), channel_id=3, replica_groups=mesh['expert'=8,'tensor'=4] {'expert'}, use_global_device_ids=true, to_apply=%region_9.10.clone | all-reduce | flops 2048 | bytes 8192
  536.1 6.4 %fusion.2 = (f32[384,2048]{1,0:T(8,128)}, bf16[384,2048]{1,0:T(8,128)(2,1)}) fusion(bf16[384,2048]{1,0:T(8,128)(2,1)} %get-tuple-element.60, bf16[384,2048]{1,0:T(8,128)(2,1)S(1)} %copy-done.1, f32[384]{0:T(512)S(1)} %get-tuple-element.120, f32[384]{0:T(512)S(1)} %get-tuple-element.123, f32[2048]{0:T(1024)S(1)} %copy-done.12, f32[384]{0:T(512)S(1)} %get-tuple-element.121, ...), kind=kLoop, calls=%fused_computation.7 | loop fusion | flops 15728640 | bytes 15754240 | tf_op jit(solution)/shard_map/sub | solution.py:1662
  542.5 2.1 copy.71
  544.6 1.6 copy-done.8
  546.2 2.1 copy.72
  548.3 1.6 copy-done.7
  549.9 2.0 copy.73
  (70 shorter events, 13.5 us)
Async XLA Ops:
  7.2 205.1 %all-gather.3.cloned.1.call-start = ((), (), s32[]{:S(2)}) async-start(), calls=%async_computation | async-start | bytes 14155776 | tf_op jit(solution)/shard_map/all_gather | solution.py:1614
  13.7 128.8 %copy-start.11 = (bf16[2048,16]{0,1:T(8,128)(2,1)S(1)}, bf16[2048,16]{0,1:T(8,128)(2,1)}, u32[]{:S(2)}) copy-start(bf16[2048,16]{0,1:T(8,128)(2,1)} %param.23) | copy-start | bytes 196612
  140.6 2.3 copy-start.5
  140.6 3.0 copy-start.14
  140.6 4.0 copy-start.15
  140.6 6.0 %copy-start.10 = (f32[384,128]{1,0:T(8,128)S(1)}, f32[384,128]{1,0:T(8,128)}, u32[]{:S(2)}) copy-start(f32[384,128]{1,0:T(8,128)} %get-tuple-element.41.stats) | copy-start | bytes 589828
  212.3 131.4 %copy-start = (bf16[384,2048]{1,0:T(8,128)(2,1)S(1)}, bf16[384,2048]{1,0:T(8,128)(2,1)}, u32[]{:S(2)}) copy-start(bf16[384,2048]{1,0:T(8,128)(2,1)} %tokens.1) | copy-start | bytes 4718596
  212.3 131.4 %copy-start.13 = (f32[2048]{0:T(1024)S(1)}, f32[2048]{0:T(1024)}, u32[]{:S(2)}) copy-start(f32[2048]{0:T(1024)} %param.21) | copy-start | bytes 24580
  343.7 3.5 copy-start.2
  343.7 3.5 copy-start.6
  347.2 2.4 copy-start.4
  511.4 9.9 %copy-start.1 = (bf16[384,2048]{1,0:T(8,128)(2,1)S(1)}, bf16[384,2048]{1,0:T(8,128)(2,1)}, u32[]{:S(2)}) copy-start(bf16[384,2048]{1,0:T(8,128)(2,1)} %tokens.1) | copy-start | bytes 4718596
  511.4 9.9 %copy-start.12 = (f32[2048]{0:T(1024)S(1)}, f32[2048]{0:T(1024)}, u32[]{:S(2)}) copy-start(f32[2048]{0:T(1024)} %param.20) | copy-start | bytes 24580
  514.4 21.7 %copy-start.3 = (bf16[384,2048]{1,0:T(8,128)(2,1)S(1)}, bf16[384,2048]{1,0:T(8,128)(2,1)}, u32[]{:S(2)}) copy-start(bf16[384,2048]{1,0:T(8,128)(2,1)} %cotangent.1) | copy-start | bytes 4718596
  536.1 6.4 %copy-start.9 = (f32[2,2048,256]{2,1,0:T(8,128)S(1)}, f32[2,2048,256]{2,1,0:T(8,128)}, u32[]{:S(2)}) copy-start(f32[2,2048,256]{2,1,0:T(8,128)} %get-tuple-element.164) | copy-start | bytes 12582916
  542.5 3.7 copy-start.8
  546.2 3.7 copy-start.7
Sparse Core Ops, SparseCore 0:
  140.8 71.4 all-gather.2

commit v6 on v5

--- a/solution.py
+++ b/solution.py
@@ -1,3 +1,5 @@
+import functools
+
 import jax
 import jax.numpy as jnp
 from jax import lax
@@ -339,7 +341,7 @@
     def far_copy(self, piece):
         rows = self.rows(piece)
         came, goes = (
-            (self.place.x_chip, self.place.y_chip) if piece < self.pieces // 2 else (self.place.y_chip, self.place.x_chip)
+            (self.place.x_chip, self.place.y_chip) if piece % 2 == 0 else (self.place.y_chip, self.place.x_chip)
         )
         return remote(
             self.target.at[came, rows], self.target.at[came, rows],
@@ -367,11 +369,11 @@
 
     def near(self, piece):
         self.x_copy(piece).wait_recv()
-        if piece < self.pieces // 2:
+        if piece % 2 == 0:
             self.far_copy(piece).start()
         self.pair_copy(1, piece).start()
         self.y_copy(piece).wait_recv()
-        if piece >= self.pieces // 2:
+        if piece % 2 == 1:
             self.far_copy(piece).start()
         self.pair_copy(2, piece).start()
 
@@ -574,9 +576,6 @@
     )(arrived, arrived_grad, mask, router, bias, w_gate, w_up, w_down)
 
 
-GATHER_PIECES = 4
-
-
 def crossed_dot(left, right):
     return lax.dot_general(left, right, (((0,), (0,)), ((), ())), preferred_element_type=jnp.float32)
 
@@ -584,11 +583,14 @@
 def closing_kernel(
     normed, query_grad, key_grad, value_grad, attended, attention_grad, extras,
     w_query, w_key, w_value, mixed, x_all, g_all, gated_all, gate_all, up_all,
-    total, sums, mixture, gate_out, up_out, down_out,
+    total, sums, gain, mixture, gate_out, up_out, down_out,
     line_own, line_in, part, paired, from_x, from_y,
     mix_own, mix_paired, mix_x, mix_y, mix_in, tiles, factors, results, downs,
     line_sems, pair_sems, x_sems, y_sems, mix_line_sems, mix_pair_sems, mix_x_sems, mix_y_sems,
     load_sems, weight_sems, factor_sems, tile_sems, out_sems,
+    gains, mine, theirs, peer_sent, peer_got,
+    *,
+    gain_column,
 ):
     width = normed.shape[1]
     heads = query_grad.shape[1]
@@ -601,6 +603,7 @@
     plane = Plane(part.at[1], part.at[0], paired, from_x, from_y, pair_sems, x_sems, y_sems)
     mix = Plane(mix_own, mixed, mix_paired, mix_x, mix_y, mix_pair_sems, mix_x_sems, mix_y_sems, by_device=True)
     mix_line = Line(mix_own.at[3], mix_in, mixture, mix_line_sems)
+    peers = Peers(mine, theirs, peer_sent, peer_got)
     half = width // 2
 
     def load_own(chip):
@@ -707,7 +710,7 @@
         part[sub, chip, :, 3 * heads : 4 * heads] = crossed_dot(
             attention_grad[:, columns], attended[...]
         ).astype(jnp.bfloat16)
-        part[sub, chip, :, 4 * heads :] = extras[block]
+        part[sub, chip, :, 4 * heads :] = extras[block] + gains[columns]
 
         @pl.when(sub == 0)
         def _():
@@ -717,7 +720,7 @@
         copy.start()
     for chip in range(4):
         load_own(chip).start()
-    greet(plane.neighbours() + line.neighbours())
+    greet(plane.neighbours() + peers.neighbours())
     for chip in range(4):
         mix.pair_copy(chip).start()
     for copy in weight_loads:
@@ -730,6 +733,12 @@
             + turned_dot(key_grad[...], factors[1, columns])
             + turned_dot(value_grad[...], factors[start // half, later : later + column_tile])
         ).astype(jnp.bfloat16)
+    place = lax.broadcasted_iota(jnp.int32, (normed.shape[0], LANE), 1)
+    chosen = jnp.where(place == gain_column, 1.0, 0.0).astype(jnp.bfloat16)
+    for start in range(0, width, column_tile):
+        columns = slice(start, start + column_tile)
+        pull = line_own[:, columns].astype(jnp.float32) * normed[:, columns].astype(jnp.float32)
+        gains[columns] = crossed_dot(pull.astype(jnp.bfloat16), chosen).astype(jnp.bfloat16)
     factor_load(0).start()
     factor_load(1).start()
     start_tile(0)
@@ -790,13 +799,17 @@
 
     steps = jnp.maximum(mix_last + mix_line.steps(), jnp.maximum(3 * count, dense_last + plane.pieces))
     lax.fori_loop(0, steps, step, 0)
+    column = 4 * heads + gain_column
+    mine[...] = to_rows([sums[:, column : column + 1]], share)
+    peers.start()
     for s in (2 * count - 2, 2 * count - 1):
         for copy in across(up_out, s):
             copy.wait()
     for s in (3 * count - 2, 3 * count - 1):
         for copy in down(s):
             copy.wait()
-    for each in (plane, line, mix, mix_line):
+    gain[...] = peers.total()
+    for each in (plane, line, mix, mix_line, peers):
         each.finish()
 
 
@@ -805,7 +818,7 @@
 
 def closing(
     normed, query_grad, key_grad, value_grad, attended, attention_grad, extras, w_query, w_key, w_value,
-    mixed, arrived, arrived_grad, gated, gate_grad, up_grad, experts,
+    mixed, arrived, arrived_grad, gated, gate_grad, up_grad, experts, gain_column,
 ):
     rows, width = normed.shape
     heads = query_grad.shape[1]
@@ -818,18 +831,20 @@
     vmem = pl.BlockSpec(memory_space=pltpu.VMEM)
     any_space = pl.BlockSpec(memory_space=pl.ANY)
     every = ranks * rows
+    size = lax.axis_size("tensor")
     return pl.pallas_call(
-        closing_kernel,
+        functools.partial(closing_kernel, gain_column=gain_column),
         out_shape=(
             jax.ShapeDtypeStruct((rows, width), low),
             jax.ShapeDtypeStruct((share, wide), jnp.float32),
+            jax.ShapeDtypeStruct((8, share), jnp.float32),
             jax.ShapeDtypeStruct((rows, width), low),
             jax.ShapeDtypeStruct((experts, width, hidden), jnp.float32),
             jax.ShapeDtypeStruct((experts, width, hidden), jnp.float32),
             jax.ShapeDtypeStruct((experts, hidden, width), jnp.float32),
         ),
         in_specs=[vmem] * 7 + [any_space] * 9,
-        out_specs=(vmem,) * 3 + (any_space,) * 3,
+        out_specs=(vmem,) * 4 + (any_space,) * 3,
         scratch_shapes=[
             pltpu.VMEM((rows, width), low),
             pltpu.VMEM((rows, width), low),
@@ -855,6 +870,11 @@
             pltpu.SemaphoreType.DMA((3,)),
             pltpu.SemaphoreType.DMA((2,)),
             pltpu.SemaphoreType.DMA((2, 2, experts)),
+            pltpu.VMEM((width, LANE), low),
+            pltpu.VMEM((8, share), jnp.float32),
+            pltpu.VMEM((size - 1, 8, share), jnp.float32),
+            pltpu.SemaphoreType.DMA((size - 1,)),
+            pltpu.SemaphoreType.DMA((size - 1,)),
         ],
         compiler_params=pltpu.CompilerParams(
             collective_id=2, has_side_effects=True, vmem_limit_bytes=63 * 2**20
@@ -918,10 +938,14 @@
     return jnp.concatenate([field[:, half:], field[:, :half]], axis=1)
 
 
+SPREAD = 32
+SPREAD_LAG = 2
+
+
 def front_kernel(
-    tokens, attn_gain, ffn_gain, w_query, w_key, w_value, w_out, qk_gain, cosine, sine, bias, routes, cotangent,
-    total, normed, normed_two, attended, query_rot, keys_values, query_raw, key_raw, stats, routes_all, spread_all,
-    line_own, line_in, prompt, mine, theirs,
+    tokens, attn_gain, ffn_gain, w_query, w_key, w_value, w_out, qk_gain, cosine, sine, bias, routes,
+    total, normed, normed_two, attended, query_rot, keys_values, query_raw, key_raw, stats, routes_all, arrived,
+    line_own, line_in, prompt, mine, theirs, two,
     line_sems, peer_sent, peer_got, *gather_sems,
 ):
     rows, width = tokens.shape
@@ -933,13 +957,11 @@
     place = Place()
     line = Line(line_own, line_in, total, line_sems)
     peers = Peers(mine, theirs, peer_sent, peer_got)
-    spread = Gather(cotangent, spread_all, place, *gather_sems[0:5], pieces=GATHER_PIECES)
-    names = Gather(routes, routes_all, place, *gather_sems[5:10], pieces=2)
-    prompts = Gather(prompt, keys_values, place, *gather_sems[10:15], pieces=2)
+    names = Gather(routes, routes_all, place, *gather_sems[0:5], pieces=2)
+    prompts = Gather(prompt, keys_values, place, *gather_sems[5:10], pieces=2)
+    spread = Gather(normed_two, arrived, place, *gather_sems[10:15], pieces=rows // SPREAD)
     greet(place.neighbours() + peers.neighbours())
     names.start()
-    spread.own_copy().start()
-    spread.start_piece(0)
     source = tokens[...].astype(jnp.float32)
     scale_one = lax.rsqrt(jnp.sum(source * source, axis=1, keepdims=True) / width + epsilon)
     normed[...] = (source * scale_one * attn_gain[...]).astype(jnp.bfloat16)
@@ -970,8 +992,6 @@
     prompts.own_copy().start()
     for piece in range(2):
         prompts.start_piece(piece)
-    for piece in range(1, GATHER_PIECES):
-        spread.start_piece(piece)
     for head in range(heads):
         columns = slice(head * HD, (head + 1) * HD)
         turned = query_raw[:, columns] * scale_query * qk_gain[0:1, columns]
@@ -1010,38 +1030,53 @@
         columns = slice(start, start + tile)
         line_own[:, columns] = wide_dot(attended[...], w_out[:, columns]).astype(jnp.bfloat16)
     steps = line.pieces + 2 * (line.size - 1)
+    ratio = SPREAD // STEP
+    groups = line.pieces // ratio
+
+    def norm_rows(piece):
+        span = slice(piece * SPREAD, (piece + 1) * SPREAD)
+        hidden = tokens[span].astype(jnp.float32) + total[span].astype(jnp.float32)
+        scale = lax.rsqrt(jnp.sum(hidden * hidden, axis=1, keepdims=True) / width + epsilon)
+        normed_two[span] = (hidden * scale * ffn_gain[...]).astype(jnp.bfloat16)
+        two[span] = jnp.broadcast_to(scale, (SPREAD, LANE))
+
     done = 0
-    for piece in range(GATHER_PIECES):
-        upto = steps * (piece + 1) // (2 * GATHER_PIECES)
-        lax.fori_loop(done, upto, line.step_body, 0)
-        done = upto
-        spread.near(piece)
-    for piece in range(GATHER_PIECES):
-        upto = done + (steps - done) * (piece + 1) // GATHER_PIECES
-        lax.fori_loop(done, upto, line.step_body, 0)
-        done = upto
-        spread.far(piece)
-    hidden = tokens[...].astype(jnp.float32) + total[...].astype(jnp.float32)
-    scale_two = lax.rsqrt(jnp.sum(hidden * hidden, axis=1, keepdims=True) / width + epsilon)
-    normed_two[...] = (hidden * scale_two * ffn_gain[...]).astype(jnp.bfloat16)
-    stats[...] = jnp.where(lane == 3, scale_two, kept)
+    passed = 0
+    for group in range(groups):
+        ready = 2 * (line.size - 1) + (group + 1) * ratio
+        lax.fori_loop(done, ready, line.step_body, 0)
+        done = ready
+        for piece in (group, groups + group):
+            norm_rows(piece)
+            spread.start_piece(piece)
+        if group >= SPREAD_LAG:
+            for piece in (passed, groups + passed):
+                spread.near(piece)
+            passed += 1
+    spread.own_copy().start()
+    for group in range(passed, groups):
+        for piece in (group, groups + group):
+            spread.near(piece)
+    for group in range(groups):
+        for piece in (group, groups + group):
+            spread.far(piece)
+    stats[...] = jnp.where(lane == 3, two[...], kept)
     for kind in range(4):
-        for piece in range(GATHER_PIECES):
+        for piece in range(spread.pieces):
             spread.paired(kind, piece)
+    spread.own_copy().wait()
     names.own_copy().wait()
-    spread.own_copy().wait()
     for each in (names, prompts, spread, line, peers):
         each.finish()
 
 
-def front(tokens, attn_gain, ffn_gain, w_query, w_key, w_value, w_out, qk_gain, cosine, sine, bias, routes, cotangent):
+def front(tokens, attn_gain, ffn_gain, w_query, w_key, w_value, w_out, qk_gain, cosine, sine, bias, routes):
     rows, width = tokens.shape
     local = w_query.shape[1]
     ranks = lax.axis_size("expert")
     size = lax.axis_size("tensor")
     low, full = jnp.bfloat16, jnp.float32
     vmem = pl.BlockSpec(memory_space=pltpu.VMEM)
-    any_space = pl.BlockSpec(memory_space=pl.ANY)
     blocks = ranks + rows // PROMPT_DEV - 1
     return pl.pallas_call(
         front_kernel,
@@ -1058,25 +1093,27 @@
             jax.ShapeDtypeStruct((ranks,) + routes.shape, jnp.int32),
             jax.ShapeDtypeStruct((ranks, rows, width), low),
         ),
-        in_specs=[vmem] * 12 + [any_space],
-        out_specs=(vmem,) * 10 + (any_space,),
+        in_specs=[vmem] * 12,
+        out_specs=(vmem,) * 10 + (pl.BlockSpec(memory_space=pl.ANY),),
         scratch_shapes=[
             pltpu.VMEM((rows, width), low),
             pltpu.VMEM((rows, width), low),
             pltpu.VMEM((PROMPT_DEV, 2 * local), low),
             pltpu.VMEM((8, rows), full),
             pltpu.VMEM((size - 1, 8, rows), full),
+            pltpu.VMEM((rows, LANE), full),
             Line.semaphores(rows),
             pltpu.SemaphoreType.DMA((size - 1,)),
             pltpu.SemaphoreType.DMA((size - 1,)),
-            *Gather.semaphores(GATHER_PIECES),
             *Gather.semaphores(2),
             *Gather.semaphores(2),
+            *Gather.semaphores(rows // SPREAD),
         ],
         compiler_params=pltpu.CompilerParams(
             collective_id=1, has_side_effects=True, vmem_limit_bytes=60 * 2**20
         ),
-    )(tokens, attn_gain, ffn_gain, w_query, w_key, w_value, w_out, qk_gain, cosine, sine, bias, routes, cotangent)
+        cost_estimate=pl.CostEstimate(flops=100 * 10**9, bytes_accessed=200 * 10**6, transcendentals=0),
+    )(tokens, attn_gain, ffn_gain, w_query, w_key, w_value, w_out, qk_gain, cosine, sine, bias, routes)
 
 
 def backward_kernel(
@@ -1602,16 +1639,16 @@
     hits = routes[:, :, None] == jnp.arange(experts_total, dtype=jnp.int32)
     routed = jnp.any(hits, axis=1).astype(full)
     (
-        attention, normed, normed_two, attended, query_rot, keys_values, query_raw, key_raw, stats, routes_all, arrived_grad,
+        attention, normed, normed_two, attended, query_rot, keys_values, query_raw, key_raw, stats, routes_all, arrived,
     ) = front(
         tokens, attn_gain[None], ffn_gain[None], w_query, w_key, w_value, w_out, qk_gain, cosine, sine, bias,
-        turned_routes, cotangent,
-    )
+        turned_routes,
+    )
+    arrived_grad = lax.all_gather(cotangent, "expert", axis=0)
     own_expert = device * local_experts + jnp.arange(local_experts, dtype=jnp.int32)
     names = routes_all[:, : turned_routes.shape[0] // 2]
     expert_mask = jnp.any(names[:, :, :, None] == own_expert, axis=1).astype(full)
     expert_mask = jnp.pad(expert_mask, ((0, 0), (0, 0), (0, LANE - local_experts)))
-    arrived = lax.all_gather(normed_two, "expert", axis=0)
     reduced, gated, gate_grad, up_grad, mixed_part = experts_fused(
         arrived, arrived_grad, expert_mask, own_first, expert_bias, w_gate, w_up, w_down
     )
@@ -1650,14 +1687,13 @@
         [grad_router.reshape(ranks, share, experts_total), grad_ffn_gain.reshape(ranks, share, 1), gains], axis=2
     ).astype(jnp.bfloat16)
     extras = jnp.pad(extras, ((0, 0), (0, 0), (0, LANE - experts_total - 3)))
-    normed_grad, sums, mixture, grad_w_gate, grad_w_up, grad_w_down = closing(
+    normed_grad, sums, gain_total, mixture, grad_w_gate, grad_w_up, grad_w_down = closing(
         normed, query_raw_grad, key_raw_grad, value_raw_grad, attended, attention_grad, extras, w_query, w_key, w_value,
-        mixed_part, arrived, arrived_grad, gated, gate_grad, up_grad, local_experts,
+        mixed_part, arrived, arrived_grad, gated, gate_grad, up_grad, local_experts, experts_total + 3,
     )
     normed_grad = normed_grad.astype(full)
     output = (hidden + mixture.astype(full)).astype(jnp.bfloat16)
     weighted_one = attn_gain * normed_grad
-    grad_attn_gain = jnp.sum(normed_grad * source * scale_one, axis=0)
     input_grad = (
         hidden_grad
         + scale_one * weighted_one
@@ -1671,9 +1707,7 @@
         sums[:, local_width : 2 * local_width],
         sums[:, 2 * local_width : 3 * local_width],
         sums[:, 3 * local_width : edge].T,
-        lax.psum_scatter(
-            grad_attn_gain.astype(jnp.bfloat16), "expert", scatter_dimension=0, tiled=True
-        ).astype(full),
+        gain_total[0] / lax.dynamic_slice_in_dim(attn_gain, device * share, share),
         sums[:, edge + experts_total],
         sums[:small_part, edge + experts_total + 1 : edge + experts_total + 3].T,
         sums[:, edge : edge + experts_total],

time: 567 us -> 504 us (0.89)
  waiting for transfers between devices: 64 us -> 0.68 us
  blocking collectives: 11.8 us -> 0 us
  Pallas kernels: 415 us -> 426 us
    all_gather x1, waiting for transfers between devices: 64 us -> 0.01 us  [compact(): arrived_grad = lax.all_gather(cotangent, 'expert', axis=0)]
    unnamed x1 -> x0, blocking collectives: 11.8 us -> none
    pallas_call x1, Pallas kernels: 127 us -> 134 us  [front(): pl.pallas_call(front_kernel, out_shape=(jax.ShapeDtypeStruct((rows, width...]
    unnamed x41 -> x42, local copies, waits for them, and re-layouts: 13.7 us -> 13.1 us
  transfers between devices with their start and end apart: 1 -> 1, of which waited for: 1 -> 0; matrix products, arithmetic and copies ran while one was open for 1% -> 3% of each run, Pallas kernels for 0% -> 27%
where the time goes in v6:
time: 504 us; the launch traced here: 499 us
  Pallas kernels  426 us (85%)
  local copies, waits for them, and re-layouts  25.1 us (5%)
  other arithmetic  23.2 us (5%)
  between operations  15.3 us (3%)
  matrix products  8.93 us (2%)
    pallas_call x1, Pallas kernels, front(): pl.pallas_call(front_kernel, out_shape=(jax.ShapeDtypeStruct((rows, width...  134 us
    pallas_call x1, Pallas kernels, closing(): pl.pallas_call(functools.partial(closing_kernel, gain_column=gain_column)...  130 us
    pallas_call x1, Pallas kernels, experts_fused(): pl.pallas_call(expert_kernel, out_shape=(jax.ShapeDtypeStruct((rows, wide...  130 us
    pallas_call x1, Pallas kernels, backward(): pl.pallas_call(backward_kernel, out_shape=(small, small, small, jax.Shape...  32.3 us
    unnamed x42, local copies, waits for them, and re-layouts  13.1 us
  transfers between devices with their start and end apart: 1, of which 0 were waited for; matrix products, arithmetic and copies ran while one was open for 3% of the time, Pallas kernels for 27%

profile of v6, /device:TPU:0, one launch (start us, length us, event | category | flops | bytes accessed | tf_op | source)
XLA Modules:
  0.0 499.0 jit_solution(5534829417248272245)
XLA Ops:
  9.6 0.9 fusion.12
  14.4 1.5 add_select_fusion.bias
  15.8 134.3 %shard_map.246 = (bf16[384,2048]{1,0:T(8,128)(2,1)}, bf16[384,2048]{1,0:T(8,128)(2,1)}, bf16[384,2048]{1,0:T(8,128)(2,1)}, bf16[384,512]{1,0:T(8,128)(2,1)}, bf1...) custom-call(bf16[384,2048]{1,0:T(8,128)(2,1)} %tokens.1, ...), custom_call_target="tpu_custom_call" | custom-call | flops 99999997952 | bytes 200000000 | tf_op jit(solution)/shard_map/pallas_call | solution.py:1081
  150.1 0.9 slice.48
  151.0 1.9 fusion.31
  153.9 0.9 pad.21.router
  156.5 1.3 pad_convert_fusion.mask
  157.8 129.6 %shard_map.247 = (bf16[384,2176]{1,0:T(8,128)(2,1)}, bf16[8,384,512]{2,1,0:T(8,128)(2,1)}, bf16[8,384,512]{2,1,0:T(8,128)(2,1)}, bf16[8,384,512]{2,1,0:T(8,128)(2,1)}, bf16[8,384,2048]{2,1,0:T(8,128)(2,1)}) custom-call(bf16[8,384,2048]{2,1,0:T(8,128)(2,1)} %get-tuple-element.43.x_all, bf16[8,384,2048]{2,1,0:T(8,128)(2,1)} %bitcast.26, ...), custom_call_target="tpu_custom_call" | custom-call | flops 38654705664 | bytes 50331648 | tf_op jit(solution)/shard_map/pallas_call | solution.py:547
  287.4 1.2 multiply_reduce_fusion.2
  288.5 1.9 convolution_convert_fusion
  290.5 5.1 %multiply_reduce_fusion = (bf16[2048]{0:T(1024)(128)(2,1)S(1)}, f32[384]{0:T(512)S(1)}, f32[384,2048]{1,0:T(8,128)}) fusion(bf16[384,2048]{1,0:T(8,128)(2,1)} %get-tuple-element.40, bf16[384,2048]{1,0:T(8,128)(2,1)S(1)} %copy-done.2, f32[384]{0:T(512)S(1)} %get-tuple-element.124, f32[2048]{0:T(1024)S(1)} %copy-done.14, bf16[2048,16]{0,1:T(8,128)(2,1)S(1)} %copy-done.10, ...), kind=kOutput, calls=%fused_computation.8 | convolution fusion | flops 33857152 | bytes 8078848 | tf_op jit(solution)/shard_map/te,de->td/dot_general | solution.py:1666
  295.6 4.6 fusion.30.attention_grad
  300.3 32.3 %shard_map.248 = (bf16[384,512]{1,0:T(8,128)(2,1)}, bf16[384,512]{1,0:T(8,128)(2,1)}, bf16[384,512]{1,0:T(8,128)(2,1)}, f32[2,512]{1,0:T(2,128)}) custom-call(bf16[384,2048]{1,0:T(8,128)(2,1)} %fusion.30.attention_grad, bf16[512,2048]{1,0:T(8,128)(2,1)} %w_out.3, bf16[384,512]{1,0:T(8,128)(2,1)} %get-tuple-element.47.query_rot, ...), custom_call_target="tpu_custom_call" | custom-call | tf_op jit(solution)/shard_map/pallas_call | solution.py:1208
  334.6 129.6 %shard_map.249 = (bf16[384,2048]{1,0:T(8,128)(2,1)}, f32[256,2176]{1,0:T(8,128)}, f32[8,256]{1,0:T(8,128)}, bf16[384,2048]{1,0:T(8,128)(2,1)}, f32[2,2048,256]{2...) custom-call(bf16[384,2048]{1,0:T(8,128)(2,1)} %get-tuple-element.41.normed, ...), custom_call_target="tpu_custom_call" | custom-call | tf_op jit(solution)/shard_map/pallas_call | solution.py:835
  464.3 1.8 slice_reduce_fusion.2
  466.9 0.9 slice.59
  467.8 2.9 slice_bitcast_fusion
  473.4 2.0 copy.59
  476.1 6.3 %fusion.1 = (f32[384,2048]{1,0:T(8,128)}, bf16[384,2048]{1,0:T(8,128)(2,1)}) fusion(bf16[384,2048]{1,0:T(8,128)(2,1)S(1)} %copy-done.3, bf16[384,2048]{1,0:T(8,128)(2,1)} %get-tuple-element.61, f32[384]{0:T(512)S(1)} %fusion.2, f32[384]{0:T(512)S(1)} %copy-done.15, f32[2048]{0:T(1024)S(1)} %copy-done.13, f32[384]{0:T(512)S(1)} %get-tuple-element.121, ...), kind=kLoop, calls=%fused_computation.4 | loop fusion | flops 15728640 | bytes 15754240 | tf_op jit(solution)/shard_map/sub | solution.py:1698
  482.5 2.1 copy.71
  484.6 1.6 copy-done.6
  486.2 2.1 copy.72
  488.3 1.6 copy-done.5
  489.9 2.0 copy.73
  (71 shorter events, 14.3 us)
Async XLA Ops:
  7.2 6.0 %copy-start.12 = (s32[384,8]{0,1:T(8,128)S(1)}, s32[384,8]{0,1:T(8,128)}, u32[]{:S(2)}) copy-start(s32[384,8]{0,1:T(8,128)} %param.27) | copy-start | bytes 36868
  7.2 150.6 %all-gather.3.cloned.1.call-start = ((), (), s32[]{:S(2)}) async-start(), calls=%async_computation | async-start | bytes 14155776 | tf_op jit(solution)/shard_map/all_gather | solution.py:1647
  9.6 279.0 %copy-start.11 = (pred[384,16]{1,0:T(32,128)(4,1)}, pred[384,16]{1,0:T(32,128)(4,1)S(1)}, u32[]{:S(2)}) copy-start(pred[384,16]{1,0:T(32,128)(4,1)S(1)} %copy.57) | copy-start | bytes 18436
  15.8 135.2 %copy-start.9 = (bf16[2048,16]{0,1:T(8,128)(2,1)S(1)}, bf16[2048,16]{0,1:T(8,128)(2,1)}, u32[]{:S(2)}) copy-start(bf16[2048,16]{0,1:T(8,128)(2,1)} %param.23) | copy-start | bytes 196612
  150.1 5.5 %copy-start.8 = (f32[384,128]{1,0:T(8,128)S(1)}, f32[384,128]{1,0:T(8,128)}, u32[]{:S(2)}) copy-start(f32[384,128]{1,0:T(8,128)} %get-tuple-element.42.stats) | copy-start | bytes 589828
  155.6 133.0 %copy-start.16 = (f32[384]{0:T(512)}, f32[384]{0:T(512)S(1)}, u32[]{:S(2)}) copy-start(f32[384]{0:T(512)S(1)} %fusion.9) | copy-start | bytes 4612
  157.8 132.7 %copy-start.2 = (bf16[384,2048]{1,0:T(8,128)(2,1)S(1)}, bf16[384,2048]{1,0:T(8,128)(2,1)}, u32[]{:S(2)}) copy-start(bf16[384,2048]{1,0:T(8,128)(2,1)} %tokens.1) | copy-start | bytes 4718596
  157.8 132.7 %copy-start.10 = (bf16[2048,16]{0,1:T(8,128)(2,1)S(1)}, bf16[2048,16]{0,1:T(8,128)(2,1)}, u32[]{:S(2)}) copy-start(bf16[2048,16]{0,1:T(8,128)(2,1)} %param.23) | copy-start | bytes 196612
  157.8 132.7 %copy-start.14 = (f32[2048]{0:T(1024)S(1)}, f32[2048]{0:T(1024)}, u32[]{:S(2)}) copy-start(f32[2048]{0:T(1024)} %param.21) | copy-start | bytes 24580
  290.5 5.1 %copy-start = (bf16[384,2048]{1,0:T(8,128)(2,1)S(1)}, bf16[384,2048]{1,0:T(8,128)(2,1)}, u32[]{:S(2)}) copy-start(bf16[384,2048]{1,0:T(8,128)(2,1)} %param.29) | copy-start | bytes 4718596
  464.2 7.3 %copy-start.3 = (bf16[384,2048]{1,0:T(8,128)(2,1)S(1)}, bf16[384,2048]{1,0:T(8,128)(2,1)}, u32[]{:S(2)}) copy-start(bf16[384,2048]{1,0:T(8,128)(2,1)} %tokens.1) | copy-start | bytes 4718596
  464.3 7.3 %copy-start.4 = (bf16[384,2048]{1,0:T(8,128)(2,1)S(1)}, bf16[384,2048]{1,0:T(8,128)(2,1)}, u32[]{:S(2)}) copy-start(bf16[384,2048]{1,0:T(8,128)(2,1)} %get-tuple-element.61) | copy-start | bytes 4718596
  464.3 7.3 %copy-start.13 = (f32[2048]{0:T(1024)S(1)}, f32[2048]{0:T(1024)}, u32[]{:S(2)}) copy-start(f32[2048]{0:T(1024)} %param.20) | copy-start | bytes 24580
  470.7 5.4 %copy-start.1 = (bf16[384,2048]{1,0:T(8,128)(2,1)S(1)}, bf16[384,2048]{1,0:T(8,128)(2,1)}, u32[]{:S(2)}) copy-start(bf16[384,2048]{1,0:T(8,128)(2,1)} %param.29) | copy-start | bytes 4718596
  470.7 5.4 %copy-start.15 = (f32[384]{0:T(512)S(1)}, f32[384]{0:T(512)}, u32[]{:S(2)}) copy-start(f32[384]{0:T(512)} %get-tuple-element.123) | copy-start | bytes 4612
  476.1 6.3 %copy-start.7 = (f32[2,2048,256]{2,1,0:T(8,128)S(1)}, f32[2,2048,256]{2,1,0:T(8,128)}, u32[]{:S(2)}) copy-start(f32[2,2048,256]{2,1,0:T(8,128)} %get-tuple-element.164) | copy-start | bytes 12582916
  482.5 3.7 copy-start.6
  486.2 3.7 copy-start.5
Sparse Core Ops, SparseCore 0:
  9.9 89.3 all-gather.2

commit v7 on v6

--- a/solution.py
+++ b/solution.py
@@ -49,17 +49,27 @@
 
 
 class Line:
-    def __init__(self, own, arrived, total, sems):
-        self.own, self.arrived, self.total = own, arrived, total
-        self.up_sent, self.up_got, self.down_sent, self.down_got = (sems.at[i] for i in range(4))
+    def __init__(self, own, arrived, spare, total, sems, step=STEP):
+        self.step = step
+        self.own, self.arrived, self.spare, self.total = own, arrived, spare, total
+        self.up_sent, self.far_got, self.near_got, self.far_sent, self.near_sent, self.down_got = (
+            sems.at[i] for i in range(6)
+        )
         self.size = lax.axis_size("tensor")
         self.here = lax.axis_index("tensor")
+        self.root = self.size // 2 - 1
+        self.rise_steps = self.size - 1 - self.root
+        self.trip = 2 * self.rise_steps
         self.half = own.shape[0] // 2
-        self.pieces = self.half // STEP
+        self.pieces = self.half // step
 
     @staticmethod
-    def semaphores(rows):
-        return pltpu.SemaphoreType.DMA((4, 2, rows // 2 // STEP))
+    def semaphores(rows, step=STEP):
+        return pltpu.SemaphoreType.DMA((6, 2, rows // 2 // step))
+
+    @staticmethod
+    def spare_shape(rows, width):
+        return pltpu.VMEM((rows // 2, width), jnp.bfloat16)
 
     def neighbours(self):
         here, size = self.here, self.size
@@ -68,95 +78,130 @@
             (here < size - 1, {"tensor": jnp.minimum(here + 1, size - 1)}),
         ]
 
-    def lane(self, lane):
-        here, size = self.here, self.size
-        if lane == 0:
-            return here, here + 1, here - 1
-        return size - 1 - here, here - 1, here + 1
+    def place(self, lane):
+        return self.here if lane == 0 else self.size - 1 - self.here
+
+    def device(self, lane, place):
+        return place if lane == 0 else self.size - 1 - place
 
     def rows(self, lane, piece):
-        return pl.ds(pl.multiple_of(lane * self.half + piece * STEP, STEP), STEP)
-
-    def up_copy(self, lane, piece):
-        rows = self.rows(lane, piece)
-        onward = self.lane(lane)[1]
+        return pl.ds(pl.multiple_of(lane * self.half + piece * self.step, self.step), self.step)
+
+    def landing(self, piece):
+        return pl.ds(pl.multiple_of(piece * self.step, self.step), self.step)
+
+    def far_up(self, lane, piece):
+        rows, place = self.rows(lane, piece), self.place(lane)
+        inward = jnp.where(place > self.root, place - 1, place + 1)
         return remote(
             self.own.at[rows], self.arrived.at[rows],
-            self.up_sent.at[lane, piece], self.up_got.at[lane, piece], tensor=onward,
-        )
-
-    def down_copy(self, lane, piece):
+            self.up_sent.at[lane, piece], self.far_got.at[lane, piece], tensor=self.device(lane, inward),
+        )
+
+    def near_up(self, lane, piece):
+        return remote(
+            self.own.at[self.rows(lane, piece)], self.spare.at[self.landing(piece)],
+            self.up_sent.at[lane, piece], self.near_got.at[lane, piece], tensor=self.device(lane, self.root),
+        )
+
+    def down(self, lane, piece, away):
         rows = self.rows(lane, piece)
-        back = self.lane(lane)[2]
+        sent = self.far_sent if away == 1 else self.near_sent
         return remote(
             self.total.at[rows], self.total.at[rows],
-            self.down_sent.at[lane, piece], self.down_got.at[lane, piece], tensor=back,
+            sent.at[lane, piece], self.down_got.at[lane, piece], tensor=self.device(lane, self.place(lane) + away),
         )
 
     def rise(self, lane, piece):
-        place = self.lane(lane)[0]
+        place, root = self.place(lane), self.root
         rows = self.rows(lane, piece)
 
-        @pl.when(place > 0)
-        def _():
-            self.up_copy(lane, piece).wait_recv()
-            summed = (
-                self.own[rows].astype(jnp.float32) + self.arrived[rows].astype(jnp.float32)
-            ).astype(jnp.bfloat16)
-
-            @pl.when(place < self.size - 1)
+        def value(field):
+            return field.astype(jnp.float32)
+
+        @pl.when((place > root) & (place < self.size - 1) | (place > 0) & (place < root))
+        def _():
+            self.far_up(lane, piece).wait_recv()
+            self.own[rows] = (value(self.own[rows]) + value(self.arrived[rows])).astype(jnp.bfloat16)
+
+        @pl.when(place == root)
+        def _():
+            self.far_up(lane, piece).wait_recv()
+            summed = value(self.own[rows]) + value(self.arrived[rows])
+            if root > 0:
+                self.near_up(lane, piece).wait_recv()
+                summed = summed + value(self.spare[self.landing(piece)])
+            self.total[rows] = summed.astype(jnp.bfloat16)
+            self.down(lane, piece, 1).start()
+            if root > 0:
+                self.down(lane, piece, -1).start()
+
+        if root > 0:
+
+            @pl.when(place == root - 1)
             def _():
-                self.own[rows] = summed
-
-            @pl.when(place == self.size - 1)
+                self.near_up(lane, piece).start()
+
+        @pl.when((place > root) | (place < root - 1))
+        def _():
+            self.far_up(lane, piece).start()
+
+    def fall(self, lane, piece):
+        place, root = self.place(lane), self.root
+
+        @pl.when(place != root)
+        def _():
+            self.down(lane, piece, 1).wait_recv()
+
+        @pl.when((place > root) & (place < self.size - 1))
+        def _():
+            self.down(lane, piece, 1).start()
+
+        @pl.when((place > 0) & (place < root))
+        def _():
+            self.down(lane, piece, -1).start()
+
+    def advance(self, step):
+        for lane in range(2):
+            place = self.place(lane)
+            steps_in = self.rise_steps - jnp.abs(place - self.root)
+            piece = step - steps_in
+
+            @pl.when((piece >= 0) & (piece < self.pieces))
             def _():
-                self.total[rows] = summed
-                self.down_copy(lane, piece).start()
-
-        @pl.when(place < self.size - 1)
-        def _():
-            self.up_copy(lane, piece).start()
-
-    def fall(self, lane, piece):
-        place = self.lane(lane)[0]
-
-        @pl.when(place < self.size - 1)
-        def _():
-            self.down_copy(lane, piece).wait_recv()
-
-            @pl.when(place > 0)
+                self.rise(lane, piece)
+
+        for lane in range(2):
+            place = self.place(lane)
+            piece = step - self.rise_steps - jnp.abs(place - self.root)
+
+            @pl.when((piece >= 0) & (piece < self.pieces))
             def _():
-                self.down_copy(lane, piece).start()
-
-    def advance(self, step, skew=1):
-        for act, far in ((self.rise, False), (self.fall, True)):
-            for lane in range(2):
-                place = self.lane(lane)[0]
-                piece = step - skew * (2 * (self.size - 1) - place if far else place)
-
-                @pl.when((piece >= 0) & (piece < self.pieces))
-                def _():
-                    act(lane, piece)
+                self.fall(lane, piece)
 
     def step_body(self, step, carry):
         self.advance(step)
         return carry
 
-    def steps(self, skew=1):
-        return self.pieces + skew * 2 * (self.size - 1)
+    def steps(self):
+        return self.pieces + self.trip
 
     def finish(self):
         def one(piece, carry):
             for lane in range(2):
-                place = self.lane(lane)[0]
-
-                @pl.when(place < self.size - 1)
+                place, root = self.place(lane), self.root
+
+                @pl.when(place != root)
                 def _():
-                    self.up_copy(lane, piece).wait_send()
-
-                @pl.when(place > 0)
+                    self.far_up(lane, piece).wait_send()
+
+                @pl.when((place >= root) & (place < self.size - 1))
                 def _():
-                    self.down_copy(lane, piece).wait_send()
+                    self.down(lane, piece, 1).wait_send()
+
+                @pl.when((place <= root) & (place > 0))
+                def _():
+                    self.down(lane, piece, -1).wait_send()
             return carry
 
         lax.fori_loop(0, self.pieces, one, 0)
@@ -181,17 +226,18 @@
 
 
 class Plane(Place):
-    def __init__(self, own, spare, paired, from_x, from_y, pair_sems, x_sems, y_sems, by_device=False):
+    def __init__(self, own, spare, paired, from_x, from_y, pair_sems, x_sems, y_sems, by_device=False, step=STEP):
+        self.step = step
         self.by_device = by_device
         self.own, self.spare, self.paired, self.from_x, self.from_y = own, spare, paired, from_x, from_y
         self.pair_sems, self.x_sems, self.y_sems = pair_sems, x_sems, y_sems
         super().__init__()
         self.half = own.shape[1] // 2
-        self.pieces = self.half // STEP
+        self.pieces = self.half // step
 
     @staticmethod
-    def semaphores(rows):
-        pieces = rows // 2 // STEP
+    def semaphores(rows, step=STEP):
+        pieces = rows // 2 // step
         return [
             pltpu.SemaphoreType.DMA((2, 4)),
             pltpu.SemaphoreType.DMA((2, 3, pieces)),
@@ -206,10 +252,10 @@
         )
 
     def rows(self, side, piece):
-        return pl.ds(pl.multiple_of(side * self.half + piece * STEP, STEP), STEP)
+        return pl.ds(pl.multiple_of(side * self.half + piece * self.step, self.step), self.step)
 
     def landing(self, piece):
-        return pl.ds(pl.multiple_of(piece * STEP, STEP), STEP)
+        return pl.ds(pl.multiple_of(piece * self.step, self.step), self.step)
 
     def x_copy(self, kind, piece):
         chip, side = ((0, 0), (1, 0), (1, 1))[kind]
@@ -248,6 +294,13 @@
                 self.y_copy(chip // 2, piece).start()
 
         self.each(step)
+
+    def first_piece(self, piece):
+        for chip, side in ((0, 0), (0, 1), (1, 0), (2, 1)):
+            self.add_pair(chip, side, piece)
+        for kind in range(2):
+            self.x_copy(kind, piece).start()
+            self.y_copy(kind, piece).start()
 
     def second_piece(self, piece):
         landed = self.landing(piece)
@@ -401,17 +454,20 @@
     return lax.dot_general(left, right, (((1,), (1,)), ((), ())), preferred_element_type=jnp.float32)
 
 
+BLOCK_STEP = 32
+
+
 def expert_kernel(
     x_all, g_all, mask, router, bias, w_gate, w_up, w_down,
     reduced, gated_all, gate_all, up_all, mixed_all,
-    x_buf, g_buf, part, paired, from_x, from_y, line_in, small, mixed,
+    x_buf, g_buf, part, paired, from_x, from_y, line_in, line_spare, small, mixed,
     in_sems, out_sems, pair_sems, x_sems, y_sems, line_sems,
 ):
     experts, width, hidden = w_gate.shape
     rows = x_buf.shape[1]
     tile = min(512, width)
-    plane = Plane(part.at[1], part.at[0], paired, from_x, from_y, pair_sems, x_sems, y_sems)
-    line = Line(part.at[1, 3], line_in, reduced, line_sems)
+    plane = Plane(part.at[1], part.at[0], paired, from_x, from_y, pair_sems, x_sems, y_sems, step=BLOCK_STEP)
+    line = Line(part.at[1, 3], line_in, line_spare, reduced, line_sems, step=BLOCK_STEP)
     first_expert = lax.axis_index("expert") * experts
     outs = (gated_all, gate_all, up_all)
 
@@ -560,12 +616,13 @@
             pltpu.VMEM((3, half, wide), low),
             pltpu.VMEM((3, half, wide), low),
             pltpu.VMEM((rows, wide), low),
+            Line.spare_shape(rows, wide),
             pltpu.VMEM((2, 3, rows, inner), low),
             pltpu.VMEM((2, rows, width), low),
             pltpu.SemaphoreType.DMA((2, 2)),
             pltpu.SemaphoreType.DMA((4, 2)),
-            *Plane.semaphores(rows),
-            Line.semaphores(rows),
+            *Plane.semaphores(rows, step=BLOCK_STEP),
+            Line.semaphores(rows, step=BLOCK_STEP),
         ],
         compiler_params=pltpu.CompilerParams(
             collective_id=0, has_side_effects=True, vmem_limit_bytes=61 * 2**20
@@ -584,8 +641,8 @@
     normed, query_grad, key_grad, value_grad, attended, attention_grad, extras,
     w_query, w_key, w_value, mixed, x_all, g_all, gated_all, gate_all, up_all,
     total, sums, gain, mixture, gate_out, up_out, down_out,
-    line_own, line_in, part, paired, from_x, from_y,
-    mix_own, mix_paired, mix_x, mix_y, mix_in, tiles, factors, results, downs,
+    line_own, line_in, line_spare, part, paired, from_x, from_y,
+    mix_own, mix_paired, mix_x, mix_y, mix_in, mix_spare, tiles, factors, results, downs,
     line_sems, pair_sems, x_sems, y_sems, mix_line_sems, mix_pair_sems, mix_x_sems, mix_y_sems,
     load_sems, weight_sems, factor_sems, tile_sems, out_sems,
     gains, mine, theirs, peer_sent, peer_got,
@@ -599,10 +656,10 @@
     column_tile = min(512, width // 2)
     tile = tiles.shape[2]
     count = width // tile
-    line = Line(line_own, line_in, total, line_sems)
+    line = Line(line_own, line_in, line_spare, total, line_sems)
     plane = Plane(part.at[1], part.at[0], paired, from_x, from_y, pair_sems, x_sems, y_sems)
     mix = Plane(mix_own, mixed, mix_paired, mix_x, mix_y, mix_pair_sems, mix_x_sems, mix_y_sems, by_device=True)
-    mix_line = Line(mix_own.at[3], mix_in, mixture, mix_line_sems)
+    mix_line = Line(mix_own.at[3], mix_in, mix_spare, mixture, mix_line_sems)
     peers = Peers(mine, theirs, peer_sent, peer_got)
     half = width // 2
 
@@ -742,25 +799,26 @@
     factor_load(0).start()
     factor_load(1).start()
     start_tile(0)
-    mix_last = mix.pieces + 1
-    dense_first = 8 + 5
-    dense_second = dense_first + plane.pieces // 2 + 2
-    dense_last = dense_second + plane.pieces // 2 + 1
+    mix_second, mix_last, dense_first, dense_second, dense_last = PLAN
 
     def step(s, carry):
         line.advance(s)
-        for chip in range(4):
-
-            @pl.when(s == chip)
-            def _():
+
+        @pl.when(s == 0)
+        def _():
+            for chip in range(4):
                 load_own(chip).wait()
                 mix.pair_copy(chip).wait_recv()
-                if chip < 3:
-                    mix.send_first(chip)
-
-        @pl.when((s >= 3) & (s - 3 < mix.pieces))
-        def _():
-            mix.second_piece(s - 3)
+            for piece in range(AHEAD):
+                mix.first_piece(piece)
+
+        @pl.when((s > 0) & (s + AHEAD - 1 < mix.pieces))
+        def _():
+            mix.first_piece(s + AHEAD - 1)
+
+        @pl.when((s >= mix_second) & (s - mix_second < mix.pieces))
+        def _():
+            mix.second_piece(s - mix_second)
 
         @pl.when((s >= mix_last) & (s - mix_last < mix.pieces))
         def _():
@@ -813,6 +871,8 @@
         each.finish()
 
 
+PLAN = (1, 3, 12, 15, 18)
+AHEAD = 2
 TILE = 256
 
 
@@ -848,6 +908,7 @@
         scratch_shapes=[
             pltpu.VMEM((rows, width), low),
             pltpu.VMEM((rows, width), low),
+            Line.spare_shape(rows, width),
             pltpu.VMEM((2, 4, share, wide), low),
             pltpu.VMEM((4, share, wide), low),
             pltpu.VMEM((3, share // 2, wide), low),
@@ -857,6 +918,7 @@
             pltpu.VMEM((3, rows // 2, width), low),
             pltpu.VMEM((3, rows // 2, width), low),
             pltpu.VMEM((rows, width), low),
+            Line.spare_shape(rows, width),
             pltpu.VMEM((2, every, tile), low),
             pltpu.VMEM((2, every, inner), low),
             pltpu.VMEM((2, tile, inner), jnp.float32),
@@ -945,7 +1007,7 @@
 def front_kernel(
     tokens, attn_gain, ffn_gain, w_query, w_key, w_value, w_out, qk_gain, cosine, sine, bias, routes,
     total, normed, normed_two, attended, query_rot, keys_values, query_raw, key_raw, stats, routes_all, arrived,
-    line_own, line_in, prompt, mine, theirs, two,
+    line_own, line_in, line_spare, prompt, mine, theirs, two,
     line_sems, peer_sent, peer_got, *gather_sems,
 ):
     rows, width = tokens.shape
@@ -955,7 +1017,7 @@
     own_blocks = rows // PROMPT_DEV - 1
     devices = keys_values.shape[0] - own_blocks
     place = Place()
-    line = Line(line_own, line_in, total, line_sems)
+    line = Line(line_own, line_in, line_spare, total, line_sems)
     peers = Peers(mine, theirs, peer_sent, peer_got)
     names = Gather(routes, routes_all, place, *gather_sems[0:5], pieces=2)
     prompts = Gather(prompt, keys_values, place, *gather_sems[5:10], pieces=2)
@@ -1029,7 +1091,6 @@
     for start in range(0, width, tile):
         columns = slice(start, start + tile)
         line_own[:, columns] = wide_dot(attended[...], w_out[:, columns]).astype(jnp.bfloat16)
-    steps = line.pieces + 2 * (line.size - 1)
     ratio = SPREAD // STEP
     groups = line.pieces // ratio
 
@@ -1043,7 +1104,7 @@
     done = 0
     passed = 0
     for group in range(groups):
-        ready = 2 * (line.size - 1) + (group + 1) * ratio
+        ready = line.trip + (group + 1) * ratio
         lax.fori_loop(done, ready, line.step_body, 0)
         done = ready
         for piece in (group, groups + group):
@@ -1098,6 +1159,7 @@
         scratch_shapes=[
             pltpu.VMEM((rows, width), low),
             pltpu.VMEM((rows, width), low),
+            Line.spare_shape(rows, width),
             pltpu.VMEM((PROMPT_DEV, 2 * local), low),
             pltpu.VMEM((8, rows), full),
             pltpu.VMEM((size - 1, 8, rows), full),

time: 504 us -> 489 us (0.970)
  Pallas kernels: 426 us -> 413 us
    pallas_call x1, Pallas kernels: 130 us -> 121 us  [experts_fused(): pl.pallas_call(expert_kernel, out_shape=(jax.ShapeDtypeStruct((rows, wide...]
  transfers between devices with their start and end apart: 1 -> 1, of which waited for: 0 -> 0; matrix products, arithmetic and copies ran while one was open for 3% -> 3% of each run, Pallas kernels for 27% -> 28%
where the time goes in v7:
time: 489 us; the launch traced here: 486 us
  Pallas kernels  413 us (84%)
  local copies, waits for them, and re-layouts  25.1 us (5%)
  other arithmetic  23.2 us (5%)
  between operations  15.2 us (3%)
  matrix products  8.93 us (2%)
    pallas_call x1, Pallas kernels, front(): pl.pallas_call(front_kernel, out_shape=(jax.ShapeDtypeStruct((rows, width...  135 us
    pallas_call x1, Pallas kernels, closing(): pl.pallas_call(functools.partial(closing_kernel, gain_column=gain_column)...  125 us
    pallas_call x1, Pallas kernels, experts_fused(): pl.pallas_call(expert_kernel, out_shape=(jax.ShapeDtypeStruct((rows, wide...  121 us
    pallas_call x1, Pallas kernels, backward(): pl.pallas_call(backward_kernel, out_shape=(small, small, small, jax.Shape...  32.2 us
    unnamed x42, local copies, waits for them, and re-layouts  13.1 us
  transfers between devices with their start and end apart: 1, of which 0 were waited for; matrix products, arithmetic and copies ran while one was open for 3% of the time, Pallas kernels for 28%

profile of v7, /device:TPU:0, one launch (start us, length us, event | category | flops | bytes accessed | tf_op | source)
XLA Modules:
  0.0 485.9 jit_solution(13205458055592628235)
XLA Ops:
  9.6 0.9 fusion.12
  14.4 1.5 add_select_fusion.bias
  15.8 135.1 %shard_map.246 = (bf16[384,2048]{1,0:T(8,128)(2,1)}, bf16[384,2048]{1,0:T(8,128)(2,1)}, bf16[384,2048]{1,0:T(8,128)(2,1)}, bf16[384,512]{1,0:T(8,128)(2,1)}, bf1...) custom-call(bf16[384,2048]{1,0:T(8,128)(2,1)} %tokens.1, ...), custom_call_target="tpu_custom_call" | custom-call | flops 99999997952 | bytes 200000000 | tf_op jit(solution)/shard_map/pallas_call | solution.py:1142
  151.0 0.9 slice.48
  151.9 1.9 fusion.31
  154.8 0.9 pad.21.router
  157.4 1.3 pad_convert_fusion.mask
  158.7 120.8 %shard_map.247 = (bf16[384,2176]{1,0:T(8,128)(2,1)}, bf16[8,384,512]{2,1,0:T(8,128)(2,1)}, bf16[8,384,512]{2,1,0:T(8,128)(2,1)}, bf16[8,384,512]{2,1,0:T(8,128)(2,1)}, bf16[8,384,2048]{2,1,0:T(8,128)(2,1)}) custom-call(bf16[8,384,2048]{2,1,0:T(8,128)(2,1)} %get-tuple-element.43.x_all, bf16[8,384,2048]{2,1,0:T(8,128)(2,1)} %bitcast.26, ...), custom_call_target="tpu_custom_call" | custom-call | flops 38654705664 | bytes 50331648 | tf_op jit(solution)/shard_map/pallas_call | solution.py:603
  279.4 1.2 multiply_reduce_fusion.2
  280.6 1.9 convolution_convert_fusion
  282.6 5.1 %multiply_reduce_fusion = (bf16[2048]{0:T(1024)(128)(2,1)S(1)}, f32[384]{0:T(512)S(1)}, f32[384,2048]{1,0:T(8,128)}) fusion(bf16[384,2048]{1,0:T(8,128)(2,1)} %get-tuple-element.40, bf16[384,2048]{1,0:T(8,128)(2,1)S(1)} %copy-done.2, f32[384]{0:T(512)S(1)} %get-tuple-element.124, f32[2048]{0:T(1024)S(1)} %copy-done.14, bf16[2048,16]{0,1:T(8,128)(2,1)S(1)} %copy-done.10, ...), kind=kOutput, calls=%fused_computation.8 | convolution fusion | flops 33857152 | bytes 8078848 | tf_op jit(solution)/shard_map/te,de->td/dot_general | solution.py:1728
  287.7 4.6 fusion.30.attention_grad
  292.3 32.2 %shard_map.248 = (bf16[384,512]{1,0:T(8,128)(2,1)}, bf16[384,512]{1,0:T(8,128)(2,1)}, bf16[384,512]{1,0:T(8,128)(2,1)}, f32[2,512]{1,0:T(2,128)}) custom-call(bf16[384,2048]{1,0:T(8,128)(2,1)} %fusion.30.attention_grad, bf16[512,2048]{1,0:T(8,128)(2,1)} %w_out.3, bf16[384,512]{1,0:T(8,128)(2,1)} %get-tuple-element.47.query_rot, ...), custom_call_target="tpu_custom_call" | custom-call | tf_op jit(solution)/shard_map/pallas_call | solution.py:1270
  326.5 124.7 %shard_map.249 = (bf16[384,2048]{1,0:T(8,128)(2,1)}, f32[256,2176]{1,0:T(8,128)}, f32[8,256]{1,0:T(8,128)}, bf16[384,2048]{1,0:T(8,128)(2,1)}, f32[2,2048,256]{2...) custom-call(bf16[384,2048]{1,0:T(8,128)(2,1)} %get-tuple-element.41.normed, ...), custom_call_target="tpu_custom_call" | custom-call | tf_op jit(solution)/shard_map/pallas_call | solution.py:895
  451.2 1.8 slice_reduce_fusion.2
  453.9 0.9 slice.59
  454.8 2.9 slice_bitcast_fusion
  460.4 2.0 copy.59
  463.1 6.3 %fusion.1 = (f32[384,2048]{1,0:T(8,128)}, bf16[384,2048]{1,0:T(8,128)(2,1)}) fusion(bf16[384,2048]{1,0:T(8,128)(2,1)S(1)} %copy-done.3, bf16[384,2048]{1,0:T(8,128)(2,1)} %get-tuple-element.61, f32[384]{0:T(512)S(1)} %fusion.2, f32[384]{0:T(512)S(1)} %copy-done.15, f32[2048]{0:T(1024)S(1)} %copy-done.13, f32[384]{0:T(512)S(1)} %get-tuple-element.121, ...), kind=kLoop, calls=%fused_computation.4 | loop fusion | flops 15728640 | bytes 15754240 | tf_op jit(solution)/shard_map/sub | solution.py:1760
  469.4 2.1 copy.71
  471.6 1.6 copy-done.6
  473.1 2.1 copy.72
  475.3 1.6 copy-done.5
  476.8 2.0 copy.73
  (71 shorter events, 14.3 us)
Async XLA Ops:
  7.2 6.0 %copy-start.12 = (s32[384,8]{0,1:T(8,128)S(1)}, s32[384,8]{0,1:T(8,128)}, u32[]{:S(2)}) copy-start(s32[384,8]{0,1:T(8,128)} %param.27) | copy-start | bytes 36868
  7.2 151.5 %all-gather.3.cloned.1.call-start = ((), (), s32[]{:S(2)}) async-start(), calls=%async_computation | async-start | bytes 14155776 | tf_op jit(solution)/shard_map/all_gather | solution.py:1709
  9.6 271.1 %copy-start.11 = (pred[384,16]{1,0:T(32,128)(4,1)}, pred[384,16]{1,0:T(32,128)(4,1)S(1)}, u32[]{:S(2)}) copy-start(pred[384,16]{1,0:T(32,128)(4,1)S(1)} %copy.57) | copy-start | bytes 18436
  15.8 136.1 %copy-start.9 = (bf16[2048,16]{0,1:T(8,128)(2,1)S(1)}, bf16[2048,16]{0,1:T(8,128)(2,1)}, u32[]{:S(2)}) copy-start(bf16[2048,16]{0,1:T(8,128)(2,1)} %param.23) | copy-start | bytes 196612
  151.0 5.5 %copy-start.8 = (f32[384,128]{1,0:T(8,128)S(1)}, f32[384,128]{1,0:T(8,128)}, u32[]{:S(2)}) copy-start(f32[384,128]{1,0:T(8,128)} %get-tuple-element.42.stats) | copy-start | bytes 589828
  156.5 124.1 %copy-start.16 = (f32[384]{0:T(512)}, f32[384]{0:T(512)S(1)}, u32[]{:S(2)}) copy-start(f32[384]{0:T(512)S(1)} %fusion.9) | copy-start | bytes 4612
  158.7 123.9 %copy-start.2 = (bf16[384,2048]{1,0:T(8,128)(2,1)S(1)}, bf16[384,2048]{1,0:T(8,128)(2,1)}, u32[]{:S(2)}) copy-start(bf16[384,2048]{1,0:T(8,128)(2,1)} %tokens.1) | copy-start | bytes 4718596
  158.7 123.9 %copy-start.10 = (bf16[2048,16]{0,1:T(8,128)(2,1)S(1)}, bf16[2048,16]{0,1:T(8,128)(2,1)}, u32[]{:S(2)}) copy-start(bf16[2048,16]{0,1:T(8,128)(2,1)} %param.23) | copy-start | bytes 196612
  158.7 123.9 %copy-start.14 = (f32[2048]{0:T(1024)S(1)}, f32[2048]{0:T(1024)}, u32[]{:S(2)}) copy-start(f32[2048]{0:T(1024)} %param.21) | copy-start | bytes 24580
  282.6 5.1 %copy-start = (bf16[384,2048]{1,0:T(8,128)(2,1)S(1)}, bf16[384,2048]{1,0:T(8,128)(2,1)}, u32[]{:S(2)}) copy-start(bf16[384,2048]{1,0:T(8,128)(2,1)} %param.29) | copy-start | bytes 4718596
  451.2 7.3 %copy-start.3 = (bf16[384,2048]{1,0:T(8,128)(2,1)S(1)}, bf16[384,2048]{1,0:T(8,128)(2,1)}, u32[]{:S(2)}) copy-start(bf16[384,2048]{1,0:T(8,128)(2,1)} %tokens.1) | copy-start | bytes 4718596
  451.2 7.3 %copy-start.4 = (bf16[384,2048]{1,0:T(8,128)(2,1)S(1)}, bf16[384,2048]{1,0:T(8,128)(2,1)}, u32[]{:S(2)}) copy-start(bf16[384,2048]{1,0:T(8,128)(2,1)} %get-tuple-element.61) | copy-start | bytes 4718596
  451.2 7.3 %copy-start.13 = (f32[2048]{0:T(1024)S(1)}, f32[2048]{0:T(1024)}, u32[]{:S(2)}) copy-start(f32[2048]{0:T(1024)} %param.20) | copy-start | bytes 24580
  457.7 5.4 %copy-start.1 = (bf16[384,2048]{1,0:T(8,128)(2,1)S(1)}, bf16[384,2048]{1,0:T(8,128)(2,1)}, u32[]{:S(2)}) copy-start(bf16[384,2048]{1,0:T(8,128)(2,1)} %param.29) | copy-start | bytes 4718596
  457.7 5.4 %copy-start.15 = (f32[384]{0:T(512)S(1)}, f32[384]{0:T(512)}, u32[]{:S(2)}) copy-start(f32[384]{0:T(512)} %get-tuple-element.123) | copy-start | bytes 4612
  463.1 6.3 %copy-start.7 = (f32[2,2048,256]{2,1,0:T(8,128)S(1)}, f32[2,2048,256]{2,1,0:T(8,128)}, u32[]{:S(2)}) copy-start(f32[2,2048,256]{2,1,0:T(8,128)} %get-tuple-element.164) | copy-start | bytes 12582916
  469.4 3.7 copy-start.6
  473.1 3.7 copy-start.5
Sparse Core Ops, SparseCore 0:
  9.9 96.5 all-gather.2

commit v8 on v7

--- a/solution.py
+++ b/solution.py
@@ -729,7 +729,7 @@
                 for copy in across(gate_out, s):
                     copy.wait()
 
-            results[s % 2] = crossed_dot(tiles[s % 2], factors[s // count])
+            results[s % 2] = crossed_dot(tiles[s % 2], factors[s // count]).astype(jnp.bfloat16)
 
             @pl.when(s < count)
             def _():
@@ -748,7 +748,7 @@
                 for copy in down(s):
                     copy.wait()
 
-            downs[s % 2] = crossed_dot(factors[0], tiles[s % 2])
+            downs[s % 2] = crossed_dot(factors[0], tiles[s % 2]).astype(jnp.bfloat16)
             for copy in down(s):
                 copy.start()
 
@@ -806,11 +806,16 @@
 
         @pl.when(s == 0)
         def _():
-            for chip in range(4):
+            for chip in range(3):
                 load_own(chip).wait()
                 mix.pair_copy(chip).wait_recv()
             for piece in range(AHEAD):
                 mix.first_piece(piece)
+
+        @pl.when(s == mix_last - 1)
+        def _():
+            load_own(3).wait()
+            mix.pair_copy(3).wait_recv()
 
         @pl.when((s > 0) & (s + AHEAD - 1 < mix.pieces))
         def _():
@@ -899,9 +904,9 @@
             jax.ShapeDtypeStruct((share, wide), jnp.float32),
             jax.ShapeDtypeStruct((8, share), jnp.float32),
             jax.ShapeDtypeStruct((rows, width), low),
-            jax.ShapeDtypeStruct((experts, width, hidden), jnp.float32),
-            jax.ShapeDtypeStruct((experts, width, hidden), jnp.float32),
-            jax.ShapeDtypeStruct((experts, hidden, width), jnp.float32),
+            jax.ShapeDtypeStruct((experts, width, hidden), low),
+            jax.ShapeDtypeStruct((experts, width, hidden), low),
+            jax.ShapeDtypeStruct((experts, hidden, width), low),
         ),
         in_specs=[vmem] * 7 + [any_space] * 9,
         out_specs=(vmem,) * 4 + (any_space,) * 3,
@@ -921,8 +926,8 @@
             Line.spare_shape(rows, width),
             pltpu.VMEM((2, every, tile), low),
             pltpu.VMEM((2, every, inner), low),
-            pltpu.VMEM((2, tile, inner), jnp.float32),
-            pltpu.VMEM((2, inner, tile), jnp.float32),
+            pltpu.VMEM((2, tile, inner), low),
+            pltpu.VMEM((2, inner, tile), low),
             Line.semaphores(rows),
             *Plane.semaphores(share),
             Line.semaphores(rows),
@@ -1179,10 +1184,13 @@
 
 
 def backward_kernel(
-    attention_grad, w_out, query_rot, keys_values, bias, stats, query_raw, key_raw, cosine, sine, qk_gain,
-    query_out, key_out, value_out, gain_out,
+    reduced, tokens, attention, cotangent, normed_two, router, expert_bias, routed, ffn_gain,
+    w_out, query_rot, keys_values, bias, stats, query_raw, key_raw, cosine, sine, qk_gain,
+    query_out, key_out, value_out, gain_out, hidden_grad, attention_grad, extras,
     out_grad, query_grad, prompt_grads, own_grads, own, paired, from_x, from_y, mine, theirs,
     pair_sems, x_sems, y_sems, peer_sent, peer_got,
+    *,
+    gain_column,
 ):
     rows, local = query_rot.shape
     width = attention_grad.shape[1]
@@ -1195,6 +1203,39 @@
     plane = Plane(own, prompt_grads, paired, from_x, from_y, pair_sems, x_sems, y_sems, by_device=True)
     peers = Peers(mine, theirs, peer_sent, peer_got)
     greet(plane.neighbours() + peers.neighbours())
+    tile = min(512, width)
+    starts = range(0, width, tile)
+    scale_two = stats[:, 3:4]
+    logits = wide_dot(normed_two[...], router[...]) + expert_bias[...]
+    weights = jnp.exp(logits - jnp.max(logits, axis=1, keepdims=True))
+    chances = weights / jnp.sum(weights, axis=1, keepdims=True)
+    chance_grad = routed[...] * reduced[:, width:].astype(jnp.float32)
+    logit_grad = (
+        chances * (chance_grad - jnp.sum(chances * chance_grad, axis=1, keepdims=True))
+    ).astype(jnp.bfloat16)
+
+    def hidden_of(columns):
+        return tokens[:, columns].astype(jnp.float32) + attention[:, columns].astype(jnp.float32)
+
+    def input_part(columns):
+        return reduced[:, columns].astype(jnp.float32) + turned_dot(logit_grad, router[columns])
+
+    pull = jnp.zeros((rows, 1), jnp.float32)
+    for start in starts:
+        columns = slice(start, start + tile)
+        weighted = ffn_gain[:, columns] * input_part(columns)
+        hidden_grad[:, columns] = weighted
+        pull = pull + jnp.sum(weighted * hidden_of(columns), axis=1, keepdims=True)
+    pull = scale_two * scale_two * scale_two / width * pull
+    for start in starts:
+        columns = slice(start, start + tile)
+        grad = (
+            cotangent[:, columns].astype(jnp.float32)
+            + scale_two * hidden_grad[:, columns]
+            - hidden_of(columns) * pull
+        )
+        hidden_grad[:, columns] = grad
+        attention_grad[:, columns] = grad.astype(jnp.bfloat16)
     out_grad[...] = turned_dot(attention_grad[...], w_out[...]).astype(jnp.bfloat16)
     for head in range(heads):
         columns = slice(head * HD, (head + 1) * HD)
@@ -1238,6 +1279,14 @@
     scale_query, scale_key = stats[:, 1:2], stats[:, 2:3]
     query_inner = normed_part(query_grad, query_raw, 0, scale_query)
     plane.send_second()
+    chosen = lax.broadcasted_iota(jnp.int32, (rows, LANE), 1) == gain_column
+    chosen = jnp.where(chosen, 1.0, 0.0).astype(jnp.bfloat16)
+    for start in starts:
+        columns = slice(start, start + tile)
+        sway = input_part(columns) * hidden_of(columns) * scale_two
+        extras[columns] = (
+            crossed_dot(normed_two[:, columns], logit_grad) + crossed_dot(sway.astype(jnp.bfloat16), chosen)
+        ).astype(jnp.bfloat16)
 
     def last(piece, carry):
         for side, summed in enumerate(plane.last_sum(piece)):
@@ -1260,7 +1309,10 @@
     peers.finish()
 
 
-def backward(attention_grad, w_out, query_rot, keys_values, bias, stats, query_raw, key_raw, cosine, sine, qk_gain):
+def backward(
+    reduced, tokens, attention, cotangent, normed_two, router, expert_bias, routed, ffn_gain,
+    w_out, query_rot, keys_values, bias, stats, query_raw, key_raw, cosine, sine, qk_gain, gain_column,
+):
     rows, local = query_rot.shape
     size = lax.axis_size("tensor")
     ranks = lax.axis_size("expert")
@@ -1268,10 +1320,14 @@
     vmem = pl.BlockSpec(memory_space=pltpu.VMEM)
     small = jax.ShapeDtypeStruct((rows, local), low)
     return pl.pallas_call(
-        backward_kernel,
-        out_shape=(small, small, small, jax.ShapeDtypeStruct((2, local), full)),
-        in_specs=[vmem] * 11,
-        out_specs=(vmem,) * 4,
+        functools.partial(backward_kernel, gain_column=gain_column),
+        out_shape=(
+            small, small, small, jax.ShapeDtypeStruct((2, local), full),
+            jax.ShapeDtypeStruct(tokens.shape, full), jax.ShapeDtypeStruct(tokens.shape, low),
+            jax.ShapeDtypeStruct((tokens.shape[1], LANE), low),
+        ),
+        in_specs=[vmem] * 19,
+        out_specs=(vmem,) * 7,
         scratch_shapes=[
             pltpu.VMEM((rows, local), low),
             pltpu.VMEM((rows, local), full),
@@ -1290,7 +1346,10 @@
         compiler_params=pltpu.CompilerParams(
             collective_id=3, has_side_effects=True, vmem_limit_bytes=60 * 2**20
         ),
-    )(attention_grad, w_out, query_rot, keys_values, bias, stats, query_raw, key_raw, cosine, sine, qk_gain)
+    )(
+        reduced, tokens, attention, cotangent, normed_two, router, expert_bias, routed, ffn_gain,
+        w_out, query_rot, keys_values, bias, stats, query_raw, key_raw, cosine, sine, qk_gain,
+    )
 
 
 def rotate(field, cosine, sine):
@@ -1688,18 +1747,18 @@
     device = lax.axis_index("expert")
     full = jnp.float32
     group, position, tag = layout(rows, ranks, device, cont_group)
-    frequency = 10000.0 ** (-jnp.arange(HD // 2, dtype=full) * 2.0 / HD)
+    channel = jnp.arange(HD)
+    frequency = 10000.0 ** (-(channel % (HD // 2)).astype(full) * 2.0 / HD)
     angle = position.astype(full)[:, None] * frequency[None, :]
-    cosine, sine = jnp.cos(angle), jnp.sin(angle)
-    cosine = jnp.concatenate([cosine, cosine], axis=1)
-    sine = jnp.concatenate([-sine, sine], axis=1)
+    cosine = jnp.cos(angle)
+    sine = jnp.sin(angle) * jnp.where(channel < HD // 2, -1.0, 1.0)
     bias = jnp.where(attention_mask(group, position, tag, ranks), 0.0, masked_value).astype(full)
     own_first = jnp.roll(router, -device * local_experts, axis=1)
     own_first = jnp.pad(own_first, ((0, 0), (0, LANE - experts_total)))
     expert_bias = jnp.where(jnp.arange(LANE) < experts_total, 0.0, masked_value).astype(full)[None]
     turned_routes = jnp.tile(jnp.pad(routes.T, ((0, -routes.shape[1] % 8), (0, 0)), constant_values=-1), (2, 1))
     hits = routes[:, :, None] == jnp.arange(experts_total, dtype=jnp.int32)
-    routed = jnp.any(hits, axis=1).astype(full)
+    routed = jnp.pad(jnp.any(hits, axis=1).astype(full), ((0, 0), (0, LANE - experts_total)))
     (
         attention, normed, normed_two, attended, query_rot, keys_values, query_raw, key_raw, stats, routes_all, arrived,
     ) = front(
@@ -1714,45 +1773,26 @@
     reduced, gated, gate_grad, up_grad, mixed_part = experts_fused(
         arrived, arrived_grad, expert_mask, own_first, expert_bias, w_gate, w_up, w_down
     )
-    source = tokens.astype(full)
-    hidden = source + attention.astype(full)
-    scale_one, scale_two = stats[:, 0:1], stats[:, 3:4]
-    logits = jnp.dot(normed_two, router, preferred_element_type=full)
-    weights = jnp.exp(logits - jnp.max(logits, axis=1, keepdims=True))
-    chances = weights / jnp.sum(weights, axis=1, keepdims=True)
-    chance_grad = routed * reduced[:, width : width + experts_total].astype(full)
-    logit_grad = (
-        chances * (chance_grad - jnp.sum(chances * chance_grad, axis=1, keepdims=True))
-    ).astype(jnp.bfloat16)
-    grad_router = jnp.einsum("td,te->de", normed_two, logit_grad, preferred_element_type=full)
-    normed_two_grad = reduced[:, :width].astype(full) + jnp.einsum(
-        "te,de->td", logit_grad, router, preferred_element_type=full
-    )
-    grad_out = cotangent.astype(full)
-    weighted_two = ffn_gain * normed_two_grad
-    grad_ffn_gain = jnp.sum(normed_two_grad * hidden * scale_two, axis=0)
-    hidden_grad = (
-        grad_out
-        + scale_two * weighted_two
-        - hidden * (scale_two**3 / width) * jnp.sum(weighted_two * hidden, axis=1, keepdims=True)
-    )
-    attention_grad = hidden_grad.astype(jnp.bfloat16)
-    query_raw_grad, key_raw_grad, value_raw_grad, grad_qk_gain = backward(
-        attention_grad, w_out, query_rot, keys_values, bias, stats, query_raw, key_raw, cosine, sine, qk_gain
+    all_experts = jnp.pad(router, ((0, 0), (0, LANE - experts_total)))
+    (
+        query_raw_grad, key_raw_grad, value_raw_grad, grad_qk_gain, hidden_grad, attention_grad, extras,
+    ) = backward(
+        reduced, tokens, attention, cotangent, normed_two, all_experts, expert_bias, routed, ffn_gain[None],
+        w_out, query_rot, keys_values, bias, stats, query_raw, key_raw, cosine, sine, qk_gain, experts_total,
     )
     small_part = local_width // ranks
     share = width // ranks
-    gains = jnp.pad(
-        grad_qk_gain.reshape(2, ranks, small_part).transpose(1, 2, 0), ((0, 0), (0, share - small_part), (0, 0))
-    )
-    extras = jnp.concatenate(
-        [grad_router.reshape(ranks, share, experts_total), grad_ffn_gain.reshape(ranks, share, 1), gains], axis=2
-    ).astype(jnp.bfloat16)
-    extras = jnp.pad(extras, ((0, 0), (0, 0), (0, LANE - experts_total - 3)))
+    gains = grad_qk_gain.reshape(2, ranks, small_part).transpose(1, 2, 0).astype(jnp.bfloat16)
+    extras = extras.reshape(ranks, share, LANE) + jnp.pad(
+        gains, ((0, 0), (0, share - small_part), (experts_total + 1, LANE - experts_total - 3))
+    )
     normed_grad, sums, gain_total, mixture, grad_w_gate, grad_w_up, grad_w_down = closing(
         normed, query_raw_grad, key_raw_grad, value_raw_grad, attended, attention_grad, extras, w_query, w_key, w_value,
         mixed_part, arrived, arrived_grad, gated, gate_grad, up_grad, local_experts, experts_total + 3,
     )
+    source = tokens.astype(full)
+    hidden = source + attention.astype(full)
+    scale_one = stats[:, 0:1]
     normed_grad = normed_grad.astype(full)
     output = (hidden + mixture.astype(full)).astype(jnp.bfloat16)
     weighted_one = attn_gain * normed_grad
@@ -1773,9 +1813,9 @@
         sums[:, edge + experts_total],
         sums[:small_part, edge + experts_total + 1 : edge + experts_total + 3].T,
         sums[:, edge : edge + experts_total],
-        grad_w_gate,
-        grad_w_up,
-        grad_w_down,
+        grad_w_gate.astype(full),
+        grad_w_up.astype(full),
+        grad_w_down.astype(full),
     )
 
 

time: 489 us -> 475 us (0.971)
  matrix products: 8.93 us -> 0 us
  local copies, waits for them, and re-layouts: 25.1 us -> 17.3 us
    dot_general x3 -> x0, matrix products: 8.93 us -> none  [the longest x1 5.09 us: compact(): jnp.einsum('te,de->td', logit_grad, router, preferred_element_type=full)]
    unnamed x42 -> x25, local copies, waits for them, and re-layouts: 13.1 us -> 5.81 us
    pallas_call x1, Pallas kernels: 32.2 us -> 37.9 us  [backward(): pl.pallas_call(functools.partial(backward_kernel, gain_column=gain_column...]
    convert_element_type x1 -> x4, other arithmetic: 4.64 us -> 9.77 us  [the longest x1 4.08 us: compact(): grad_w_gate.astype(full)]
where the time goes in v8:
time: 475 us; the launch traced here: 472 us
  Pallas kernels  414 us (87%)
  other arithmetic  24.6 us (5%)
  local copies, waits for them, and re-layouts  17.3 us (4%)
  between operations  15.2 us (3%)
    pallas_call x1, Pallas kernels, front(): pl.pallas_call(front_kernel, out_shape=(jax.ShapeDtypeStruct((rows, width...  132 us
    pallas_call x1, Pallas kernels, closing(): pl.pallas_call(functools.partial(closing_kernel, gain_column=gain_column)...  123 us
    pallas_call x1, Pallas kernels, experts_fused(): pl.pallas_call(expert_kernel, out_shape=(jax.ShapeDtypeStruct((rows, wide...  121 us
    pallas_call x1, Pallas kernels, backward(): pl.pallas_call(functools.partial(backward_kernel, gain_column=gain_column...  37.9 us
  transfers between devices with their start and end apart: 1, of which 0 were waited for; matrix products, arithmetic and copies ran while one was open for 3% of the time, Pallas kernels for 28%

profile of v8, /device:TPU:0, one launch (start us, length us, event | category | flops | bytes accessed | tf_op | source)
XLA Modules:
  0.0 471.5 jit_solution(7516287689333511226)
XLA Ops:
  8.7 0.7 fusion.8
  9.6 1.1 copy.53
  11.1 0.9 pad.25.router
  12.0 0.9 pad.26.router
  13.7 1.5 fusion.5
  15.6 1.5 add_select_fusion.bias
  17.1 132.3 %shard_map.246 = (bf16[384,2048]{1,0:T(8,128)(2,1)}, bf16[384,2048]{1,0:T(8,128)(2,1)}, bf16[384,2048]{1,0:T(8,128)(2,1)}, bf16[384,512]{1,0:T(8,128)(2,1)}, bf1...) custom-call(bf16[384,2048]{1,0:T(8,128)(2,1)} %tokens.3, ...), custom_call_target="tpu_custom_call" | custom-call | flops 99999997952 | bytes 200000000 | tf_op jit(solution)/shard_map/pallas_call | solution.py:1147
  149.4 0.9 slice.38
  151.6 0.7 pad_convert_fusion.1.routed
  152.3 1.1 slice_reduce_fusion
  153.4 1.3 pad_convert_fusion.mask
  154.7 121.0 %shard_map.247 = (bf16[384,2176]{1,0:T(8,128)(2,1)}, bf16[8,384,512]{2,1,0:T(8,128)(2,1)}, bf16[8,384,512]{2,1,0:T(8,128)(2,1)}, bf16[8,384,512]{2,1,0:T(8,128)(2,1)}, bf16[8,384,2048]{2,1,0:T(8,128)(2,1)}) custom-call(bf16[8,384,2048]{2,1,0:T(8,128)(2,1)} %get-tuple-element.45.x_all, bf16[8,384,2048]{2,1,0:T(8,128)(2,1)} %bitcast.21, ...), custom_call_target="tpu_custom_call" | custom-call | flops 38654705664 | bytes 50331648 | tf_op jit(solution)/shard_map/pallas_call | solution.py:603
  275.7 37.9 %shard_map.248 = (bf16[384,512]{1,0:T(8,128)(2,1)}, bf16[384,512]{1,0:T(8,128)(2,1)}, bf16[384,512]{1,0:T(8,128)(2,1)}, f32[2,512]{1,0:T(2,128)}, f32[384,2048]{...) custom-call(bf16[384,2176]{1,0:T(8,128)(2,1)} %get-tuple-element.47.reduced, ...), custom_call_target="tpu_custom_call" | custom-call | tf_op jit(solution)/shard_map/pallas_call | solution.py:1322
  314.4 1.9 pad_add_fusion.extras
  316.4 122.6 %shard_map.249 = (bf16[384,2048]{1,0:T(8,128)(2,1)}, f32[256,2176]{1,0:T(8,128)}, f32[8,256]{1,0:T(8,128)}, bf16[384,2048]{1,0:T(8,128)(2,1)}, bf16[2,2048,256]{...) custom-call(bf16[384,2048]{1,0:T(8,128)(2,1)} %get-tuple-element.44.normed, ...), custom_call_target="tpu_custom_call" | custom-call | tf_op jit(solution)/shard_map/pallas_call | solution.py:900
  439.0 1.7 slice_reduce_fusion.1
  440.7 0.8 slice_bitcast_fusion.1
  441.5 1.1 slice.47
  442.6 2.9 slice_bitcast_fusion
  448.1 2.0 copy.56
  450.1 4.1 convert_element_type.68
  454.2 2.3 convert_element_type.69
  456.5 2.7 convert_element_type.70
  460.9 3.6 fusion.3
  (47 shorter events, 8.9 us)
Async XLA Ops:
  7.2 5.7 %copy-start.8 = (s32[384,8]{0,1:T(8,128)S(1)}, s32[384,8]{0,1:T(8,128)}, u32[]{:S(2)}) copy-start(s32[384,8]{0,1:T(8,128)} %param.27) | copy-start | bytes 36868
  7.2 3.5 copy-start.7
  7.2 147.5 %all-gather.3.cloned.1.call-start = ((), (), s32[]{:S(2)}) async-start(), calls=%async_computation | async-start | bytes 14155776 | tf_op jit(solution)/shard_map/all_gather | solution.py:1768
  441.5 4.7 copy-start
  441.5 4.7 copy-start.1
  441.5 4.7 copy-start.9
  450.1 4.1 copy-start.5
  454.2 2.3 copy-start.4
  456.5 3.3 copy-start.2
  456.5 3.9 copy-start.3
  456.5 4.3 copy-start.6
Sparse Core Ops, SparseCore 0:
  9.9 91.9 all-gather.2
